TPU v7x, 256 devices: a whole 4x4x8 slice. The times are simulated.
256 devices in a mesh: dom: 16 (over x, y), col: 8 (over z), rep: 2 (over core).
Axes of the slice: x: 4, y: 4, z: 8, core: 2. Of those that a mesh axis runs over, the one named last changes fastest.
Arguments:
- density: float32 [48, 16, 10, 128, 128], P('dom', 'col', 'rep'), may hold values from -2.5 to 2.5
- pattern: int32 [48, 16, 10], P('dom', 'col', 'rep'), may hold values from -1 to 767, as said below
- filt: int32 [48, 16, 10], P('dom', 'col', 'rep'), may hold values from -1 to 767, as said below
Outputs:
- purified: float32 [48, 16, 10, 128, 128], P('dom', 'col', 'rep')
Inputs may be any that keep to these rules, and one draw needn't show every extreme that they name: `pattern`: in every block row the valid entries come first and are distinct; slot 0 is the row's own cell; every valid entry names a cell at most 2 cells away along the first grid dimension and at most 1 along the second, both periodic; empty slots hold -1; some bands of rows use all 10 slots. `filt`: in every block row the valid entries come first and are distinct; slot 0 is the row's own cell; every valid entry names a cell at most 2 cells away along the first grid dimension and at most 1 along the second, both periodic; empty slots hold -1; some bands of rows use all 10 slots.
All inputs are finite; a program needn't handle non-finite values.
Results may differ from a plain program's by a relative error of at most 0.0003.
Values sent between devices are 32-bit elements; how exact they have to be, the bound alone decides.
No kernel may reach another device: no remote copies, remote signals or barrier semaphores. Data moves between devices by JAX's collectives and lax.ppermute only.
A program may use at most 128 MiB of HBM per device.

v0:
```python
import jax
import jax.numpy as jnp
from jax import lax
from jax.sharding import PartitionSpec as P


def with_halo(array, sides, width):
    for axis, dim in sides:
        peers, length = (lax.axis_size(axis), array.shape[dim])
        up = [(i, (i + 1) % peers) for i in range(peers)]
        down = [(j, i) for i, j in up]
        last = lax.slice_in_dim(array, length - width, length, axis=dim)
        initial = lax.slice_in_dim(array, 0, width, axis=dim)
        before = lax.ppermute(last, axis, up)
        after = lax.ppermute(initial, axis, down)
        array = jnp.concatenate([before, array, after], axis=dim)
    return array


def matched(block_cols, left_cols, want_cols):
    table = block_cols[:, None, :] == want_cols[None, :, None]
    table = table & (left_cols[:, None, None] >= 0) & (want_cols[None, :, None] >= 0)
    return table.astype(jnp.float32)


def select_first(left_all, cols_all, targets, rim_vals, rim_cols, locate):

    def one_row(row_item):
        left_vals, left_cols, want_cols = row_item
        where_rows = locate(left_cols)
        block_rows = rim_vals[where_rows]
        block_cols = rim_cols[where_rows]
        picked = jnp.einsum(
            "sft,stab->sfab",
            matched(block_cols, left_cols, want_cols),
            block_rows,
            precision=lax.Precision.HIGHEST,
        )
        return jnp.einsum("sab,sfbc->fac", left_vals, picked, precision=lax.Precision.HIGHEST)

    return lax.map(one_row, (left_all, cols_all, targets))


def body(density, pattern, filt):
    rows_d, rows_c, half_k, width, _ = density.shape
    half_f = filt.shape[2]
    count = rows_d * rows_c
    grid_d = rows_d * lax.axis_size("dom")
    grid_c = rows_c * lax.axis_size("col")
    dom_index = lax.axis_index("dom")
    col_index = lax.axis_index("col")
    rep_index = lax.axis_index("rep")
    total_rim = (rows_d + 4) * (rows_c + 2)

    def locate(cols):
        safe = jnp.maximum(cols, 0)
        cell_d = safe // grid_c
        cell_c = safe % grid_c
        local_d = (cell_d - dom_index * rows_d + 2) % grid_d
        local_c = (cell_c - col_index * rows_c + 1) % grid_c
        return jnp.minimum(local_d * (rows_c + 2) + local_c, total_rim - 1)

    whole_vals, whole_cols, whole_filt = (
        lax.all_gather(density, "rep", axis=2, tiled=True),
        lax.all_gather(pattern, "rep", axis=2, tiled=True),
        lax.all_gather(filt, "rep", axis=2, tiled=True),
    )
    full_f = whole_filt.shape[2]
    targets = whole_filt.reshape(count, full_f)
    side_vals, side_cols = (
        with_halo(whole_vals, (("col", 1),), 1),
        with_halo(whole_cols, (("col", 1),), 1),
    )
    rim_vals, rim_cols = (
        with_halo(side_vals, (("dom", 0),), 2),
        with_halo(side_cols, (("dom", 0),), 2),
    )
    rim_vals = rim_vals.reshape(total_rim, -1, width, width)
    rim_cols = rim_cols.reshape(total_rim, -1)
    square_terms = select_first(
        density.reshape(count, half_k, width, width),
        pattern.reshape(count, half_k),
        targets,
        rim_vals,
        rim_cols,
        locate,
    )
    square = lax.psum_scatter(
        square_terms.reshape(rows_d, rows_c, full_f, width, width),
        "rep",
        scatter_dimension=2,
        tiled=True,
    )
    square_flat = square.reshape(count, half_f, width, width)
    cube_terms = select_first(
        square_flat, filt.reshape(count, half_f), targets, rim_vals, rim_cols, locate
    )
    placed = lax.dynamic_update_slice_in_dim(
        jnp.zeros((count, full_f, width, width), jnp.float32),
        3.0 * square_flat,
        rep_index * half_f,
        1,
    )
    combined = (placed - 2.0 * cube_terms).reshape(rows_d, rows_c, full_f, width, width)
    purified = lax.psum_scatter(combined, "rep", scatter_dimension=2, tiled=True)
    return purified


def solution(mesh):
    in_specs = (P("dom", "col", "rep", None, None), P("dom", "col", "rep"), P("dom", "col", "rep"))
    out_specs = P("dom", "col", "rep", None, None)
    return jax.shard_map(body, mesh=mesh, in_specs=in_specs, out_specs=out_specs, check_vma=False)
```

profile of v0, /device:TPU:1, one launch (start us, length us, event | category | flops | bytes accessed | tf_op | source)
XLA Modules:
  0.0 564.2 jit_solution(6116871218752495551)
XLA Ops:
  6.5 0.7 all-gather.2.cloned.1.call-update
  7.3 25.0 %all-gather.2.cloned.1.call-done = f32[3,2,10,128,128]{4,3,2,1,0:T(8,128)} async-done(((f32[3,2,5,128,128]{4,3,2,1,0:T(8,128)}), f32[3,2,10,128,128]{4,3,2,1,0:T(8,128)}) %all-gather.2.cloned.1.call-update) | async-done | bytes 3932176 | tf_op jit(solution)/shard_map/all_gather | solution.py:64
  32.3 2.6 fusion.61
  34.9 1.1 collective-permute-start.4
  36.0 1.8 collective-permute-start.5
  37.9 42.8 %collective-permute-done.4 = f32[3,1,10,128,128]{4,3,2,1,0:T(8,128)S(1)} collective-permute-done((f32[3,1,10,128,128]{4,3,2,1,0:T(8,128)S(1)}, f32[3,1,10,128,128]{4,3,2,1,0:T(8,128)S(1)}, u32[]{:S(2)}, u32[]{:S(2)}) %collective-permute-start.4) | collective-permute-done | bytes 1966112 | tf_op jit(solution)/shard_map/ppermute | solution.py:14
  81.3 5.7 %fusion.60 = (f32[2,4,10,128,128]{4,3,2,1,0:T(8,128)}, f32[2,4,10,128,128]{4,3,2,1,0:T(8,128)}) fusion(f32[3,4,10,128,128]{4,3,2,1,0:T(8,128)S(1)} %constant_dynamic-update-slice_fusion), kind=kLoop, calls=%fused_computation.88 | loop fusion | bytes 20971520 | tf_op jit(solution)/shard_map/slice | solution.py:12
  87.0 0.8 copy-done
  87.7 1.4 collective-permute-start.6
  89.1 3.4 collective-permute-start.7
  92.6 2.9 all_gather.9
  95.6 0.6 collective-permute-start
  96.2 2.1 collective-permute-start.1
  98.5 2.3 all_gather.10
  101.3 4.8 collective-permute-start.3
  106.1 99.0 %collective-permute-done.2 = s32[2,4,10]{2,1,0:T(4,128)S(1)} collective-permute-done((s32[2,4,10]{2,1,0:T(4,128)S(1)}, s32[2,4,10]{2,1,0:T(4,128)S(1)}, u32[]{:S(2)}, u32[]{:S(2)}) %collective-permute-start.2) | collective-permute-done | bytes 352 | tf_op jit(solution)/shard_map/ppermute | solution.py:14
  205.2 14.8 %pad_maximum_fusion = f32[7,4,10,128,128]{4,3,2,1,0:T(8,128)} fusion(f32[2,4,10,128,128]{4,3,2,1,0:T(8,128)} %collective-permute-done.7, f32[3,4,10,128,128]{4,3,2,1,0:T(8,128)} %copy-done, f32[2,4,10,128,128]{4,3,2,1,0:T(8,128)} %collective-permute-done.6), kind=kLoop, calls=%fused_computation.78 | loop fusion | flops 9175040 | bytes 36700160 | tf_op jit(solution)/shard_map/concatenate | solution.py:16
  220.0 2.5 broadcast.720.clone.1
  222.4 120.0 %while.26 = (s32[]{:T(128)}, f32[6,10,128,128]{2,3,1,0:T(8,128)}, s32[6,5]{1,0:T(8,128)S(1)}, s32[]{:T(128)}, s32[]{:T(128)}, /*index=5*/s32[28,10]{1,0:T(8,128)...) while((s32[]{:T(128)}, f32[6,10,128,128]{2,3,1,0:T(8,128)}, ...), condition=%wide.region_1.2_spmd, body=%wide.region_0.1_spmd.sunk | while | flops 1356597888 | bytes 17373152 | solution.py:41
  222.5 7.0 %gather_fusion = f32[5,10,128,128]{3,2,1,0:T(8,128)S(1)} fusion(f32[28,10,128,128]{3,2,1,0:T(8,128)} %get-tuple-element.550, s32[1024]{0:T(1024)S(1)} %pad_clamp_fusion.4), kind=kCustom, calls=%fused_computation.1.clone.1 | custom fusion | bytes 6553620 | tf_op jit(solution)/shard_map/while/body/eval_jaxpr/gather | solution.py:31
  230.1 4.6 fusion.83
  234.6 7.8 %fusion.84 = f32[6,10,128,128]{2,3,1,0:T(8,128)} fusion(f32[6,10,128,128]{2,3,1,0:T(8,128)} %get-tuple-element.534, s32[]{:T(128)} %get-tuple-element.533, f32[5,10,128,128]{3,1,2,0:T(8,128)S(1)} %fusion.83, f32[6,5,128,128]{3,2,1,0:T(8,128)} %get-tuple-element.551), kind=kOutput, calls=%fused_computation.9.clone.1 | convolution fusion | flops 1258291200 | bytes 4260864 | tf_op jit(solution)/shard_map/while/body/eval_jaxpr/sab,sfbc->fac/dot_general | solution.py:39
  242.5 7.0 %gather_fusion = f32[5,10,128,128]{3,2,1,0:T(8,128)S(1)} fusion(f32[28,10,128,128]{3,2,1,0:T(8,128)} %get-tuple-element.550, s32[1024]{0:T(1024)S(1)} %pad_clamp_fusion.4), kind=kCustom, calls=%fused_computation.1.clone.1 | custom fusion | bytes 6553620 | tf_op jit(solution)/shard_map/while/body/eval_jaxpr/gather | solution.py:31
  250.0 4.6 fusion.83
  254.6 7.8 %fusion.84 = f32[6,10,128,128]{2,3,1,0:T(8,128)} fusion(f32[6,10,128,128]{2,3,1,0:T(8,128)} %get-tuple-element.534, s32[]{:T(128)} %get-tuple-element.533, f32[5,10,128,128]{3,1,2,0:T(8,128)S(1)} %fusion.83, f32[6,5,128,128]{3,2,1,0:T(8,128)} %get-tuple-element.551), kind=kOutput, calls=%fused_computation.9.clone.1 | convolution fusion | flops 1258291200 | bytes 4260864 | tf_op jit(solution)/shard_map/while/body/eval_jaxpr/sab,sfbc->fac/dot_general | solution.py:39
  262.4 7.0 %gather_fusion = f32[5,10,128,128]{3,2,1,0:T(8,128)S(1)} fusion(f32[28,10,128,128]{3,2,1,0:T(8,128)} %get-tuple-element.550, s32[1024]{0:T(1024)S(1)} %pad_clamp_fusion.4), kind=kCustom, calls=%fused_computation.1.clone.1 | custom fusion | bytes 6553620 | tf_op jit(solution)/shard_map/while/body/eval_jaxpr/gather | solution.py:31
  270.0 4.6 fusion.83
  274.6 7.8 %fusion.84 = f32[6,10,128,128]{2,3,1,0:T(8,128)} fusion(f32[6,10,128,128]{2,3,1,0:T(8,128)} %get-tuple-element.534, s32[]{:T(128)} %get-tuple-element.533, f32[5,10,128,128]{3,1,2,0:T(8,128)S(1)} %fusion.83, f32[6,5,128,128]{3,2,1,0:T(8,128)} %get-tuple-element.551), kind=kOutput, calls=%fused_computation.9.clone.1 | convolution fusion | flops 1258291200 | bytes 4260864 | tf_op jit(solution)/shard_map/while/body/eval_jaxpr/sab,sfbc->fac/dot_general | solution.py:39
  282.4 7.0 %gather_fusion = f32[5,10,128,128]{3,2,1,0:T(8,128)S(1)} fusion(f32[28,10,128,128]{3,2,1,0:T(8,128)} %get-tuple-element.550, s32[1024]{0:T(1024)S(1)} %pad_clamp_fusion.4), kind=kCustom, calls=%fused_computation.1.clone.1 | custom fusion | bytes 6553620 | tf_op jit(solution)/shard_map/while/body/eval_jaxpr/gather | solution.py:31
  290.0 4.6 fusion.83
  294.6 7.8 %fusion.84 = f32[6,10,128,128]{2,3,1,0:T(8,128)} fusion(f32[6,10,128,128]{2,3,1,0:T(8,128)} %get-tuple-element.534, s32[]{:T(128)} %get-tuple-element.533, f32[5,10,128,128]{3,1,2,0:T(8,128)S(1)} %fusion.83, f32[6,5,128,128]{3,2,1,0:T(8,128)} %get-tuple-element.551), kind=kOutput, calls=%fused_computation.9.clone.1 | convolution fusion | flops 1258291200 | bytes 4260864 | tf_op jit(solution)/shard_map/while/body/eval_jaxpr/sab,sfbc->fac/dot_general | solution.py:39
  302.4 7.0 %gather_fusion = f32[5,10,128,128]{3,2,1,0:T(8,128)S(1)} fusion(f32[28,10,128,128]{3,2,1,0:T(8,128)} %get-tuple-element.550, s32[1024]{0:T(1024)S(1)} %pad_clamp_fusion.4), kind=kCustom, calls=%fused_computation.1.clone.1 | custom fusion | bytes 6553620 | tf_op jit(solution)/shard_map/while/body/eval_jaxpr/gather | solution.py:31
  310.0 4.6 fusion.83
  314.6 7.8 %fusion.84 = f32[6,10,128,128]{2,3,1,0:T(8,128)} fusion(f32[6,10,128,128]{2,3,1,0:T(8,128)} %get-tuple-element.534, s32[]{:T(128)} %get-tuple-element.533, f32[5,10,128,128]{3,1,2,0:T(8,128)S(1)} %fusion.83, f32[6,5,128,128]{3,2,1,0:T(8,128)} %get-tuple-element.551), kind=kOutput, calls=%fused_computation.9.clone.1 | convolution fusion | flops 1258291200 | bytes 4260864 | tf_op jit(solution)/shard_map/while/body/eval_jaxpr/sab,sfbc->fac/dot_general | solution.py:39
  322.5 7.0 %gather_fusion = f32[5,10,128,128]{3,2,1,0:T(8,128)S(1)} fusion(f32[28,10,128,128]{3,2,1,0:T(8,128)} %get-tuple-element.550, s32[1024]{0:T(1024)S(1)} %pad_clamp_fusion.4), kind=kCustom, calls=%fused_computation.1.clone.1 | custom fusion | bytes 6553620 | tf_op jit(solution)/shard_map/while/body/eval_jaxpr/gather | solution.py:31
  330.0 4.6 fusion.83
  334.6 7.8 %fusion.84 = f32[6,10,128,128]{2,3,1,0:T(8,128)} fusion(f32[6,10,128,128]{2,3,1,0:T(8,128)} %get-tuple-element.534, s32[]{:T(128)} %get-tuple-element.533, f32[5,10,128,128]{3,1,2,0:T(8,128)S(1)} %fusion.83, f32[6,5,128,128]{3,2,1,0:T(8,128)} %get-tuple-element.551), kind=kOutput, calls=%fused_computation.9.clone.1 | convolution fusion | flops 1258291200 | bytes 4260864 | tf_op jit(solution)/shard_map/while/body/eval_jaxpr/sab,sfbc->fac/dot_general | solution.py:39
  344.3 36.0 %all-reduce.5.cloned.1.call-done = f32[3,2,10,128,128]{3,4,2,1,0:T(8,128)} async-done(((f32[3,2,10,128,128]{3,4,2,1,0:T(8,128)}), f32[3,2,10,128,128]{3,4,2,1,0:T(8,128)}) %all-reduce.5.cloned.1.call-update) | async-done | bytes 3932176
  380.4 3.0 constant_dynamic-slice_fusion.5
  383.4 2.4 broadcast.720.clone.2
  385.8 119.9 %while.27 = (s32[]{:T(128)}, f32[6,10,128,128]{2,3,1,0:T(8,128)}, s32[6,5]{1,0:T(8,128)S(1)}, s32[]{:T(128)}, s32[]{:T(128)}, /*index=5*/s32[28,10]{1,0:T(8,128)...) while((s32[]{:T(128)}, f32[6,10,128,128]{2,3,1,0:T(8,128)}, ...), condition=%wide.region_4.5_spmd, body=%wide.region_3.4_spmd.sunk | while | flops 1356597888 | bytes 17373152 | solution.py:41
  385.8 7.0 %gather_fusion.2 = f32[5,10,128,128]{3,2,1,0:T(8,128)S(1)} fusion(f32[28,10,128,128]{3,2,1,0:T(8,128)} %get-tuple-element.580, s32[1024]{0:T(1024)S(1)} %pad_clamp_fusion.5), kind=kCustom, calls=%fused_computation.3.clone.1 | custom fusion | bytes 6553620 | tf_op jit(solution)/shard_map/while/body/eval_jaxpr/gather | solution.py:31
  393.4 4.6 fusion.90
  398.0 7.8 %fusion.91 = f32[6,10,128,128]{2,3,1,0:T(8,128)} fusion(f32[6,10,128,128]{2,3,1,0:T(8,128)} %get-tuple-element.564, s32[]{:T(128)} %get-tuple-element.563, f32[5,10,128,128]{3,1,2,0:T(8,128)S(1)} %fusion.90, f32[6,5,128,128]{2,3,1,0:T(8,128)} %get-tuple-element.581), kind=kOutput, calls=%fused_computation.46.clone.1 | convolution fusion | flops 1258291200 | bytes 4260864 | tf_op jit(solution)/shard_map/while/body/eval_jaxpr/sab,sfbc->fac/dot_general | solution.py:39
  405.8 7.0 %gather_fusion.2 = f32[5,10,128,128]{3,2,1,0:T(8,128)S(1)} fusion(f32[28,10,128,128]{3,2,1,0:T(8,128)} %get-tuple-element.580, s32[1024]{0:T(1024)S(1)} %pad_clamp_fusion.5), kind=kCustom, calls=%fused_computation.3.clone.1 | custom fusion | bytes 6553620 | tf_op jit(solution)/shard_map/while/body/eval_jaxpr/gather | solution.py:31
  413.4 4.6 fusion.90
  418.0 7.8 %fusion.91 = f32[6,10,128,128]{2,3,1,0:T(8,128)} fusion(f32[6,10,128,128]{2,3,1,0:T(8,128)} %get-tuple-element.564, s32[]{:T(128)} %get-tuple-element.563, f32[5,10,128,128]{3,1,2,0:T(8,128)S(1)} %fusion.90, f32[6,5,128,128]{2,3,1,0:T(8,128)} %get-tuple-element.581), kind=kOutput, calls=%fused_computation.46.clone.1 | convolution fusion | flops 1258291200 | bytes 4260864 | tf_op jit(solution)/shard_map/while/body/eval_jaxpr/sab,sfbc->fac/dot_general | solution.py:39
  425.8 7.0 %gather_fusion.2 = f32[5,10,128,128]{3,2,1,0:T(8,128)S(1)} fusion(f32[28,10,128,128]{3,2,1,0:T(8,128)} %get-tuple-element.580, s32[1024]{0:T(1024)S(1)} %pad_clamp_fusion.5), kind=kCustom, calls=%fused_computation.3.clone.1 | custom fusion | bytes 6553620 | tf_op jit(solution)/shard_map/while/body/eval_jaxpr/gather | solution.py:31
  433.4 4.6 fusion.90
  437.9 7.8 %fusion.91 = f32[6,10,128,128]{2,3,1,0:T(8,128)} fusion(f32[6,10,128,128]{2,3,1,0:T(8,128)} %get-tuple-element.564, s32[]{:T(128)} %get-tuple-element.563, f32[5,10,128,128]{3,1,2,0:T(8,128)S(1)} %fusion.90, f32[6,5,128,128]{2,3,1,0:T(8,128)} %get-tuple-element.581), kind=kOutput, calls=%fused_computation.46.clone.1 | convolution fusion | flops 1258291200 | bytes 4260864 | tf_op jit(solution)/shard_map/while/body/eval_jaxpr/sab,sfbc->fac/dot_general | solution.py:39
  445.8 7.0 %gather_fusion.2 = f32[5,10,128,128]{3,2,1,0:T(8,128)S(1)} fusion(f32[28,10,128,128]{3,2,1,0:T(8,128)} %get-tuple-element.580, s32[1024]{0:T(1024)S(1)} %pad_clamp_fusion.5), kind=kCustom, calls=%fused_computation.3.clone.1 | custom fusion | bytes 6553620 | tf_op jit(solution)/shard_map/while/body/eval_jaxpr/gather | solution.py:31
  453.3 4.6 fusion.90
  457.9 7.8 %fusion.91 = f32[6,10,128,128]{2,3,1,0:T(8,128)} fusion(f32[6,10,128,128]{2,3,1,0:T(8,128)} %get-tuple-element.564, s32[]{:T(128)} %get-tuple-element.563, f32[5,10,128,128]{3,1,2,0:T(8,128)S(1)} %fusion.90, f32[6,5,128,128]{2,3,1,0:T(8,128)} %get-tuple-element.581), kind=kOutput, calls=%fused_computation.46.clone.1 | convolution fusion | flops 1258291200 | bytes 4260864 | tf_op jit(solution)/shard_map/while/body/eval_jaxpr/sab,sfbc->fac/dot_general | solution.py:39
  465.7 7.0 %gather_fusion.2 = f32[5,10,128,128]{3,2,1,0:T(8,128)S(1)} fusion(f32[28,10,128,128]{3,2,1,0:T(8,128)} %get-tuple-element.580, s32[1024]{0:T(1024)S(1)} %pad_clamp_fusion.5), kind=kCustom, calls=%fused_computation.3.clone.1 | custom fusion | bytes 6553620 | tf_op jit(solution)/shard_map/while/body/eval_jaxpr/gather | solution.py:31
  473.3 4.6 fusion.90
  477.9 7.8 %fusion.91 = f32[6,10,128,128]{2,3,1,0:T(8,128)} fusion(f32[6,10,128,128]{2,3,1,0:T(8,128)} %get-tuple-element.564, s32[]{:T(128)} %get-tuple-element.563, f32[5,10,128,128]{3,1,2,0:T(8,128)S(1)} %fusion.90, f32[6,5,128,128]{2,3,1,0:T(8,128)} %get-tuple-element.581), kind=kOutput, calls=%fused_computation.46.clone.1 | convolution fusion | flops 1258291200 | bytes 4260864 | tf_op jit(solution)/shard_map/while/body/eval_jaxpr/sab,sfbc->fac/dot_general | solution.py:39
  485.7 7.0 %gather_fusion.2 = f32[5,10,128,128]{3,2,1,0:T(8,128)S(1)} fusion(f32[28,10,128,128]{3,2,1,0:T(8,128)} %get-tuple-element.580, s32[1024]{0:T(1024)S(1)} %pad_clamp_fusion.5), kind=kCustom, calls=%fused_computation.3.clone.1 | custom fusion | bytes 6553620 | tf_op jit(solution)/shard_map/while/body/eval_jaxpr/gather | solution.py:31
  493.3 4.6 fusion.90
  497.9 7.8 %fusion.91 = f32[6,10,128,128]{2,3,1,0:T(8,128)} fusion(f32[6,10,128,128]{2,3,1,0:T(8,128)} %get-tuple-element.564, s32[]{:T(128)} %get-tuple-element.563, f32[5,10,128,128]{3,1,2,0:T(8,128)S(1)} %fusion.90, f32[6,5,128,128]{2,3,1,0:T(8,128)} %get-tuple-element.581), kind=kOutput, calls=%fused_computation.46.clone.1 | convolution fusion | flops 1258291200 | bytes 4260864 | tf_op jit(solution)/shard_map/while/body/eval_jaxpr/sab,sfbc->fac/dot_general | solution.py:39
  506.1 1.1 copy-done.1
  507.5 4.8 multiply_subtract_fusion
  512.2 5.4 copy.29
  517.7 37.0 %all-reduce.7.cloned.1.call-done = f32[3,2,10,128,128]{4,3,2,1,0:T(8,128)} async-done(((f32[3,2,10,128,128]{4,3,2,1,0:T(8,128)}), f32[3,2,10,128,128]{4,3,2,1,0:T(8,128)}) %all-reduce.7.cloned.1.call-update) | async-done | bytes 3932176
  554.7 3.0 constant_dynamic-slice_fusion.4
  (102 shorter events, 10.7 us)
Async XLA Ops:
  6.5 25.8 %all-gather.2.cloned.1.call-start = ((), (), s32[]{:S(2)}) async-start(), calls=%async_computation | async-start | bytes 5898240 | tf_op jit(solution)/shard_map/all_gather | solution.py:64
  7.3 373.1 %all-reduce.5.cloned.1.call-start = ((), (), s32[]{:S(2)}) async-start(), calls=%async_computation.1 | async-start | bytes 7864320
  34.9 45.9 %copy-start.2 = (f32[3,2,10,128,128]{4,3,2,1,0:T(8,128)S(1)}, f32[3,2,10,128,128]{4,3,2,1,0:T(8,128)}, u32[]{:S(2)}) copy-start(f32[3,2,10,128,128]{4,3,2,1,0:T(8,128)} %all-gather.2.cloned.1.call-done) | copy-start | bytes 11796484
  34.9 45.7 %collective-permute-start.4 = (f32[3,1,10,128,128]{4,3,2,1,0:T(8,128)S(1)}, f32[3,1,10,128,128]{4,3,2,1,0:T(8,128)S(1)}, u32[]{:S(2)}, u32[]{:S(2)}) collective-permute-start(f32[3,1,10,128,128]{4,3,2,1,0:T(8,128)S(1)} %get-tuple-element.400), channel_id=1, source_target_pairs={{0,2},{2,4},{4,6},{6,8},{8,10},{10,12},{12,14},{14,0},{1,3},{3,5},... | collective-permute-start | bytes 5898248 | tf_op jit(solution)/shard_map/ppermute | solution.py:14
  36.0 45.0 %collective-permute-start.5 = (f32[3,1,10,128,128]{4,3,2,1,0:T(8,128)S(1)}, f32[3,1,10,128,128]{4,3,2,1,0:T(8,128)S(1)}, u32[]{:S(2)}, u32[]{:S(2)}) collective-permute-start(f32[3,1,10,128,128]{4,3,2,1,0:T(8,128)S(1)} %get-tuple-element.399), channel_id=1, source_target_pairs={{2,0},{4,2},{6,4},{8,6},{10,8},{12,10},{14,12},{0,14},{3,1},{5,3},... | collective-permute-start | bytes 5898248 | tf_op jit(solution)/shard_map/ppermute | solution.py:15
  81.2 6.5 %copy-start = (f32[3,4,10,128,128]{4,3,2,1,0:T(8,128)}, f32[3,4,10,128,128]{4,3,2,1,0:T(8,128)S(1)}, u32[]{:S(2)}) copy-start(f32[3,4,10,128,128]{4,3,2,1,0:T(8,128)S(1)} %constant_dynamic-update-slice_fusion) | copy-start | bytes 23592964
  81.2 11.3 %copy-start.3 = (s32[3,2,5]{2,1,0:T(2,128)S(1)}, s32[3,2,5]{2,1,0:T(2,128)}, u32[]{:S(2)}) copy-start(s32[3,2,5]{2,1,0:T(2,128)} %param.8) | copy-start | bytes 364
  81.2 17.2 %copy-start.4 = (s32[3,2,5]{2,1,0:T(2,128)S(1)}, s32[3,2,5]{2,1,0:T(2,128)}, u32[]{:S(2)}) copy-start(s32[3,2,5]{2,1,0:T(2,128)} %param.9) | copy-start | bytes 364
  87.7 117.4 %collective-permute-start.6 = (f32[2,4,10,128,128]{4,3,2,1,0:T(8,128)}, f32[2,4,10,128,128]{4,3,2,1,0:T(8,128)}, u32[]{:S(2)}, u32[]{:S(2)}) collective-permute-start(f32[2,4,10,128,128]{4,3,2,1,0:T(8,128)} %get-tuple-element.397), channel_id=1, source_target_pairs={{0,16},{16,32},{32,48},{48,64},{64,80},{80,96},{96,112},{112,128},... | collective-permute-start | bytes 15728648 | tf_op jit(solution)/shard_map/ppermute | solution.py:14
  89.1 116.0 %collective-permute-start.7 = (f32[2,4,10,128,128]{4,3,2,1,0:T(8,128)}, f32[2,4,10,128,128]{4,3,2,1,0:T(8,128)}, u32[]{:S(2)}, u32[]{:S(2)}) collective-permute-start(f32[2,4,10,128,128]{4,3,2,1,0:T(8,128)} %get-tuple-element.398), channel_id=1, source_target_pairs={{16,0},{32,16},{48,32},{64,48},{80,64},{96,80},{112,96},{128,112},... | collective-permute-start | bytes 15728648 | tf_op jit(solution)/shard_map/ppermute | solution.py:15
  95.6 5.4 collective-permute-start
  96.2 4.9 collective-permute-start.1
  101.2 103.9 %collective-permute-start.2 = (s32[2,4,10]{2,1,0:T(4,128)S(1)}, s32[2,4,10]{2,1,0:T(4,128)S(1)}, u32[]{:S(2)}, u32[]{:S(2)}) collective-permute-start(s32[2,4,10]{2,1,0:T(4,128)S(1)} %get-tuple-element.403), channel_id=1, source_target_pairs={{0,16},{16,32},{32,48},{48,64},{64,80},{80,96},{96,112},{112,128},... | collective-permute-start | bytes 968 | tf_op jit(solution)/shard_map/ppermute | solution.py:14
  101.3 103.8 %collective-permute-start.3 = (s32[2,4,10]{2,1,0:T(4,128)S(1)}, s32[2,4,10]{2,1,0:T(4,128)S(1)}, u32[]{:S(2)}, u32[]{:S(2)}) collective-permute-start(s32[2,4,10]{2,1,0:T(4,128)S(1)} %get-tuple-element.404), channel_id=1, source_target_pairs={{16,0},{32,16},{48,32},{64,48},{80,64},{96,80},{112,96},{128,112},... | collective-permute-start | bytes 968 | tf_op jit(solution)/shard_map/ppermute | solution.py:15
  342.4 0.7 copy-start.5
  342.5 212.2 %all-reduce.7.cloned.1.call-start = ((), (), s32[]{:S(2)}) async-start(), calls=%async_computation.2 | async-start | bytes 7864320
  505.7 1.5 copy-start.1
Sparse Core Ops, SparseCore 0:
  9.2 23.1 all-gather.1
  342.6 37.7 all-reduce.4
  517.8 36.7 all-reduce.6
where the time goes:
time: 565 us; the launch traced here: 564 us
  waiting for transfers between devices  241 us (43%)
  matrix products  148 us (26%)
  local copies, waits for them, and re-layouts  119 us (21%)
  other arithmetic  20.6 us (4%)
  starting transfers between devices  15.6 us (3%)
  between operations  13.9 us (2%)
    ppermute x4, waiting for transfers between devices, with_halo(): before = lax.ppermute(last, axis, up)  142 us
    dot_general x12, matrix products, one_row(): jnp.einsum('sab,sfbc->fac', left_vals, picked, precision=lax.Precision.HI...  93.5 us
    gather x12, local copies, waits for them, and re-layouts, one_row(): block_rows = rim_vals[where_rows]  83.7 us
    unnamed x5, waiting for transfers between devices  73.7 us
    dot_general x12, matrix products, one_row(): jnp.einsum('sft,stab->sfab', matched(block_cols, left_cols, want_cols), b...  54.8 us
    all_gather x1, waiting for transfers between devices, body(): lax.all_gather(density, 'rep', axis=2, tiled=True)  25 us
    concatenate x3, other arithmetic, with_halo(): array = jnp.concatenate([before, array, after], axis=dim)  14.8 us
    ppermute x4, starting transfers between devices, with_halo(): after = lax.ppermute(initial, axis, down)  12.1 us
  transfers between devices with their start and end apart: 11, of which 5 were waited for; matrix products, arithmetic and copies ran while one was open for 0% of the time, Pallas kernels for 0%

commit v1 on v0

v1 whole, which is shorter than its diff:
```python
import functools

import jax
import jax.numpy as jnp
import numpy as np
from jax import lax
from jax.experimental import pallas as pl
from jax.experimental.pallas import tpu as pltpu
from jax.sharding import PartitionSpec as P

UNROLL = 16
ROWS, COLS = 3, 2
HALF = 5
CUTS = ((2, 3), (3, 2))
RIM_D, RIM_C = ROWS + 4, COLS + 2
RIM = RIM_D * RIM_C
CELLS = ROWS * COLS
SLOTS = 2 * HALF
OWN = 60
EARLY = 200
LATE = 40
ZERO = EARLY + 2 * LATE
TOTAL = ZERO + 1
SPOT = OWN


def block_places():
    places = np.zeros((2, RIM, HALF), np.int32)
    by_col, by_dom = corner_slots()
    for other in range(2):
        for rd in range(RIM_D):
            for rc in range(RIM_C):
                for s in range(HALF):
                    mid_d, mid_c = 2 <= rd < 2 + ROWS, 1 <= rc < 1 + COLS
                    low, far = int(rd >= 2 + ROWS), int(rc == RIM_C - 1)
                    row = rd - 2 - ROWS if low else rd
                    if mid_d and mid_c:
                        at = other * 30 + ((rd - 2) * 2 + rc - 1) * 5 + s
                    elif mid_d:
                        at = 60 + other * 30 + far * 15 + (rd - 2) * 5 + s
                    elif mid_c:
                        at = 120 + other * 40 + low * 20 + (row * 2 + rc - 1) * 5 + s
                    elif (low, row, s) in by_col:
                        at = EARLY + other * LATE + far * 10 + by_col.index((low, row, s))
                    else:
                        at = EARLY + other * LATE + 20 + low * 10 + by_dom[low].index((far, row, s))
                    places[other, rd * RIM_C + rc, s] = at
    return places


def corner_slots():
    by_col = [(low, row, s) for low in range(2) for row in range(2) for s in range(CUTS[low][row])]
    by_dom = [
        [(far, row, s) for far in range(2) for row in range(2) for s in range(CUTS[low][row], HALF)] for low in range(2)
    ]
    return by_col, by_dom


def shift(array, axis, step):
    peers = lax.axis_size(axis)
    return lax.ppermute(array, axis, [(i, (i + step) % peers) for i in range(peers)])


SQUARE_LEN = SPOT * SLOTS + 2 * UNROLL
CUBE_LEN = CELLS * HALF * SLOTS + 2 * UNROLL
TAIL_LEN = 2 * CELLS * HALF * SLOTS + 2 * UNROLL
LANES = 128
NONE = RIM + 3
TABLE = 32


def list_kernel(
    grid, known, stored, first, early, late, late_other, cube, tail, touched, counts, table_v, place_v, table, place, flag, sems
):
    grid_d, grid_c = grid
    dom, col, rep = lax.axis_index("dom"), lax.axis_index("col"), lax.axis_index("rep")
    lane = lax.broadcasted_iota(jnp.int32, (1, LANES), 1)
    names = jnp.full((1, LANES), -5, jnp.int32)
    name = []
    for j in range(RIM):
        d, c = dom * ROWS + (j // RIM_C - 2), col * COLS + (j % RIM_C - 1)
        d = jnp.where(d < 0, d + grid_d, jnp.where(d >= grid_d, d - grid_d, d))
        c = jnp.where(c < 0, c + grid_c, jnp.where(c >= grid_c, c - grid_c, c))
        name.append(d * grid_c + c)
        names = jnp.where(lane == j, name[j], names)
    table_v[...] = jnp.full((TABLE, LANES), -1, jnp.int32)
    for r in range(RIM_D):
        x, at = known[r], stored[r]
        row = jnp.full((RIM_C, LANES), -1, jnp.int32)
        for t in range(SLOTS):
            row = jnp.where(x[:, t:t + 1] == names, at[:, t:t + 1], row)
        table_v[r * RIM_C:(r + 1) * RIM_C, :] = row
    one = pltpu.make_async_copy(table_v, table, sems.at[0])
    one.start()
    for q in range(2):
        for r in range(ROWS):
            x = known[2 + r, 1:1 + COLS] if q == 0 else known[RIM_D + r, :COLS]
            at = jnp.full((COLS, SLOTS), NONE, jnp.int32)
            for j in range(RIM):
                at = jnp.where(x == name[j], j, at)
            place_v[q * CELLS + r * COLS:q * CELLS + (r + 1) * COLS, :SLOTS] = at
    two = pltpu.make_async_copy(place_v, place, sems.at[1])
    two.start()
    two.wait()
    one.wait()

    blank = ZERO | (ZERO << 10) | (SPOT << 20)
    blank_cube = 2 * SPOT | (ZERO << 10) | ((CELLS * HALF) << 20)

    def pad(ref, n, code):
        ref[n] = code
        return n + (n & 1)

    def square_cell(i, carry):
        rows = [place[i, s] for s in range(SLOTS)]
        own = [i * HALF + s % HALF + jnp.where(rep == s // HALF, 0, CELLS * HALF) for s in range(SLOTS)]

        def square_row(f, carry):
            nf, ne, nl, no, nt = carry
            before = nl + no
            k = place[CELLS + i, f]
            spot = i * SLOTS + f
            o = spot << 20
            values = [table[j, k] for j in rows]
            for s in range(SLOTS):
                v = values[s]
                code = own[s] | (v << 10) | o
                first[nf] = code
                early[ne] = code
                late[nl] = code
                late_other[no] = code
                third, second = jnp.where(v >= EARLY + LATE, 1, 0), jnp.where(v >= EARLY, 1, 0)
                beyond = jnp.where(v >= OWN, 1, 0)
                nf = nf + jnp.where(v >= 0, 1, 0) - beyond
                ne = ne + beyond - second
                nl = nl + second - third
                no = no + third
            again = jnp.where(nl + no > before, 1, 0)
            flag[spot] = again
            touched[nt] = spot
            nf, ne = pad(first, nf, blank), pad(early, ne, blank)
            return nf, ne, pad(late, nl, blank), pad(late_other, no, blank), nt + again

        return lax.fori_loop(0, SLOTS, square_row, carry)

    def cube_cell(i, carry):
        rows = [place[CELLS + i, g] for g in range(SLOTS)]
        again = [flag[i * SLOTS + g] for g in range(SLOTS)]

        def cube_row(f, carry):
            nc, nt = carry
            k = place[CELLS + i, rep * HALF + f]
            o = (i * SLOTS) | ((i * HALF + f) << 20)
            values = [table[j, k] for j in rows]
            for g in range(SLOTS):
                v = values[g]
                code = (o + (g + SPOT)) | (v << 10)
                hit, is_late = jnp.where(v >= 0, 1, 0), jnp.where(v >= EARLY, 1, 0)
                cube[nc] = code
                nc = nc + hit - is_late
                tail[nt] = code
                nt = nt + is_late
                tail[nt] = code - SPOT
                nt = nt + hit * again[g]
            return pad(cube, nc, blank_cube), pad(tail, nt, blank_cube)

        return lax.fori_loop(0, HALF, cube_row, carry)

    zero = jnp.int32(0)
    nf, ne, nl, no, touches = lax.fori_loop(0, CELLS, square_cell, (zero,) * 5)
    nc, nt = lax.fori_loop(0, CELLS, cube_cell, (zero, zero))
    for u in range(2 * UNROLL):
        first[nf + u] = blank
        early[ne + u] = blank
        late[nl + u] = blank
        late_other[no + u] = blank
        cube[nc + u] = blank_cube
        tail[nt + u] = blank_cube
    for q, n in enumerate((nf, ne, nl, no, nc, nt)):
        counts[q] = n // 2
    counts[6] = touches
    counts[7] = rep * HALF


def make_lists(known, stored):
    grid = (ROWS * lax.axis_size("dom"), COLS * lax.axis_size("col"))
    lengths = (SQUARE_LEN,) * 4 + (CUBE_LEN, TAIL_LEN, SPOT + 1, 8)
    return pl.pallas_call(
        functools.partial(list_kernel, grid),
        out_shape=[jax.ShapeDtypeStruct((n,), jnp.int32) for n in lengths],
        in_specs=[vmem()] * 2,
        out_specs=[smem()] * len(lengths),
        scratch_shapes=[
            pltpu.VMEM((TABLE, LANES), jnp.int32),
            pltpu.VMEM((16, LANES), jnp.int32),
            pltpu.SMEM((TABLE, LANES), jnp.int32),
            pltpu.SMEM((16, LANES), jnp.int32),
            pltpu.SMEM((SPOT,), jnp.int32),
            pltpu.SemaphoreType.DMA((2,)),
        ],
        compiler_params=pltpu.CompilerParams(vmem_limit_bytes=2 << 20),
        cost_estimate=pl.CostEstimate(flops=1000, bytes_accessed=1000, transcendentals=0),
        name="lists",
    )(known, stored)


def split(x):
    high = x.astype(jnp.bfloat16)
    low = (x - high.astype(jnp.float32)).astype(jnp.bfloat16)
    return high, low


def split_blocks(src, src_at, dst, dst_at, count):
    def step(b, _):
        high, low = split(src[src_at + b])
        dst[dst_at + b, :, :128] = high
        dst[dst_at + b, :, 128:] = low
        return 0

    lax.fori_loop(0, count, step, 0, unroll=2)


def run_list(codes, pairs, left, right, total, unroll=UNROLL):
    def step(at, _):
        for u in range(unroll):
            first = codes[at * (2 * unroll) + 2 * u]
            second = codes[at * (2 * unroll) + 2 * u + 1]
            l1, r1 = first & 1023, (first >> 10) & 1023
            l2, r2 = second & 1023, (second >> 10) & 1023
            o = first >> 20
            a1, a2 = left[l1], left[l2]
            lhs = jnp.concatenate(
                [
                    jnp.concatenate([a1[:, :128], a2[:, :128]], axis=1),
                    jnp.concatenate([a1[:, 128:], a2[:, 128:]], axis=1),
                ],
                axis=0,
            )
            rhs = jnp.concatenate([right[r1], right[r2]], axis=0)
            out = jnp.dot(lhs, rhs, preferred_element_type=jnp.float32)
            total[o] += (out[:128, :128] + out[:128, 128:]) + (out[128:, :128] + out[128:, 128:])
        return 0

    lax.fori_loop(0, (pairs + unroll - 1) // unroll, step, 0)


def zero_blocks(ref, count):
    def step(b, _):
        ref[b] = jnp.zeros(ref.shape[1:], ref.dtype)
        return 0

    lax.fori_loop(0, count, step, 0)


DEPTH, CHUNK = 3, 20


def chunks(pieces):
    result, at = [], 0
    for piece in pieces:
        parts = -(-piece.shape[0] // CHUNK)
        size = piece.shape[0] // parts
        for part in range(parts):
            result.append((piece, part * size, size, at))
            at += size
    return result


def load_and_split(pieces, stage, sems, blocks, base, prepare=lambda: None):
    copies, parts = [], chunks(pieces)
    for n, (piece, start, size, _) in enumerate(parts):
        slot = stage.at[pl.ds(n % DEPTH * CHUNK, size)]
        copies.append(pltpu.make_async_copy(piece.at[pl.ds(start, size)], slot, sems.at[n]))
    for copy in copies[:DEPTH]:
        copy.start()
    prepare()
    for n, (_, _, size, at) in enumerate(parts):
        copies[n].wait()
        split_blocks(stage, n % DEPTH * CHUNK, blocks, base + at, size)
        if n + DEPTH < len(parts):
            copies[n + DEPTH].start()


def first_kernel(codes, counts, *refs):
    pieces, (blocks, square, stage, sems) = refs[:-4], refs[-4:]

    def prepare():
        blocks[ZERO] = jnp.zeros(blocks.shape[1:], blocks.dtype)
        zero_blocks(square, SPOT + 1)

    load_and_split(pieces, stage, sems, blocks, 0, prepare)
    run_list(codes, counts[0], blocks, blocks, square)


def early_kernel(codes, cube_codes, counts, _, square_in, *refs):
    pieces, (blocks, square, halves, cube, stage, sems) = refs[:-6], refs[-6:]

    def prepare():
        zero_blocks(cube, CELLS * HALF + 1)
        halves[2 * SPOT] = jnp.zeros(blocks.shape[1:], blocks.dtype)

    load_and_split(pieces, stage, sems, blocks, OWN, prepare)
    run_list(codes, counts[1], blocks, blocks, square)
    split_blocks(square, 0, halves, SPOT, SPOT)
    run_list(cube_codes, counts[4], halves, blocks, cube)
    base = counts[7]

    def combine(i, _):
        for f in range(HALF):
            cube[i * HALF + f] = cube[i * HALF + f] - 1.5 * square[i * SLOTS + base + f]
        return 0

    lax.fori_loop(0, CELLS, combine, 0)
    zero_blocks(square, SPOT + 1)


def corner_kernel(codes, counts, blocks_in, square_in, *refs):
    pieces, (blocks, square, stage, sems) = refs[:-4], refs[-4:]
    load_and_split(pieces, stage, sems, blocks, EARLY)
    run_list(codes, counts[2], blocks, blocks, square, 8)


def late_kernel(codes, tail_codes, touched, counts, blocks_in, square_in, halves_in, cube_in, *refs):
    pieces, (out, blocks, square, halves, cube, stage, sems) = refs[:-7], refs[-7:]
    load_and_split(pieces, stage, sems, blocks, EARLY + LATE)
    run_list(codes, counts[3], blocks, blocks, square, 8)

    def resplit(n, _):
        o = touched[n]
        high, low = split(square[o])
        halves[o, :, :128] = high
        halves[o, :, 128:] = low
        return 0

    lax.fori_loop(0, counts[6], resplit, 0)
    run_list(tail_codes, counts[5], halves, blocks, cube, 8)
    base = counts[7]
    copies = []
    for i in range(CELLS):
        for f in range(HALF):
            o = i * HALF + f
            stage[o] = 3.0 * square[i * SLOTS + base + f] - 2.0 * cube[o]
        at = pl.ds(i * HALF, HALF)
        copies.append(pltpu.make_async_copy(stage.at[at], out.at[at], sems.at[i]))
        copies[-1].start()
    for copy in copies:
        copy.wait()


def pack_kernel(plan, count, *refs):
    sources, dests, sems = refs[:count], refs[count:-1], refs[-1]
    copies = []
    for n, (d, at, q, start, length) in enumerate(plan):
        copies.append(pltpu.make_async_copy(sources[q].at[pl.ds(start, length)], dests[d].at[pl.ds(at, length)], sems.at[n]))
        copies[-1].start()
    for copy in copies:
        copy.wait()


def pack(arrays, wanted):
    plan, sizes = [], []
    for d, ranges in enumerate(wanted):
        at = 0
        for q, start, length in ranges:
            plan.append((d, at, q, start, length))
            at += length
        sizes.append(at)
    return pl.pallas_call(
        functools.partial(pack_kernel, tuple(plan), len(arrays)),
        out_shape=[jax.ShapeDtypeStruct((n, 128, 128), jnp.float32) for n in sizes],
        in_specs=[anyspace()] * len(arrays),
        out_specs=[vmem()] * len(sizes),
        scratch_shapes=[pltpu.SemaphoreType.DMA((len(plan),))],
        compiler_params=pltpu.CompilerParams(vmem_limit_bytes=6 << 20),
        cost_estimate=pl.CostEstimate(flops=1000, bytes_accessed=1000, transcendentals=0),
        name="pack",
    )(*arrays)


def smem():
    return pl.BlockSpec(memory_space=pltpu.SMEM)


def anyspace():
    return pl.BlockSpec(memory_space=pl.ANY)


def vmem():
    return pl.BlockSpec(memory_space=pltpu.VMEM)


def hbm():
    return pl.BlockSpec(memory_space=pltpu.HBM)


BLOCKS = pltpu.VMEM((TOTAL, 128, 256), jnp.bfloat16)
SQUARE = pltpu.VMEM((SPOT + 1, 128, 128), jnp.float32)
HALVES = pltpu.VMEM((2 * SPOT + 1, 128, 256), jnp.bfloat16)
CUBE = pltpu.VMEM((CELLS * HALF + 1, 128, 128), jnp.float32)


def call(kernel, name, lists, held, pieces, outs, aliases):
    kinds = [hbm() if isinstance(o, jax.ShapeDtypeStruct) else vmem() for o in outs]
    return pl.pallas_call(
        kernel,
        out_shape=outs,
        in_specs=[smem()] * len(lists) + [vmem()] * len(held) + [anyspace()] * len(pieces),
        out_specs=kinds,
        scratch_shapes=[pltpu.VMEM((DEPTH * CHUNK, 128, 128), jnp.float32), pltpu.SemaphoreType.DMA((8,))],
        input_output_aliases={len(lists) + i: o for i, o in aliases.items()},
        compiler_params=pltpu.CompilerParams(vmem_limit_bytes=4 << 20),
        cost_estimate=pl.CostEstimate(flops=1000, bytes_accessed=1000, transcendentals=0),
        name=name,
    )(*lists, *held, *pieces)


def stored_places():
    mine, other = block_places()
    first = np.concatenate([mine, other], axis=1).reshape(RIM_D, RIM_C, SLOTS)
    second = np.concatenate([other, mine], axis=1).reshape(RIM_D, RIM_C, SLOTS)
    return jnp.where(lax.axis_index("rep") == 0, first, second)


def flat(x):
    return x.reshape(-1, 128, 128)


def body(density, pattern, filt):
    blocks = flat(density)
    row = COLS * HALF
    above, below = shift(pattern[1:], "dom", 1), shift(pattern[:2], "dom", -1)
    edges = [[(0, r * row + q, HALF) for r in range(ROWS)] for q in (HALF, 0)]
    edge_d, edge_u, edge_r, edge_l = pack([blocks], [[(0, row, 2 * row)], [(0, 0, 2 * row)]] + edges)
    down, up = shift(edge_d, "dom", 1), shift(edge_u, "dom", -1)
    own_other = shift(blocks, "rep", 1)
    near = jnp.concatenate([above, pattern, below], axis=0)
    before, after = shift(near[:, 1:], "col", 1), shift(near[:, :1], "col", -1)
    before, after, edge_r, edge_l = lax.optimization_barrier((before, after, edge_r, edge_l))
    right, left = shift(edge_r, "col", 1), shift(edge_l, "col", -1)
    rim = jnp.concatenate([before, near, after], axis=1)
    own_filt = jnp.pad(filt, ((0, 0), (0, RIM_C - COLS), (0, 0)), constant_values=-1)
    known = lax.all_gather(jnp.concatenate([rim, own_filt], axis=0), "rep", axis=2, tiled=True)
    first_codes, early_codes, late_codes, other_codes, cube_codes, tail_codes, touched, counts = make_lists(
        known, stored_places()
    )
    held, square = call(first_kernel, "first", [first_codes, counts], [], [blocks, own_other], [BLOCKS, SQUARE], {})
    held, square, right, left, down, up = lax.optimization_barrier((held, square, right, left, down, up))
    by_col, by_dom = corner_slots()
    to_r, to_l = [[(low, row * 10 + c * 5 + s, 1) for low, row, s in by_col] for c in (1, 0)]
    to_d, to_u = [[(2 + far, (row + 1 - low) * 5 + s, 1) for far, row, s in by_dom[low]] for low in (0, 1)]
    to_r, to_l, to_d, to_u = pack([down, up, right, left], [to_r, to_l, to_d, to_u])
    corner_r, corner_l = shift(to_r, "col", 1), shift(to_l, "col", -1)
    corner_d, corner_u = shift(to_d, "dom", 1), shift(to_u, "dom", -1)

    def with_other(*pieces):
        return list(pieces) + [shift(p, "rep", 1) for p in pieces]

    early = with_other(right, left) + with_other(down, up)
    held, square, halves, cube = call(
        early_kernel, "early", [early_codes, cube_codes, counts], [held, square], early,
        [BLOCKS, SQUARE, HALVES, CUBE], {0: 0, 1: 1},
    )
    held, square, halves, cube, *corners = lax.optimization_barrier(
        (held, square, halves, cube, corner_r, corner_l, corner_d, corner_u)
    )
    others = [shift(p, "rep", 1) for p in corners]
    held, square = call(
        corner_kernel, "corner", [late_codes, counts], [held, square], corners, [BLOCKS, SQUARE], {0: 0, 1: 1}
    )
    out = jax.ShapeDtypeStruct((CELLS * HALF, 128, 128), jnp.float32)
    out = call(
        late_kernel, "late", [other_codes, tail_codes, touched, counts], [held, square, halves, cube], others,
        [out, BLOCKS, SQUARE, HALVES, CUBE], {0: 1, 1: 2, 2: 3, 3: 4},
    )[0]
    return out.reshape(density.shape)


def solution(mesh):
    in_specs = (P("dom", "col", "rep", None, None), P("dom", "col", "rep"), P("dom", "col", "rep"))
    out_specs = P("dom", "col", "rep", None, None)
    return jax.shard_map(body, mesh=mesh, in_specs=in_specs, out_specs=out_specs, check_vma=False)
```

time: 565 us -> 93.5 us (0.17)
  waiting for transfers between devices: 241 us -> 8.92 us
  matrix products: 148 us -> 0 us
  local copies, waits for them, and re-layouts: 119 us -> 6.09 us
  Pallas kernels: 0 us -> 45.5 us
  other arithmetic: 20.6 us -> 0.18 us
  between operations: 13.9 us -> 0.35 us
  starting transfers between devices: 15.6 us -> 28.8 us
    dot_general x24 -> x0, matrix products: 148 us -> none  [the longest x12 93.5 us: one_row(): jnp.einsum('sab,sfbc->fac', left_vals, picked, precision=lax.Precision.HI...]
    ppermute x8 -> x21, waiting for transfers between devices: 142 us -> 8.92 us  [shift(): lax.ppermute(array, axis, [(i, (i + step) % peers) for i in range(peers)])]
    gather x24 -> x0, local copies, waits for them, and re-layouts: 90.3 us -> none  [the longest x12 83.7 us: one_row(): block_rows = rim_vals[where_rows]]
    unnamed x5 -> x0, waiting for transfers between devices: 73.7 us -> none
    pallas_call x0 -> x7, Pallas kernels: none -> 45.5 us  [the longest x4 28.7 us: call(): pl.pallas_call(kernel, out_shape=outs, in_specs=[smem()] * len(lists) + [...]
    all_gather x1 -> x0, waiting for transfers between devices: 25 us -> none  [body(): lax.all_gather(density, 'rep', axis=2, tiled=True)]
    concatenate x3 -> x2, other arithmetic: 14.8 us -> 0.17 us  [the longest x1 0.09 us: body(): jnp.concatenate([rim, own_filt], axis=0)]
    ppermute x8 -> x21, starting transfers between devices: 15.3 us -> 28.8 us  [shift(): lax.ppermute(array, axis, [(i, (i + step) % peers) for i in range(peers)])]
  transfers between devices with their start and end apart: 11 -> 21, of which waited for: 5 -> 7; matrix products, arithmetic and copies ran while one was open for 0% -> 3% of each run, Pallas kernels for 0% -> 41%
where the time goes in v1:
time: 93.5 us; the launch traced here: 93.8 us
  Pallas kernels  45.5 us (49%)
  starting transfers between devices  28.8 us (31%)
  waiting for transfers between devices  8.92 us (10%)
  local copies, waits for them, and re-layouts  6.09 us (7%)
  blocking collectives  3.94 us (4%)
    ppermute x21, starting transfers between devices, shift(): lax.ppermute(array, axis, [(i, (i + step) % peers) for i in range(peers)])  28.8 us
    pallas_call x4, Pallas kernels, call(): pl.pallas_call(kernel, out_shape=outs, in_specs=[smem()] * len(lists) + [...  28.7 us
    pallas_call x1, Pallas kernels, make_lists(): pl.pallas_call(functools.partial(list_kernel, grid), out_shape=[jax.Shape...  12.3 us
    ppermute x21, waiting for transfers between devices, shift(): lax.ppermute(array, axis, [(i, (i + step) % peers) for i in range(peers)])  8.92 us
    unnamed x14, local copies, waits for them, and re-layouts  5.02 us
    pallas_call x2, Pallas kernels, pack(): pl.pallas_call(functools.partial(pack_kernel, tuple(plan), len(arrays)),...  4.44 us
    all_gather x1, blocking collectives, body(): lax.all_gather(jnp.concatenate([rim, own_filt], axis=0), 'rep', axis=2, t...  3.94 us
  transfers between devices with their start and end apart: 21, of which 7 were waited for; matrix products, arithmetic and copies ran while one was open for 3% of the time, Pallas kernels for 41%

profile of v1, /device:TPU:1, one launch (start us, length us, event | category | flops | bytes accessed | tf_op | source)
XLA Modules:
  0.0 93.8 jit_solution(6051209288968060549)
XLA Ops:
  0.0 3.2 %collective-permute-start.4 = (f32[30,128,128]{2,1,0:T(8,128)}, f32[30,128,128]{2,1,0:T(8,128)}, u32[]{:S(2)}, u32[]{:S(2)}) collective-permute-start(f32[30,128,128]{2,1,0:T(8,128)} %bitcast.2), channel_id=1, source_target_pairs={{0,1},{1,0},{2,3},{3,2},{4,5},{5,4},{6,7},{7,6},{8,9},{9,8},{10,11... | collective-permute-start | bytes 5898248 | tf_op jit(solution)/shard_map/ppermute | solution.py:61
  3.2 0.8 fusion.1
  4.0 0.1 copy.15
  4.1 3.2 %collective-permute-start.1 = (s32[2,2,5]{0,1,2:T(2,128)S(1)}, s32[2,2,5]{0,1,2:T(2,128)S(1)}, u32[]{:S(2)}, u32[]{:S(2)}) collective-permute-start(s32[2,2,5]{0,1,2:T(2,128)S(1)} %copy.15), channel_id=1, source_target_pairs={{0,240},{16,0},{32,16},{48,32},{64,48},{80,64},{96,80},{112,96},{1... | collective-permute-start | bytes 248 | tf_op jit(solution)/shard_map/ppermute | solution.py:61
  7.3 0.1 copy.14
  7.4 0.0 collective-permute-start
  7.4 0.0 copy-start
  7.4 1.5 %copy-done = f32[3,2,5,128,128]{4,3,2,1,0:T(8,128)S(1)} copy-done((f32[3,2,5,128,128]{4,3,2,1,0:T(8,128)S(1)}, f32[3,2,5,128,128]{4,3,2,1,0:T(8,128)}, u32[]{:S(2)}) %copy-start) | copy-done | bytes 1966104
  9.0 2.4 %pack.2 = (f32[20,128,128]{2,1,0:T(8,128)}, f32[20,128,128]{2,1,0:T(8,128)}, f32[15,128,128]{2,1,0:T(8,128)S(1)}, f32[15,128,128]{2,1,0:T(8,128)S(1)}) custom-call(f32[30,128,128]{2,1,0:T(8,128)S(1)} %bitcast.3), custom_call_target="tpu_custom_call" | custom-call | flops 1000 | bytes 1000 | tf_op jit(solution)/shard_map/pack/pallas_call | solution.py:368
  11.4 1.0 %copy-done.2 = f32[15,128,128]{2,1,0:T(8,128)} copy-done((f32[15,128,128]{2,1,0:T(8,128)}, f32[15,128,128]{2,1,0:T(8,128)S(1)}, u32[]{:S(2)}) %copy-start.2) | copy-done | bytes 983064
  12.3 0.9 %copy-done.3 = f32[15,128,128]{2,1,0:T(8,128)} copy-done((f32[15,128,128]{2,1,0:T(8,128)}, f32[15,128,128]{2,1,0:T(8,128)S(1)}, u32[]{:S(2)}) %copy-start.3) | copy-done | bytes 983064
  13.3 0.0 collective-permute-start.7
  13.3 4.8 %collective-permute-start.8 = (f32[20,128,128]{2,1,0:T(8,128)}, f32[20,128,128]{2,1,0:T(8,128)}, u32[]{:S(2)}, u32[]{:S(2)}) collective-permute-start(f32[20,128,128]{2,1,0:T(8,128)} %get-tuple-element.65), channel_id=1, source_target_pairs={{0,240},{16,0},{32,16},{48,32},{64,48},{80,64},{96,80},{112,96},{1... | collective-permute-start | bytes 3932168 | tf_op jit(solution)/shard_map/ppermute | solution.py:61
  18.1 0.8 copy.16
  18.8 0.0 collective-permute-done.1
  18.8 0.0 collective-permute-done
  18.8 0.1 pad_add_fusion
  18.9 5.7 %collective-permute-start.3 = (s32[7,1,5]{0,1,2:T(1,128)S(1)}, s32[7,1,5]{0,1,2:T(1,128)S(1)}, u32[]{:S(2)}, u32[]{:S(2)}) collective-permute-start(s32[7,1,5]{0,1,2:T(1,128)S(1)} %get-tuple-element.91), channel_id=1, source_target_pairs={{0,14},{2,0},{4,2},{6,4},{8,6},{10,8},{12,10},{14,12},{1,15},{3,1}... | collective-permute-start | bytes 428 | tf_op jit(solution)/shard_map/ppermute | solution.py:61
  24.6 0.0 collective-permute-start.2
  24.6 0.7 collective-permute-done.3
  25.3 3.3 %collective-permute-done.2 = s32[7,1,5]{0,1,2:T(1,128)S(1)} collective-permute-done((s32[7,1,5]{0,1,2:T(1,128)S(1)}, s32[7,1,5]{0,1,2:T(1,128)S(1)}, u32[]{:S(2)}, u32[]{:S(2)}) %collective-permute-start.2) | collective-permute-done | bytes 172 | tf_op jit(solution)/shard_map/ppermute | solution.py:61
  28.6 0.0 collective-permute-start.5
  28.6 2.7 %collective-permute-start.6 = (f32[15,128,128]{2,1,0:T(8,128)}, f32[15,128,128]{2,1,0:T(8,128)}, u32[]{:S(2)}, u32[]{:S(2)}) collective-permute-start(f32[15,128,128]{2,1,0:T(8,128)} %copy-done.2), channel_id=1, source_target_pairs={{0,14},{2,0},{4,2},{6,4},{8,6},{10,8},{12,10},{14,12},{1,15},{3,1}... | collective-permute-start | bytes 2949128 | tf_op jit(solution)/shard_map/ppermute | solution.py:61
  31.3 0.8 copy.17
  32.1 0.0 copy-done.4
  32.1 0.1 select_add_fusion
  32.2 3.9 %all_gather.3 = s32[10,4,10]{0,1,2:T(4,128)S(1)} all-gather(s32[10,4,5]{0,1,2:T(4,128)S(1)} %select_add_fusion), channel_id=1, replica_groups=mesh['dom'=16,'col'=8,'rep'=2] {'rep'}, dimensions={2}, use_global_device_ids=true | all-gather | bytes 2400 | tf_op jit(solution)/shard_map/all_gather | solution.py:442
  36.1 0.1 copy.18.known
  36.2 12.3 %lists.1 = (s32[632]{0:T(1024)S(1)}, s32[632]{0:T(1024)S(1)}, s32[632]{0:T(1024)S(1)}, s32[632]{0:T(1024)S(1)}, s32[332]{0:T(512)S(1)}, /*index=5*/s32[632]{0:T(1024)S(1)}, s32[61]{0:T(128)S(1)}, s32[8]{0:T(128)S(1)}) custom-call(s32[10,4,10]{2,1,0:T(4,128)S(1)} %copy.18.known, s32[7,4,10]{2,1,0:T(4,128)S(1)} %broadcast_select_fusion.stored), custom_call_target="tpu_custom_call" | custom-call | flops 1000 | bytes 1000 | tf_op jit(solution)/shard_map/lists/pallas_call | solution.py:188
  48.6 0.0 collective-permute-done.4.refs_1_
  48.6 0.0 copy-done.1
  48.6 6.9 %first.1 = (bf16[281,128,256]{2,1,0:T(8,128)(2,1)S(1)}, f32[61,128,128]{2,1,0:T(8,128)S(1)}) custom-call(s32[632]{0:T(1024)S(1)} %get-tuple-element.59.codes, s32[8]{0:T(128)S(1)} %get-tuple-element.55.counts, f32[30,128,128]{2,1,0:T(8,128)S(1)} %bitcast.4, f32[30,128,128]{2,1,0:T(8,128)} %collective-permute-done.4.refs_1_), custom_call_target="tpu_custom_call" | custom-call | flops 1000 | bytes 1000 | tf_op jit(solution)/shard_map/first/pallas_call | solution.py:404
  55.5 0.0 collective-permute-done.5.refs_0_.refs_2_
  55.5 0.0 collective-permute-done.6.refs_1_.refs_3_
  55.6 0.0 collective-permute-done.7.refs_4_.refs_0_
  55.6 0.0 collective-permute-done.8.refs_5_.refs_1_
  55.6 0.4 collective-permute-start.11
  56.0 0.2 collective-permute-start.9
  56.2 0.3 collective-permute-start.10
  56.5 0.2 collective-permute-start.12
  56.7 2.1 %pack.3 = (f32[10,128,128]{2,1,0:T(8,128)S(1)}, f32[10,128,128]{2,1,0:T(8,128)S(1)}, f32[10,128,128]{2,1,0:T(8,128)S(1)}, f32[10,128,128]{2,1,0:T(8,128)S(1)}) custom-call(f32[20,128,128]{2,1,0:T(8,128)} %collective-permute-done.7.refs_4_.refs_0_, f32[20,128,128]{2,1,0:T(8,128)} %collective-permute-done.8.refs_5_.refs_1_, ...), custom_call_target="tpu_custom_call" | custom-call | flops 1000 | bytes 1000 | tf_op jit(solution)/shard_map/pack/pallas_call | solution.py:368
  58.8 0.1 collective-permute-start.13
  58.8 1.5 %collective-permute-done.9.refs_2_ = f32[15,128,128]{2,1,0:T(8,128)S(1)} collective-permute-done((f32[15,128,128]{2,1,0:T(8,128)}, f32[15,128,128]{2,1,0:T(8,128)S(1)}, u32[]{:S(2)}, u32[]{:S(2)}) %collective-permute-start.9) | collective-permute-done | bytes 983072 | tf_op jit(solution)/shard_map/ppermute | solution.py:61
  60.3 1.2 %collective-permute-start.14 = (f32[10,128,128]{2,1,0:T(8,128)S(1)}, f32[10,128,128]{2,1,0:T(8,128)S(1)}, u32[]{:S(2)}, u32[]{:S(2)}) collective-permute-start(f32[10,128,128]{2,1,0:T(8,128)S(1)} %get-tuple-element.77), channel_id=1, source_target_pairs={{0,14},{2,0},{4,2},{6,4},{8,6},{10,8},{12,10},{14,12},{1,15},{3,1}... | collective-permute-start | bytes 1966088 | tf_op jit(solution)/shard_map/ppermute | solution.py:61
  61.5 0.2 collective-permute-done.10.refs_3_
  61.7 0.0 collective-permute-start.15
  61.7 0.0 collective-permute-done.11.refs_6_
  61.7 4.8 %collective-permute-start.16 = (f32[10,128,128]{2,1,0:T(8,128)S(1)}, f32[10,128,128]{2,1,0:T(8,128)S(1)}, u32[]{:S(2)}, u32[]{:S(2)}) collective-permute-start(f32[10,128,128]{2,1,0:T(8,128)S(1)} %get-tuple-element.79), channel_id=1, source_target_pairs={{0,240},{16,0},{32,16},{48,32},{64,48},{80,64},{96,80},{112,96},{1... | collective-permute-start | bytes 1966088 | tf_op jit(solution)/shard_map/ppermute | solution.py:61
  66.5 0.0 collective-permute-done.12.refs_7_
  66.5 12.5 %early.1 = (bf16[281,128,256]{2,1,0:T(8,128)(2,1)S(1)}, f32[61,128,128]{2,1,0:T(8,128)S(1)}, bf16[121,128,256]{2,1,0:T(8,128)(2,1)S(1)}, f32[31,128,128]{2,1,0:T(8,128)S(1)}) custom-call(s32[632]{0:T(1024)S(1)} %get-tuple-element.57.codes, s32[332]{0:T(512)S(1)} %get-tuple-element.58.cube_codes, ...), custom_call_target="tpu_custom_call", output_to_operand_aliasing={{0}: (3, {}), {1}: (4, {})} | custom-call | flops 1000 | bytes 1000 | tf_op jit(solution)/shard_map/early/pallas_call | solution.py:404
  79.0 0.0 collective-permute-done.13.refs_0_
  79.0 0.0 collective-permute-done.14.refs_1_
  79.0 1.6 %collective-permute-done.15.refs_2_ = f32[10,128,128]{2,1,0:T(8,128)S(1)} collective-permute-done((f32[10,128,128]{2,1,0:T(8,128)S(1)}, f32[10,128,128]{2,1,0:T(8,128)S(1)}, u32[]{:S(2)}, u32[]{:S(2)}) %collective-permute-start.15) | collective-permute-done | bytes 655392 | tf_op jit(solution)/shard_map/ppermute | solution.py:61
  80.6 0.0 collective-permute-done.16.refs_3_
  80.6 1.6 %collective-permute-start.17 = (f32[10,128,128]{2,1,0:T(8,128)S(1)}, f32[10,128,128]{2,1,0:T(8,128)S(1)}, u32[]{:S(2)}, u32[]{:S(2)}) collective-permute-start(f32[10,128,128]{2,1,0:T(8,128)S(1)} %collective-permute-done.13.refs_0_), channel_id=1, source_target_pairs={{0,1},{1,0},{2,3},{3,2},{4,5},{5,4},{6,7},{7,6},{8,9},{9,8},{10,11... | collective-permute-start | bytes 1966088 | tf_op jit(solution)/shard_map/ppermute | solution.py:61
  82.2 0.0 collective-permute-start.18
  82.2 0.5 collective-permute-start.19
  82.7 0.0 collective-permute-start.20
  82.7 2.4 %corner.1 = (bf16[281,128,256]{2,1,0:T(8,128)(2,1)S(1)}, f32[61,128,128]{2,1,0:T(8,128)S(1)}) custom-call(s32[632]{0:T(1024)S(1)} %get-tuple-element.56.codes, s32[8]{0:T(128)S(1)} %get-tuple-element.55.counts, bf16[281,128,256]{2,1,0:T(8,128)(2,1)S(1)} %get-tuple-element.80.blocks_in, ...), custom_call_target="tpu_custom_call", output_to_operand_aliasing={{0}: (2, {}), {1}: (3, {})} | custom-call | flops 1000 | bytes 1000 | tf_op jit(solution)/shard_map/corner/pallas_call | solution.py:404
  85.1 0.0 collective-permute-done.17.refs_0_
  85.2 0.0 collective-permute-done.18.refs_1_
  85.2 0.6 collective-permute-done.19.refs_2_
  85.8 0.9 collective-permute-done.20.refs_3_
  86.7 6.9 %late.1 = (f32[30,128,128]{2,1,0:T(8,128)}, bf16[281,128,256]{2,1,0:T(8,128)(2,1)S(1)}, f32[61,128,128]{2,1,0:T(8,128)S(1)}, bf16[121,128,256]{2,1,0:T(8,128)(2,1)S(1)}, f32[31,128,128]{2,1,0:T(8,128)S(1)}) custom-call(s32[632]{0:T(1024)S(1)} %get-tuple-element.52.codes, ...), custom_call_target="tpu_custom_call", output_to_operand_aliasing={{1}: (4, {}), {2}: (5, {}), {3}: (6, {}), {4}: (7, {})} | custom-call | flops 1000 | bytes 1000 | tf_op jit(solution)/shard_map/late/pallas_call | solution.py:404
  (8 shorter events, 0.0 us)
Async XLA Ops:
  0.0 32.1 %copy-start.4 = (s32[7,4,10]{2,1,0:T(4,128)S(1)}, s32[7,4,10]{2,1,0:T(4,128)}, u32[]{:S(2)}) copy-start(s32[7,4,10]{2,1,0:T(4,128)} %constant.13.clone) | copy-start | bytes 3364
  0.0 32.1 %copy-start.5 = (s32[7,4,10]{2,1,0:T(4,128)S(1)}, s32[7,4,10]{2,1,0:T(4,128)}, u32[]{:S(2)}) copy-start(s32[7,4,10]{2,1,0:T(4,128)} %constant.12.clone) | copy-start | bytes 3364
  0.0 48.6 %collective-permute-start.4 = (f32[30,128,128]{2,1,0:T(8,128)}, f32[30,128,128]{2,1,0:T(8,128)}, u32[]{:S(2)}, u32[]{:S(2)}) collective-permute-start(f32[30,128,128]{2,1,0:T(8,128)} %bitcast.2), channel_id=1, source_target_pairs={{0,1},{1,0},{2,3},{3,2},{4,5},{5,4},{6,7},{7,6},{8,9},{9,8},{10,11... | collective-permute-start | bytes 5898248 | tf_op jit(solution)/shard_map/ppermute | solution.py:61
  4.1 14.7 %collective-permute-start.1 = (s32[2,2,5]{0,1,2:T(2,128)S(1)}, s32[2,2,5]{0,1,2:T(2,128)S(1)}, u32[]{:S(2)}, u32[]{:S(2)}) collective-permute-start(s32[2,2,5]{0,1,2:T(2,128)S(1)} %copy.15), channel_id=1, source_target_pairs={{0,240},{16,0},{32,16},{48,32},{64,48},{80,64},{96,80},{112,96},{1... | collective-permute-start | bytes 248 | tf_op jit(solution)/shard_map/ppermute | solution.py:61
  7.4 11.4 %collective-permute-start = (s32[2,2,5]{0,1,2:T(2,128)S(1)}, s32[2,2,5]{0,1,2:T(2,128)S(1)}, u32[]{:S(2)}, u32[]{:S(2)}) collective-permute-start(s32[2,2,5]{0,1,2:T(2,128)S(1)} %copy.14), channel_id=1, source_target_pairs={{0,16},{16,32},{32,48},{48,64},{64,80},{80,96},{96,112},{112,128},... | collective-permute-start | bytes 248 | tf_op jit(solution)/shard_map/ppermute | solution.py:61
  7.4 1.5 %copy-start = (f32[3,2,5,128,128]{4,3,2,1,0:T(8,128)S(1)}, f32[3,2,5,128,128]{4,3,2,1,0:T(8,128)}, u32[]{:S(2)}) copy-start(f32[3,2,5,128,128]{4,3,2,1,0:T(8,128)} %param.5) | copy-start | bytes 5898244
  9.0 39.7 %copy-start.1 = (f32[3,2,5,128,128]{4,3,2,1,0:T(8,128)S(1)}, f32[3,2,5,128,128]{4,3,2,1,0:T(8,128)}, u32[]{:S(2)}) copy-start(f32[3,2,5,128,128]{4,3,2,1,0:T(8,128)} %param.5) | copy-start | bytes 5898244
  11.3 1.0 %copy-start.2 = (f32[15,128,128]{2,1,0:T(8,128)}, f32[15,128,128]{2,1,0:T(8,128)S(1)}, u32[]{:S(2)}) copy-start(f32[15,128,128]{2,1,0:T(8,128)S(1)} %get-tuple-element.63) | copy-start | bytes 2949124
  12.3 0.9 %copy-start.3 = (f32[15,128,128]{2,1,0:T(8,128)}, f32[15,128,128]{2,1,0:T(8,128)S(1)}, u32[]{:S(2)}) copy-start(f32[15,128,128]{2,1,0:T(8,128)S(1)} %get-tuple-element.62) | copy-start | bytes 2949124
  13.3 42.3 %collective-permute-start.7 = (f32[20,128,128]{2,1,0:T(8,128)}, f32[20,128,128]{2,1,0:T(8,128)}, u32[]{:S(2)}, u32[]{:S(2)}) collective-permute-start(f32[20,128,128]{2,1,0:T(8,128)} %get-tuple-element.64), channel_id=1, source_target_pairs={{0,16},{16,32},{32,48},{48,64},{64,80},{80,96},{96,112},{112,128},... | collective-permute-start | bytes 3932168 | tf_op jit(solution)/shard_map/ppermute | solution.py:61
  13.3 42.3 %collective-permute-start.8 = (f32[20,128,128]{2,1,0:T(8,128)}, f32[20,128,128]{2,1,0:T(8,128)}, u32[]{:S(2)}, u32[]{:S(2)}) collective-permute-start(f32[20,128,128]{2,1,0:T(8,128)} %get-tuple-element.65), channel_id=1, source_target_pairs={{0,240},{16,0},{32,16},{48,32},{64,48},{80,64},{96,80},{112,96},{1... | collective-permute-start | bytes 3932168 | tf_op jit(solution)/shard_map/ppermute | solution.py:61
  18.9 6.4 %collective-permute-start.3 = (s32[7,1,5]{0,1,2:T(1,128)S(1)}, s32[7,1,5]{0,1,2:T(1,128)S(1)}, u32[]{:S(2)}, u32[]{:S(2)}) collective-permute-start(s32[7,1,5]{0,1,2:T(1,128)S(1)} %get-tuple-element.91), channel_id=1, source_target_pairs={{0,14},{2,0},{4,2},{6,4},{8,6},{10,8},{12,10},{14,12},{1,15},{3,1}... | collective-permute-start | bytes 428 | tf_op jit(solution)/shard_map/ppermute | solution.py:61
  24.6 4.1 %collective-permute-start.2 = (s32[7,1,5]{0,1,2:T(1,128)S(1)}, s32[7,1,5]{0,1,2:T(1,128)S(1)}, u32[]{:S(2)}, u32[]{:S(2)}) collective-permute-start(s32[7,1,5]{0,1,2:T(1,128)S(1)} %get-tuple-element.92), channel_id=1, source_target_pairs={{0,2},{2,4},{4,6},{6,8},{8,10},{10,12},{12,14},{14,0},{1,3},{3,5},... | collective-permute-start | bytes 428 | tf_op jit(solution)/shard_map/ppermute | solution.py:61
  28.6 26.9 %collective-permute-start.5 = (f32[15,128,128]{2,1,0:T(8,128)}, f32[15,128,128]{2,1,0:T(8,128)}, u32[]{:S(2)}, u32[]{:S(2)}) collective-permute-start(f32[15,128,128]{2,1,0:T(8,128)} %copy-done.3), channel_id=1, source_target_pairs={{0,2},{2,4},{4,6},{6,8},{8,10},{10,12},{12,14},{14,0},{1,3},{3,5},... | collective-permute-start | bytes 2949128 | tf_op jit(solution)/shard_map/ppermute | solution.py:61
  28.6 26.9 %collective-permute-start.6 = (f32[15,128,128]{2,1,0:T(8,128)}, f32[15,128,128]{2,1,0:T(8,128)}, u32[]{:S(2)}, u32[]{:S(2)}) collective-permute-start(f32[15,128,128]{2,1,0:T(8,128)} %copy-done.2), channel_id=1, source_target_pairs={{0,14},{2,0},{4,2},{6,4},{8,6},{10,8},{12,10},{14,12},{1,15},{3,1}... | collective-permute-start | bytes 2949128 | tf_op jit(solution)/shard_map/ppermute | solution.py:61
  55.6 6.2 %collective-permute-start.11 = (f32[20,128,128]{2,1,0:T(8,128)}, f32[20,128,128]{2,1,0:T(8,128)S(1)}, u32[]{:S(2)}, u32[]{:S(2)}) collective-permute-start(f32[20,128,128]{2,1,0:T(8,128)} %collective-permute-done.7.refs_4_.refs_0_), channel_id=1, source_target_pairs={{0,1},{1,0},{2,3},{3,2},{4,5},{5,4},{6,7},{7,6},{8,9},{9,8},{10,11... | collective-permute-start | bytes 3932168 | tf_op jit(solution)/shard_map/ppermute | solution.py:61
  56.0 4.3 %collective-permute-start.9 = (f32[15,128,128]{2,1,0:T(8,128)}, f32[15,128,128]{2,1,0:T(8,128)S(1)}, u32[]{:S(2)}, u32[]{:S(2)}) collective-permute-start(f32[15,128,128]{2,1,0:T(8,128)} %collective-permute-done.5.refs_0_.refs_2_), channel_id=1, source_target_pairs={{0,1},{1,0},{2,3},{3,2},{4,5},{5,4},{6,7},{7,6},{8,9},{9,8},{10,11... | collective-permute-start | bytes 2949128 | tf_op jit(solution)/shard_map/ppermute | solution.py:61
  56.2 5.5 %collective-permute-start.10 = (f32[15,128,128]{2,1,0:T(8,128)}, f32[15,128,128]{2,1,0:T(8,128)S(1)}, u32[]{:S(2)}, u32[]{:S(2)}) collective-permute-start(f32[15,128,128]{2,1,0:T(8,128)} %collective-permute-done.6.refs_1_.refs_3_), channel_id=1, source_target_pairs={{0,1},{1,0},{2,3},{3,2},{4,5},{5,4},{6,7},{7,6},{8,9},{9,8},{10,11... | collective-permute-start | bytes 2949128 | tf_op jit(solution)/shard_map/ppermute | solution.py:61
  56.5 10.0 %collective-permute-start.12 = (f32[20,128,128]{2,1,0:T(8,128)}, f32[20,128,128]{2,1,0:T(8,128)S(1)}, u32[]{:S(2)}, u32[]{:S(2)}) collective-permute-start(f32[20,128,128]{2,1,0:T(8,128)} %collective-permute-done.8.refs_5_.refs_1_), channel_id=1, source_target_pairs={{0,1},{1,0},{2,3},{3,2},{4,5},{5,4},{6,7},{7,6},{8,9},{9,8},{10,11... | collective-permute-start | bytes 3932168 | tf_op jit(solution)/shard_map/ppermute | solution.py:61
  58.8 20.3 %collective-permute-start.13 = (f32[10,128,128]{2,1,0:T(8,128)S(1)}, f32[10,128,128]{2,1,0:T(8,128)S(1)}, u32[]{:S(2)}, u32[]{:S(2)}) collective-permute-start(f32[10,128,128]{2,1,0:T(8,128)S(1)} %get-tuple-element.76), channel_id=1, source_target_pairs={{0,2},{2,4},{4,6},{6,8},{8,10},{10,12},{12,14},{14,0},{1,3},{3,5},... | collective-permute-start | bytes 1966088 | tf_op jit(solution)/shard_map/ppermute | solution.py:61
  60.3 18.7 %collective-permute-start.14 = (f32[10,128,128]{2,1,0:T(8,128)S(1)}, f32[10,128,128]{2,1,0:T(8,128)S(1)}, u32[]{:S(2)}, u32[]{:S(2)}) collective-permute-start(f32[10,128,128]{2,1,0:T(8,128)S(1)} %get-tuple-element.77), channel_id=1, source_target_pairs={{0,14},{2,0},{4,2},{6,4},{8,6},{10,8},{12,10},{14,12},{1,15},{3,1}... | collective-permute-start | bytes 1966088 | tf_op jit(solution)/shard_map/ppermute | solution.py:61
  61.7 18.9 %collective-permute-start.15 = (f32[10,128,128]{2,1,0:T(8,128)S(1)}, f32[10,128,128]{2,1,0:T(8,128)S(1)}, u32[]{:S(2)}, u32[]{:S(2)}) collective-permute-start(f32[10,128,128]{2,1,0:T(8,128)S(1)} %get-tuple-element.78), channel_id=1, source_target_pairs={{0,16},{16,32},{32,48},{48,64},{64,80},{80,96},{96,112},{112,128},... | collective-permute-start | bytes 1966088 | tf_op jit(solution)/shard_map/ppermute | solution.py:61
  61.7 18.9 %collective-permute-start.16 = (f32[10,128,128]{2,1,0:T(8,128)S(1)}, f32[10,128,128]{2,1,0:T(8,128)S(1)}, u32[]{:S(2)}, u32[]{:S(2)}) collective-permute-start(f32[10,128,128]{2,1,0:T(8,128)S(1)} %get-tuple-element.79), channel_id=1, source_target_pairs={{0,240},{16,0},{32,16},{48,32},{64,48},{80,64},{96,80},{112,96},{1... | collective-permute-start | bytes 1966088 | tf_op jit(solution)/shard_map/ppermute | solution.py:61
  80.6 4.5 %collective-permute-start.17 = (f32[10,128,128]{2,1,0:T(8,128)S(1)}, f32[10,128,128]{2,1,0:T(8,128)S(1)}, u32[]{:S(2)}, u32[]{:S(2)}) collective-permute-start(f32[10,128,128]{2,1,0:T(8,128)S(1)} %collective-permute-done.13.refs_0_), channel_id=1, source_target_pairs={{0,1},{1,0},{2,3},{3,2},{4,5},{5,4},{6,7},{7,6},{8,9},{9,8},{10,11... | collective-permute-start | bytes 1966088 | tf_op jit(solution)/shard_map/ppermute | solution.py:61
  82.2 3.0 %collective-permute-start.18 = (f32[10,128,128]{2,1,0:T(8,128)S(1)}, f32[10,128,128]{2,1,0:T(8,128)S(1)}, u32[]{:S(2)}, u32[]{:S(2)}) collective-permute-start(f32[10,128,128]{2,1,0:T(8,128)S(1)} %collective-permute-done.14.refs_1_), channel_id=1, source_target_pairs={{0,1},{1,0},{2,3},{3,2},{4,5},{5,4},{6,7},{7,6},{8,9},{9,8},{10,11... | collective-permute-start | bytes 1966088 | tf_op jit(solution)/shard_map/ppermute | solution.py:61
  82.2 3.6 %collective-permute-start.19 = (f32[10,128,128]{2,1,0:T(8,128)S(1)}, f32[10,128,128]{2,1,0:T(8,128)S(1)}, u32[]{:S(2)}, u32[]{:S(2)}) collective-permute-start(f32[10,128,128]{2,1,0:T(8,128)S(1)} %collective-permute-done.15.refs_2_), channel_id=1, source_target_pairs={{0,1},{1,0},{2,3},{3,2},{4,5},{5,4},{6,7},{7,6},{8,9},{9,8},{10,11... | collective-permute-start | bytes 1966088 | tf_op jit(solution)/shard_map/ppermute | solution.py:61
  82.7 4.0 %collective-permute-start.20 = (f32[10,128,128]{2,1,0:T(8,128)S(1)}, f32[10,128,128]{2,1,0:T(8,128)S(1)}, u32[]{:S(2)}, u32[]{:S(2)}) collective-permute-start(f32[10,128,128]{2,1,0:T(8,128)S(1)} %collective-permute-done.16.refs_3_), channel_id=1, source_target_pairs={{0,1},{1,0},{2,3},{3,2},{4,5},{5,4},{6,7},{7,6},{8,9},{9,8},{10,11... | collective-permute-start | bytes 1966088 | tf_op jit(solution)/shard_map/ppermute | solution.py:61

commit v2 on v1

v2 whole, which is shorter than its diff:
```python
import functools

import jax
import jax.numpy as jnp
import numpy as np
from jax import lax
from jax.experimental import pallas as pl
from jax.experimental.pallas import tpu as pltpu
from jax.sharding import PartitionSpec as P

UNROLL = 32
ROWS, COLS = 3, 2
HALF = 5
RIM_D, RIM_C = ROWS + 4, COLS + 2
RIM = RIM_D * RIM_C
CELLS = ROWS * COLS
SLOTS = 2 * HALF
OWN = 60
EARLY = 200
ROWS_PART = 70
LATE = 40
ZERO = EARLY + 2 * LATE
TOTAL = ZERO + 1
SPOT = OWN


def block_places(core):
    places = np.zeros((RIM_D, RIM_C, SLOTS), np.int32)
    for rd in range(RIM_D):
        for rc in range(RIM_C):
            for t in range(SLOTS):
                half, s = divmod(t, HALF)
                other = int(half != core)
                mid_d, mid_c = 2 <= rd < 2 + ROWS, 1 <= rc < 1 + COLS
                low, far = int(rd >= 2 + ROWS), int(rc == RIM_C - 1)
                row = rd - 2 - ROWS if low else rd
                if mid_d and mid_c:
                    at = other * 30 + ((rd - 2) * 2 + rc - 1) * 5 + s
                elif mid_d:
                    at = OWN + other * ROWS_PART + far * 15 + (rd - 2) * 5 + s
                elif mid_c:
                    at = OWN + other * ROWS_PART + 30 + int(low != half) * 20 + (row * 2 + rc - 1) * 5 + s
                else:
                    at = EARLY + other * LATE + int(low != half) * 20 + far * 10 + row * 5 + s
                places[rd, rc, t] = at
    return places


def shift(array, axis, step):
    peers = lax.axis_size(axis)
    return lax.ppermute(array, axis, [(i, (i + step) % peers) for i in range(peers)])


def cross(array, step):
    peers = lax.axis_size("dom")
    pairs = [(2 * i + core, (i + (step, -step)[core]) % peers * 2 + core) for i in range(peers) for core in range(2)]
    return lax.ppermute(array, ("dom", "rep"), pairs)


SQUARE_LEN = SPOT * SLOTS + UNROLL
CUBE_LEN = CELLS * HALF * SLOTS + UNROLL
TAIL_LEN = 2 * CELLS * HALF * SLOTS + UNROLL
LANES = 128
NONE = RIM + 3
TABLE = 32


def list_kernel(
    grid, known, stored, early, late, cube, tail, touched, counts, table_v, place_v, table, place, flag, sems
):
    grid_d, grid_c = grid
    dom, col, rep = lax.axis_index("dom"), lax.axis_index("col"), lax.axis_index("rep")
    lane = lax.broadcasted_iota(jnp.int32, (1, LANES), 1)
    names = jnp.full((1, LANES), -5, jnp.int32)
    name = []
    for j in range(RIM):
        d, c = dom * ROWS + (j // RIM_C - 2), col * COLS + (j % RIM_C - 1)
        d = jnp.where(d < 0, d + grid_d, jnp.where(d >= grid_d, d - grid_d, d))
        c = jnp.where(c < 0, c + grid_c, jnp.where(c >= grid_c, c - grid_c, c))
        name.append(d * grid_c + c)
        names = jnp.where(lane == j, name[j], names)
    table_v[...] = jnp.full((TABLE, LANES), -1, jnp.int32)
    for r in range(RIM_D):
        x, at = known[r], stored[r]
        row = jnp.full((RIM_C, LANES), -1, jnp.int32)
        for t in range(SLOTS):
            row = jnp.where(x[:, t:t + 1] == names, at[:, t:t + 1], row)
        table_v[r * RIM_C:(r + 1) * RIM_C, :] = row
    one = pltpu.make_async_copy(table_v, table, sems.at[0])
    one.start()
    for q in range(2):
        for r in range(ROWS):
            x = known[2 + r, 1:1 + COLS] if q == 0 else known[RIM_D + r, :COLS]
            at = jnp.full((COLS, SLOTS), NONE, jnp.int32)
            for j in range(RIM):
                at = jnp.where(x == name[j], j, at)
            place_v[q * CELLS + r * COLS:q * CELLS + (r + 1) * COLS, :SLOTS] = at
    two = pltpu.make_async_copy(place_v, place, sems.at[1])
    two.start()
    two.wait()
    one.wait()

    blank = ZERO | (ZERO << 10) | (SPOT << 20)
    blank_cube = 2 * SPOT | (ZERO << 10) | ((CELLS * HALF) << 20)

    def square_cell(i, carry):
        rows = [place[i, s] for s in range(SLOTS)]
        own = [i * HALF + s % HALF + jnp.where(rep == s // HALF, 0, CELLS * HALF) for s in range(SLOTS)]

        def square_row(f, carry):
            ne, nl, nt = carry
            before = nl
            k = place[CELLS + i, f]
            spot = i * SLOTS + f
            o = spot << 20
            values = [table[j, k] for j in rows]
            for s in range(SLOTS):
                v = values[s]
                code = (own[s] | o) + (v << 10)
                early[ne] = code
                late[nl] = code
                is_late = jnp.where(v >= EARLY, 1, 0)
                ne = ne + jnp.where(v >= 0, 1, 0) - is_late
                nl = nl + is_late
            again = jnp.where(nl > before, 1, 0)
            flag[spot] = again
            touched[nt] = spot
            return ne, nl, nt + again

        return lax.fori_loop(0, SLOTS, square_row, carry)

    def cube_cell(i, carry):
        rows = [place[CELLS + i, g] for g in range(SLOTS)]
        again = [flag[i * SLOTS + g] for g in range(SLOTS)]

        def cube_row(f, carry):
            nc, nt = carry
            k = place[CELLS + i, rep * HALF + f]
            o = (i * SLOTS) | ((i * HALF + f) << 20)
            values = [table[j, k] for j in rows]
            for g in range(SLOTS):
                v = values[g]
                code = (o + (g + SPOT)) | (v << 10)
                hit, is_late = jnp.where(v >= 0, 1, 0), jnp.where(v >= EARLY, 1, 0)
                cube[nc] = code
                nc = nc + hit - is_late
                tail[nt] = code
                nt = nt + is_late
                tail[nt] = code - SPOT
                nt = nt + hit * again[g]
            return nc, nt

        return lax.fori_loop(0, HALF, cube_row, carry)

    zero = jnp.int32(0)
    ne, nl, touches = lax.fori_loop(0, CELLS, square_cell, (zero,) * 3)
    nc, nt = lax.fori_loop(0, CELLS, cube_cell, (zero, zero))
    for u in range(UNROLL):
        early[ne + u] = blank
        late[nl + u] = blank
        cube[nc + u] = blank_cube
        tail[nt + u] = blank_cube
    for q, n in enumerate((ne, nl, nc, nt)):
        counts[q] = n
    counts[6] = touches
    counts[7] = rep * HALF


def make_lists(known, stored):
    grid = (ROWS * lax.axis_size("dom"), COLS * lax.axis_size("col"))
    lengths = (SQUARE_LEN,) * 2 + (CUBE_LEN, TAIL_LEN, SPOT + 1, 8)
    return pl.pallas_call(
        functools.partial(list_kernel, grid),
        out_shape=[jax.ShapeDtypeStruct((n,), jnp.int32) for n in lengths],
        in_specs=[vmem()] * 2,
        out_specs=[smem()] * len(lengths),
        scratch_shapes=[
            pltpu.VMEM((TABLE, LANES), jnp.int32),
            pltpu.VMEM((16, LANES), jnp.int32),
            pltpu.SMEM((TABLE, LANES), jnp.int32),
            pltpu.SMEM((16, LANES), jnp.int32),
            pltpu.SMEM((SPOT,), jnp.int32),
            pltpu.SemaphoreType.DMA((2,)),
        ],
        compiler_params=pltpu.CompilerParams(vmem_limit_bytes=2 << 20),
        cost_estimate=pl.CostEstimate(flops=1000, bytes_accessed=1000, transcendentals=0),
        name="lists",
    )(known, stored)


def split(x):
    high = x.astype(jnp.bfloat16)
    low = (x - high.astype(jnp.float32)).astype(jnp.bfloat16)
    return high, low


def split_blocks(src, src_at, dst, dst_at, count):
    def step(b, _):
        high, low = split(src[src_at + b])
        dst[dst_at + b, :, :128] = high
        dst[dst_at + b, :, 128:] = low
        return 0

    lax.fori_loop(0, count, step, 0, unroll=2)


def run_list(codes, count, left, right, total, unroll=UNROLL):
    def step(at, _):
        for u in range(unroll):
            code = codes[at * unroll + u]
            b = right[(code >> 10) & 1023]
            out = jnp.dot(left[code & 1023], jnp.concatenate([b, b], axis=0), preferred_element_type=jnp.float32)
            total[code >> 20] += out[:, :128] + out[:, 128:]
        return 0

    lax.fori_loop(0, (count + unroll - 1) // unroll, step, 0)


def zero_blocks(ref, count):
    def step(b, _):
        ref[b] = jnp.zeros(ref.shape[1:], ref.dtype)
        return 0

    lax.fori_loop(0, count, step, 0)


DEPTH, CHUNK = 3, 20


def chunks(pieces):
    result, at = [], 0
    for piece in pieces:
        parts = -(-piece.shape[0] // CHUNK)
        size = piece.shape[0] // parts
        for part in range(parts):
            result.append((piece, part * size, size, at))
            at += size
    return result


def load_and_split(pieces, stage, sems, blocks, base, prepare=lambda: None):
    copies, parts = [], chunks(pieces)
    for n, (piece, start, size, _) in enumerate(parts):
        slot = stage.at[pl.ds(n % DEPTH * CHUNK, size)]
        copies.append(pltpu.make_async_copy(piece.at[pl.ds(start, size)], slot, sems.at[n]))
    for copy in copies[:DEPTH]:
        copy.start()
    prepare()
    for n, (_, _, size, at) in enumerate(parts):
        copies[n].wait()
        split_blocks(stage, n % DEPTH * CHUNK, blocks, base + at, size)
        if n + DEPTH < len(parts):
            copies[n + DEPTH].start()


def first_kernel(*refs):
    pieces, (blocks, square, stage, sems) = refs[:-4], refs[-4:]

    def prepare():
        blocks[ZERO] = jnp.zeros(blocks.shape[1:], blocks.dtype)
        zero_blocks(square, SPOT + 1)

    load_and_split(pieces, stage, sems, blocks, 0, prepare)


def rows_kernel(_, *refs):
    pieces, (blocks, stage, sems) = refs[:-3], refs[-3:]
    load_and_split(pieces, stage, sems, blocks, OWN)


def early_kernel(codes, cube_codes, counts, _, square_in, *refs):
    pieces, (blocks, square, halves, cube, stage, sems) = refs[:-6], refs[-6:]

    def prepare():
        zero_blocks(cube, CELLS * HALF + 1)
        halves[2 * SPOT] = jnp.zeros(blocks.shape[1:], blocks.dtype)

    load_and_split(pieces, stage, sems, blocks, OWN + ROWS_PART, prepare)
    run_list(codes, counts[0], blocks, blocks, square)
    split_blocks(square, 0, halves, SPOT, SPOT)
    run_list(cube_codes, counts[2], halves, blocks, cube)
    base = counts[7]

    def combine(i, _):
        for f in range(HALF):
            cube[i * HALF + f] = cube[i * HALF + f] - 1.5 * square[i * SLOTS + base + f]
        return 0

    lax.fori_loop(0, CELLS, combine, 0)
    zero_blocks(square, SPOT + 1)


def corner_kernel(_, *refs):
    pieces, (blocks, stage, sems) = refs[:-3], refs[-3:]
    load_and_split(pieces, stage, sems, blocks, EARLY)


def late_kernel(codes, tail_codes, touched, counts, blocks_in, square_in, halves_in, cube_in, *refs):
    pieces, (out, blocks, square, halves, cube, stage, sems) = refs[:-7], refs[-7:]
    load_and_split(pieces, stage, sems, blocks, EARLY + LATE)
    run_list(codes, counts[1], blocks, blocks, square, 8)

    def resplit(n, _):
        o = touched[n]
        high, low = split(square[o])
        halves[o, :, :128] = high
        halves[o, :, 128:] = low
        return 0

    lax.fori_loop(0, counts[6], resplit, 0)
    run_list(tail_codes, counts[3], halves, blocks, cube, 16)
    base = counts[7]
    copies = []
    for i in range(CELLS):
        for f in range(HALF):
            o = i * HALF + f
            stage[o] = 3.0 * square[i * SLOTS + base + f] - 2.0 * cube[o]
        at = pl.ds(i * HALF, HALF)
        copies.append(pltpu.make_async_copy(stage.at[at], out.at[at], sems.at[i]))
        copies[-1].start()
    for copy in copies:
        copy.wait()


def pack_kernel(plan, count, *refs):
    sources, dests, sems = refs[:count], refs[count:-1], refs[-1]
    run_plan(plan, sources, dests, sems)


def pack_far_kernel(plan, source, *refs):
    dests, held, sems = refs[:-2], refs[-2], refs[-1]
    copy = pltpu.make_async_copy(source, held, sems.at[0])
    copy.start()
    copy.wait()
    run_plan(plan, [held], dests, sems)


def run_plan(plan, sources, dests, sems):
    copies = []
    rep = lax.axis_index("rep")
    for n, (d, at, q, start, length) in enumerate(plan):
        if isinstance(start, tuple):
            start = jnp.where(rep == 0, start[0], start[1])
        copies.append(pltpu.make_async_copy(sources[q].at[pl.ds(start, length)], dests[d].at[pl.ds(at, length)], sems.at[n]))
        copies[-1].start()
    for copy in copies:
        copy.wait()


def pack(arrays, wanted, far=False):
    plan, sizes = [], []
    for d, ranges in enumerate(wanted):
        at = 0
        for q, start, length in ranges:
            plan.append((d, at, q, start, length))
            at += length
        sizes.append(at)
    out = pltpu.HBM if far else jax.ShapeDtypeStruct
    held = [pltpu.VMEM(arrays[0].shape, jnp.float32)] if far else []
    kernel = functools.partial(pack_far_kernel, tuple(plan)) if far else functools.partial(pack_kernel, tuple(plan), len(arrays))
    return pl.pallas_call(
        kernel,
        out_shape=[out((n, 128, 128), jnp.float32) for n in sizes],
        in_specs=[anyspace()] * len(arrays),
        out_specs=[hbm() if far else vmem()] * len(sizes),
        scratch_shapes=held + [pltpu.SemaphoreType.DMA((len(plan),))],
        compiler_params=pltpu.CompilerParams(vmem_limit_bytes=3 << 20),
        cost_estimate=pl.CostEstimate(flops=1000, bytes_accessed=1000, transcendentals=0),
        name="pack",
    )(*arrays)


def smem():
    return pl.BlockSpec(memory_space=pltpu.SMEM)


def anyspace():
    return pl.BlockSpec(memory_space=pl.ANY)


def vmem():
    return pl.BlockSpec(memory_space=pltpu.VMEM)


def hbm():
    return pl.BlockSpec(memory_space=pltpu.HBM)


BLOCKS = pltpu.VMEM((TOTAL, 128, 256), jnp.bfloat16)
SQUARE = pltpu.VMEM((SPOT + 1, 128, 128), jnp.float32)
HALVES = pltpu.VMEM((2 * SPOT + 1, 128, 256), jnp.bfloat16)
CUBE = pltpu.VMEM((CELLS * HALF + 1, 128, 128), jnp.float32)


def call(kernel, name, lists, held, pieces, outs, aliases):
    kinds = [hbm() if isinstance(o, jax.ShapeDtypeStruct) else vmem() for o in outs]
    return pl.pallas_call(
        kernel,
        out_shape=outs,
        in_specs=[smem()] * len(lists) + [vmem()] * len(held) + [anyspace()] * len(pieces),
        out_specs=kinds,
        scratch_shapes=[pltpu.VMEM((DEPTH * CHUNK, 128, 128), jnp.float32), pltpu.SemaphoreType.DMA((16,))],
        input_output_aliases={len(lists) + i: o for i, o in aliases.items()},
        compiler_params=pltpu.CompilerParams(vmem_limit_bytes=4 << 20),
        cost_estimate=pl.CostEstimate(flops=1000, bytes_accessed=1000, transcendentals=0),
        name=name,
    )(*lists, *held, *pieces)


def stored_places():
    return jnp.where(lax.axis_index("rep") == 0, block_places(0), block_places(1))


def flat(x):
    return x.reshape(-1, 128, 128)


def body(density, pattern, filt):
    blocks = flat(density)
    row = COLS * HALF
    above, below = shift(pattern[1:], "dom", 1), shift(pattern[:2], "dom", -1)
    own_other = shift(blocks, "rep", 1)
    one, two = pack([blocks], [[(0, (row, 0), 2 * row)], [(0, (0, row), 2 * row)]], far=True)
    above, below, one = lax.optimization_barrier((above, below, one))
    one = cross(one, 1)
    near = jnp.concatenate([above, pattern, below], axis=0)
    before, after = shift(near[:, 1:], "col", 1), shift(near[:, :1], "col", -1)
    edge_r, edge_l = pack([blocks], [[(0, r * row + q, HALF) for r in range(ROWS)] for q in (HALF, 0)])
    before, after, two, edge_r, edge_l = lax.optimization_barrier((before, after, two, edge_r, edge_l))
    two = cross(two, -1)
    right, left = shift(edge_r, "col", 1), shift(edge_l, "col", -1)
    rim = jnp.concatenate([before, near, after], axis=1)
    own_filt = jnp.pad(filt, ((0, 0), (0, RIM_C - COLS), (0, 0)), constant_values=-1)
    known = lax.all_gather(jnp.concatenate([rim, own_filt], axis=0), "rep", axis=2, tiled=True)
    early_codes, late_codes, cube_codes, tail_codes, touched, counts = make_lists(known, stored_places())
    counts, own_other = lax.optimization_barrier((counts, own_other))
    held, square = call(first_kernel, "first", [], [], [blocks, own_other], [BLOCKS, SQUARE], {})
    held, square, one = lax.optimization_barrier((held, square, one))
    to_r, to_l = pack([one], [[(0, q, HALF), (0, row + q, HALF)] for q in (HALF, 0)])
    corner_r, corner_l = shift(to_r, "col", 1), shift(to_l, "col", -1)
    right, left, to_r, to_l = lax.optimization_barrier((right, left, to_r, to_l))
    (corner,) = pack([right, left], [[(q, (0, HALF), 2 * HALF) for q in (0, 1)]])
    right, left, two, corner = lax.optimization_barrier((right, left, two, corner))
    corner = cross(corner, -1)
    mine = [right, left, one, two]
    others = [shift(p, "rep", 1) for p in mine]
    (held,) = call(rows_kernel, "rows", [], [held], mine, [BLOCKS], {0: 0})
    held, square, halves, cube = call(
        early_kernel, "early", [early_codes, cube_codes, counts], [held, square], others,
        [BLOCKS, SQUARE, HALVES, CUBE], {0: 0, 1: 1},
    )
    held, square, halves, cube, *corners = lax.optimization_barrier(
        (held, square, halves, cube, corner_r, corner_l, corner)
    )
    others = [shift(p, "rep", 1) for p in corners]
    (held,) = call(corner_kernel, "corner", [], [held], corners, [BLOCKS], {0: 0})
    out = jax.ShapeDtypeStruct((CELLS * HALF, 128, 128), jnp.float32)
    out = call(
        late_kernel, "late", [late_codes, tail_codes, touched, counts], [held, square, halves, cube], others,
        [out, BLOCKS, SQUARE, HALVES, CUBE], {0: 1, 1: 2, 2: 3, 3: 4},
    )[0]
    return out.reshape(density.shape)


def solution(mesh):
    in_specs = (P("dom", "col", "rep", None, None), P("dom", "col", "rep"), P("dom", "col", "rep"))
    out_specs = P("dom", "col", "rep", None, None)
    return jax.shard_map(body, mesh=mesh, in_specs=in_specs, out_specs=out_specs, check_vma=False)
```

time: 93.5 us -> 83.7 us (0.90)
  Pallas kernels: 45.5 us -> 38.2 us
  starting transfers between devices: 28.8 us -> 24.1 us
  blocking collectives: 3.94 us -> 7.41 us
  local copies, waits for them, and re-layouts: 6.09 us -> 3.51 us
  waiting for transfers between devices: 8.92 us -> 10.5 us
    ppermute x21 -> x16, starting transfers between devices: 28.8 us -> 22.5 us  [shift(): lax.ppermute(array, axis, [(i, (i + step) % peers) for i in range(peers)])]
    pallas_call x4 -> x5, Pallas kernels: 28.7 us -> 23.2 us  [call(): pl.pallas_call(kernel, out_shape=outs, in_specs=[smem()] * len(lists) + [...]
    all_gather x1, blocking collectives: 3.94 us -> 7.41 us  [body(): lax.all_gather(jnp.concatenate([rim, own_filt], axis=0), 'rep', axis=2, t...]
    pallas_call x1, Pallas kernels: 12.3 us -> 9.48 us  [make_lists(): pl.pallas_call(functools.partial(list_kernel, grid), out_shape=[jax.Shape...]
    unnamed x14 -> x12, local copies, waits for them, and re-layouts: 5.02 us -> 2.44 us
    ppermute x0 -> x3, starting transfers between devices: none -> 1.64 us  [cross(): return lax.ppermute(array, ('dom', 'rep'), pairs)]
    pallas_call x2 -> x4, Pallas kernels: 4.44 us -> 5.57 us  [pack(): pl.pallas_call(kernel, out_shape=[out((n, 128, 128), jnp.float32) for n i...]
    ppermute x0 -> x3, waiting for transfers between devices: none -> 1.07 us  [cross(): return lax.ppermute(array, ('dom', 'rep'), pairs)]
  transfers between devices with their start and end apart: 21 -> 19, of which waited for: 7 -> 6; matrix products, arithmetic and copies ran while one was open for 3% -> 3% of each run, Pallas kernels for 41% -> 39%
where the time goes in v2:
time: 83.7 us; the launch traced here: 84.3 us
  Pallas kernels  38.2 us (46%)
  starting transfers between devices  24.1 us (29%)
  waiting for transfers between devices  10.5 us (13%)
  blocking collectives  7.41 us (9%)
  local copies, waits for them, and re-layouts  3.51 us (4%)
    pallas_call x5, Pallas kernels, call(): pl.pallas_call(kernel, out_shape=outs, in_specs=[smem()] * len(lists) + [...  23.2 us
    ppermute x16, starting transfers between devices, shift(): lax.ppermute(array, axis, [(i, (i + step) % peers) for i in range(peers)])  22.5 us
    pallas_call x1, Pallas kernels, make_lists(): pl.pallas_call(functools.partial(list_kernel, grid), out_shape=[jax.Shape...  9.48 us
    ppermute x16, waiting for transfers between devices, shift(): lax.ppermute(array, axis, [(i, (i + step) % peers) for i in range(peers)])  9.45 us
    all_gather x1, blocking collectives, body(): lax.all_gather(jnp.concatenate([rim, own_filt], axis=0), 'rep', axis=2, t...  7.41 us
    pallas_call x4, Pallas kernels, pack(): pl.pallas_call(kernel, out_shape=[out((n, 128, 128), jnp.float32) for n i...  5.57 us
    unnamed x12, local copies, waits for them, and re-layouts  2.44 us
  transfers between devices with their start and end apart: 19, of which 6 were waited for; matrix products, arithmetic and copies ran while one was open for 3% of the time, Pallas kernels for 39%

profile of v2, /device:TPU:1, one launch (start us, length us, event | category | flops | bytes accessed | tf_op | source)
XLA Modules:
  0.0 84.3 jit_solution(17144680726066501949)
XLA Ops:
  0.0 0.0 copy-start.2
  0.0 0.0 copy-start.3
  0.0 3.2 %collective-permute-start.4 = (f32[30,128,128]{2,1,0:T(8,128)}, f32[30,128,128]{2,1,0:T(8,128)}, u32[]{:S(2)}, u32[]{:S(2)}) collective-permute-start(f32[30,128,128]{2,1,0:T(8,128)} %bitcast.2), channel_id=1, source_target_pairs={{0,1},{1,0},{2,3},{3,2},{4,5},{5,4},{6,7},{7,6},{8,9},{9,8},{10,11... | collective-permute-start | bytes 5898248 | tf_op jit(solution)/shard_map/ppermute | solution.py:51
  3.2 0.8 fusion.1
  4.0 0.1 copy.14
  4.1 0.0 collective-permute-start
  4.1 0.1 copy.15
  4.2 4.8 %collective-permute-start.1 = (s32[2,2,5]{0,1,2:T(2,128)S(1)}, s32[2,2,5]{0,1,2:T(2,128)S(1)}, u32[]{:S(2)}, u32[]{:S(2)}) collective-permute-start(s32[2,2,5]{0,1,2:T(2,128)S(1)} %copy.15), channel_id=1, source_target_pairs={{0,240},{16,0},{32,16},{48,32},{64,48},{80,64},{96,80},{112,96},{1... | collective-permute-start | bytes 248 | tf_op jit(solution)/shard_map/ppermute | solution.py:51
  9.0 1.5 %copy-done = f32[3,2,5,128,128]{4,3,2,1,0:T(8,128)S(1)} copy-done((f32[3,2,5,128,128]{4,3,2,1,0:T(8,128)S(1)}, f32[3,2,5,128,128]{4,3,2,1,0:T(8,128)}, u32[]{:S(2)}) %copy-start) | copy-done | bytes 1966104
  10.5 1.8 %pack.4 = (f32[20,128,128]{2,1,0:T(8,128)}, f32[20,128,128]{2,1,0:T(8,128)}) custom-call(f32[30,128,128]{2,1,0:T(8,128)S(1)} %bitcast.3), custom_call_target="tpu_custom_call" | custom-call | flops 1000 | bytes 1000 | tf_op jit(solution)/shard_map/pack/pallas_call | solution.py:361
  12.4 0.8 copy.16
  13.1 0.0 collective-permute-done
  13.1 0.0 collective-permute-done.1
  13.1 1.6 %collective-permute-start.5 = (f32[20,128,128]{2,1,0:T(8,128)}, f32[20,128,128]{2,1,0:T(8,128)S(1)}, u32[]{:S(2)}, u32[]{:S(2)}) collective-permute-start(f32[20,128,128]{2,1,0:T(8,128)} %get-tuple-element.68), channel_id=1, source_target_pairs={{0,16},{1,241},{16,32},{17,1},{32,48},{33,17},{48,64},{49,33},{64,... | collective-permute-start | bytes 3932168 | tf_op jit(solution)/shard_map/ppermute | solution.py:57
  14.8 0.1 pad_add_fusion
  14.9 4.1 %collective-permute-start.3 = (s32[7,1,5]{0,1,2:T(1,128)S(1)}, s32[7,1,5]{0,1,2:T(1,128)S(1)}, u32[]{:S(2)}, u32[]{:S(2)}) collective-permute-start(s32[7,1,5]{0,1,2:T(1,128)S(1)} %get-tuple-element.95), channel_id=1, source_target_pairs={{0,14},{2,0},{4,2},{6,4},{8,6},{10,8},{12,10},{14,12},{1,15},{3,1}... | collective-permute-start | bytes 428 | tf_op jit(solution)/shard_map/ppermute | solution.py:51
  18.9 0.0 collective-permute-start.2
  18.9 0.0 copy-done.1
  18.9 2.0 %pack.5 = (f32[15,128,128]{2,1,0:T(8,128)}, f32[15,128,128]{2,1,0:T(8,128)}) custom-call(f32[30,128,128]{2,1,0:T(8,128)S(1)} %bitcast.4), custom_call_target="tpu_custom_call" | custom-call | flops 1000 | bytes 1000 | tf_op jit(solution)/shard_map/pack/pallas_call | solution.py:361
  20.9 0.0 collective-permute-done.3
  21.0 1.9 %collective-permute-done.2 = s32[7,1,5]{0,1,2:T(1,128)S(1)} collective-permute-done((s32[7,1,5]{0,1,2:T(1,128)S(1)}, s32[7,1,5]{0,1,2:T(1,128)S(1)}, u32[]{:S(2)}, u32[]{:S(2)}) %collective-permute-start.2) | collective-permute-done | bytes 172 | tf_op jit(solution)/shard_map/ppermute | solution.py:51
  22.9 0.0 collective-permute-start.8
  22.9 0.0 collective-permute-start.6
  22.9 2.7 %collective-permute-start.7 = (f32[15,128,128]{2,1,0:T(8,128)}, f32[15,128,128]{2,1,0:T(8,128)}, u32[]{:S(2)}, u32[]{:S(2)}) collective-permute-start(f32[15,128,128]{2,1,0:T(8,128)} %get-tuple-element.71), channel_id=1, source_target_pairs={{0,14},{2,0},{4,2},{6,4},{8,6},{10,8},{12,10},{14,12},{1,15},{3,1}... | collective-permute-start | bytes 2949128 | tf_op jit(solution)/shard_map/ppermute | solution.py:51
  25.6 0.0 copy-done.4
  25.6 0.1 copy.17
  25.7 0.0 copy-done.2
  25.7 0.0 copy-done.3
  25.7 0.1 select_add_fusion
  25.8 7.4 %all_gather.3 = s32[10,4,10]{0,1,2:T(4,128)S(1)} all-gather(s32[10,4,5]{0,1,2:T(4,128)S(1)} %select_add_fusion), channel_id=1, replica_groups=mesh['dom'=16,'col'=8,'rep'=2] {'rep'}, dimensions={2}, use_global_device_ids=true | all-gather | bytes 2400 | tf_op jit(solution)/shard_map/all_gather | solution.py:434
  33.2 0.1 copy.18.known
  33.3 9.5 %lists.1 = (s32[632]{0:T(1024)S(1)}, s32[632]{0:T(1024)S(1)}, s32[332]{0:T(512)S(1)}, s32[632]{0:T(1024)S(1)}, s32[61]{0:T(128)S(1)}, /*index=5*/s32[8]{0:T(128)S(1)}) custom-call(s32[10,4,10]{2,1,0:T(4,128)S(1)} %copy.18.known, s32[7,4,10]{2,1,0:T(4,128)S(1)} %broadcast_select_fusion.stored), custom_call_target="tpu_custom_call" | custom-call | flops 1000 | bytes 1000 | tf_op jit(solution)/shard_map/lists/pallas_call | solution.py:172
  42.8 0.0 collective-permute-done.4.refs_1_
  42.8 2.7 %first.1 = (bf16[281,128,256]{2,1,0:T(8,128)(2,1)S(1)}, f32[61,128,128]{2,1,0:T(8,128)S(1)}) custom-call(f32[30,128,128]{2,1,0:T(8,128)S(1)} %bitcast.5, f32[30,128,128]{2,1,0:T(8,128)} %collective-permute-done.4.refs_1_), custom_call_target="tpu_custom_call" | custom-call | flops 1000 | bytes 1000 | tf_op jit(solution)/shard_map/first/pallas_call | solution.py:397
  45.5 0.0 collective-permute-done.5.refs_0_.refs_2_
  45.5 0.5 pack.6
  46.0 0.0 collective-permute-done.6.refs_0_
  46.0 0.0 collective-permute-done.7.refs_1_
  46.0 1.3 %pack.7 = f32[20,128,128]{2,1,0:T(8,128)S(1)} custom-call(f32[15,128,128]{2,1,0:T(8,128)} %collective-permute-done.6.refs_0_, f32[15,128,128]{2,1,0:T(8,128)} %collective-permute-done.7.refs_1_), custom_call_target="tpu_custom_call" | custom-call | flops 1000 | bytes 1000 | tf_op jit(solution)/shard_map/pack/pallas_call | solution.py:361
  47.3 1.1 %collective-permute-done.8.refs_3_ = f32[20,128,128]{2,1,0:T(8,128)} collective-permute-done((f32[20,128,128]{2,1,0:T(8,128)}, f32[20,128,128]{2,1,0:T(8,128)}, u32[]{:S(2)}, u32[]{:S(2)}) %collective-permute-start.8) | collective-permute-done | bytes 1310752 | tf_op jit(solution)/shard_map/ppermute | solution.py:57
  48.4 1.6 %collective-permute-start.9 = (f32[15,128,128]{2,1,0:T(8,128)}, f32[15,128,128]{2,1,0:T(8,128)S(1)}, u32[]{:S(2)}, u32[]{:S(2)}) collective-permute-start(f32[15,128,128]{2,1,0:T(8,128)} %collective-permute-done.6.refs_0_), channel_id=1, source_target_pairs={{0,1},{1,0},{2,3},{3,2},{4,5},{5,4},{6,7},{7,6},{8,9},{9,8},{10,11... | collective-permute-start | bytes 2949128 | tf_op jit(solution)/shard_map/ppermute | solution.py:51
  50.0 0.1 collective-permute-start.10
  50.1 0.4 collective-permute-start.12
  50.5 0.1 collective-permute-start.11
  50.6 0.0 collective-permute-start.15
  50.6 1.8 %collective-permute-done.9.refs_0_ = f32[15,128,128]{2,1,0:T(8,128)S(1)} collective-permute-done((f32[15,128,128]{2,1,0:T(8,128)}, f32[15,128,128]{2,1,0:T(8,128)S(1)}, u32[]{:S(2)}, u32[]{:S(2)}) %collective-permute-start.9) | collective-permute-done | bytes 983072 | tf_op jit(solution)/shard_map/ppermute | solution.py:51
  52.4 0.0 collective-permute-start.13
  52.4 2.8 %collective-permute-done.10.refs_1_ = f32[15,128,128]{2,1,0:T(8,128)S(1)} collective-permute-done((f32[15,128,128]{2,1,0:T(8,128)}, f32[15,128,128]{2,1,0:T(8,128)S(1)}, u32[]{:S(2)}, u32[]{:S(2)}) %collective-permute-start.10) | collective-permute-done | bytes 983072 | tf_op jit(solution)/shard_map/ppermute | solution.py:51
  55.2 2.7 %collective-permute-start.14 = (f32[10,128,128]{2,1,0:T(8,128)S(1)}, f32[10,128,128]{2,1,0:T(8,128)S(1)}, u32[]{:S(2)}, u32[]{:S(2)}) collective-permute-start(f32[10,128,128]{2,1,0:T(8,128)S(1)} %get-tuple-element.74), channel_id=1, source_target_pairs={{0,14},{2,0},{4,2},{6,4},{8,6},{10,8},{12,10},{14,12},{1,15},{3,1}... | collective-permute-start | bytes 1966088 | tf_op jit(solution)/shard_map/ppermute | solution.py:51
  57.9 3.1 %rows.1._ = bf16[281,128,256]{2,1,0:T(8,128)(2,1)S(1)} custom-call(bf16[281,128,256]{2,1,0:T(8,128)(2,1)S(1)} %get-tuple-element.69._, f32[15,128,128]{2,1,0:T(8,128)} %collective-permute-done.6.refs_0_, f32[15,128,128]{2,1,0:T(8,128)} %collective-permute-done.7.refs_1_, ...), custom_call_target="tpu_custom_call", output_to_operand_aliasing={{}: (0, {})} | custom-call | flops 1000 | bytes 1000 | tf_op jit(solution)/shard_map/rows/pallas_call | solution.py:397
  61.0 0.0 collective-permute-done.12.refs_3_
  61.0 0.0 collective-permute-done.11.refs_2_
  61.0 10.8 %early.1 = (bf16[281,128,256]{2,1,0:T(8,128)(2,1)S(1)}, f32[61,128,128]{2,1,0:T(8,128)S(1)}, bf16[121,128,256]{2,1,0:T(8,128)(2,1)S(1)}, f32[31,128,128]{2,1,0:T(8,128)S(1)}) custom-call(s32[632]{0:T(1024)S(1)} %get-tuple-element.63.codes, s32[332]{0:T(512)S(1)} %get-tuple-element.64.cube_codes, ...), custom_call_target="tpu_custom_call", output_to_operand_aliasing={{0}: (3, {}), {1}: (4, {})} | custom-call | flops 1000 | bytes 1000 | tf_op jit(solution)/shard_map/early/pallas_call | solution.py:397
  71.8 0.0 collective-permute-done.13.refs_0_
  71.9 0.0 collective-permute-done.14.refs_1_
  71.9 0.0 collective-permute-done.15.refs_2_
  71.9 2.3 %collective-permute-start.18 = (f32[20,128,128]{2,1,0:T(8,128)S(1)}, f32[20,128,128]{2,1,0:T(8,128)S(1)}, u32[]{:S(2)}, u32[]{:S(2)}) collective-permute-start(f32[20,128,128]{2,1,0:T(8,128)S(1)} %collective-permute-done.15.refs_2_), channel_id=1, source_target_pairs={{0,1},{1,0},{2,3},{3,2},{4,5},{5,4},{6,7},{7,6},{8,9},{9,8},{10,11... | collective-permute-start | bytes 3932168 | tf_op jit(solution)/shard_map/ppermute | solution.py:51
  74.2 0.1 collective-permute-start.16
  74.3 0.4 collective-permute-start.17
  74.7 1.1 %corner.1.blocks_in = bf16[281,128,256]{2,1,0:T(8,128)(2,1)S(1)} custom-call(bf16[281,128,256]{2,1,0:T(8,128)(2,1)S(1)} %get-tuple-element.87._, f32[10,128,128]{2,1,0:T(8,128)S(1)} %collective-permute-done.13.refs_0_, f32[10,128,128]{2,1,0:T(8,128)S(1)} %collective-permute-done.14.refs_1_, ...), custom_call_target="tpu_custom_call", output_to_operand_aliasing={{}: (0, {})} | custom-call | flops 1000 | bytes 1000 | tf_op jit(solution)/shard_map/corner/pallas_call | solution.py:397
  75.8 2.0 %collective-permute-done.16.refs_0_ = f32[10,128,128]{2,1,0:T(8,128)S(1)} collective-permute-done((f32[10,128,128]{2,1,0:T(8,128)S(1)}, f32[10,128,128]{2,1,0:T(8,128)S(1)}, u32[]{:S(2)}, u32[]{:S(2)}) %collective-permute-start.16) | collective-permute-done | bytes 655392 | tf_op jit(solution)/shard_map/ppermute | solution.py:51
  77.8 0.9 %collective-permute-done.17.refs_1_ = f32[10,128,128]{2,1,0:T(8,128)S(1)} collective-permute-done((f32[10,128,128]{2,1,0:T(8,128)S(1)}, f32[10,128,128]{2,1,0:T(8,128)S(1)}, u32[]{:S(2)}, u32[]{:S(2)}) %collective-permute-start.17) | collective-permute-done | bytes 655392 | tf_op jit(solution)/shard_map/ppermute | solution.py:51
  78.7 0.0 collective-permute-done.18.refs_2_
  78.7 5.4 %late.1 = (f32[30,128,128]{2,1,0:T(8,128)}, bf16[281,128,256]{2,1,0:T(8,128)(2,1)S(1)}, f32[61,128,128]{2,1,0:T(8,128)S(1)}, bf16[121,128,256]{2,1,0:T(8,128)(2,1)S(1)}, f32[31,128,128]{2,1,0:T(8,128)S(1)}) custom-call(s32[632]{0:T(1024)S(1)} %get-tuple-element.58.codes, ...), custom_call_target="tpu_custom_call", output_to_operand_aliasing={{1}: (4, {}), {2}: (5, {}), {3}: (6, {}), {4}: (7, {})} | custom-call | flops 1000 | bytes 1000 | tf_op jit(solution)/shard_map/late/pallas_call | solution.py:397
  (5 shorter events, 0.0 us)
Async XLA Ops:
  0.0 25.7 %copy-start.2 = (s32[7,4,10]{2,1,0:T(4,128)S(1)}, s32[7,4,10]{2,1,0:T(4,128)}, u32[]{:S(2)}) copy-start(s32[7,4,10]{2,1,0:T(4,128)} %constant.13.clone) | copy-start | bytes 3364
  0.0 25.7 %copy-start.3 = (s32[7,4,10]{2,1,0:T(4,128)S(1)}, s32[7,4,10]{2,1,0:T(4,128)}, u32[]{:S(2)}) copy-start(s32[7,4,10]{2,1,0:T(4,128)} %constant.12.clone) | copy-start | bytes 3364
  0.0 42.8 %collective-permute-start.4 = (f32[30,128,128]{2,1,0:T(8,128)}, f32[30,128,128]{2,1,0:T(8,128)}, u32[]{:S(2)}, u32[]{:S(2)}) collective-permute-start(f32[30,128,128]{2,1,0:T(8,128)} %bitcast.2), channel_id=1, source_target_pairs={{0,1},{1,0},{2,3},{3,2},{4,5},{5,4},{6,7},{7,6},{8,9},{9,8},{10,11... | collective-permute-start | bytes 5898248 | tf_op jit(solution)/shard_map/ppermute | solution.py:51
  4.1 9.0 %collective-permute-start = (s32[2,2,5]{0,1,2:T(2,128)S(1)}, s32[2,2,5]{0,1,2:T(2,128)S(1)}, u32[]{:S(2)}, u32[]{:S(2)}) collective-permute-start(s32[2,2,5]{0,1,2:T(2,128)S(1)} %copy.14), channel_id=1, source_target_pairs={{0,16},{16,32},{32,48},{48,64},{64,80},{80,96},{96,112},{112,128},... | collective-permute-start | bytes 248 | tf_op jit(solution)/shard_map/ppermute | solution.py:51
  4.2 8.9 %collective-permute-start.1 = (s32[2,2,5]{0,1,2:T(2,128)S(1)}, s32[2,2,5]{0,1,2:T(2,128)S(1)}, u32[]{:S(2)}, u32[]{:S(2)}) collective-permute-start(s32[2,2,5]{0,1,2:T(2,128)S(1)} %copy.15), channel_id=1, source_target_pairs={{0,240},{16,0},{32,16},{48,32},{64,48},{80,64},{96,80},{112,96},{1... | collective-permute-start | bytes 248 | tf_op jit(solution)/shard_map/ppermute | solution.py:51
  9.0 1.5 %copy-start = (f32[3,2,5,128,128]{4,3,2,1,0:T(8,128)S(1)}, f32[3,2,5,128,128]{4,3,2,1,0:T(8,128)}, u32[]{:S(2)}) copy-start(f32[3,2,5,128,128]{4,3,2,1,0:T(8,128)} %param.5) | copy-start | bytes 5898244
  10.5 8.4 %copy-start.1 = (f32[3,2,5,128,128]{4,3,2,1,0:T(8,128)S(1)}, f32[3,2,5,128,128]{4,3,2,1,0:T(8,128)}, u32[]{:S(2)}) copy-start(f32[3,2,5,128,128]{4,3,2,1,0:T(8,128)} %param.5) | copy-start | bytes 5898244
  10.5 15.0 %copy-start.4 = (s32[3,2,5]{2,1,0:T(2,128)S(1)}, s32[3,2,5]{2,1,0:T(2,128)}, u32[]{:S(2)}) copy-start(s32[3,2,5]{2,1,0:T(2,128)} %param.7) | copy-start | bytes 364
  13.1 32.4 %collective-permute-start.5 = (f32[20,128,128]{2,1,0:T(8,128)}, f32[20,128,128]{2,1,0:T(8,128)S(1)}, u32[]{:S(2)}, u32[]{:S(2)}) collective-permute-start(f32[20,128,128]{2,1,0:T(8,128)} %get-tuple-element.68), channel_id=1, source_target_pairs={{0,16},{1,241},{16,32},{17,1},{32,48},{33,17},{48,64},{49,33},{64,... | collective-permute-start | bytes 3932168 | tf_op jit(solution)/shard_map/ppermute | solution.py:57
  14.9 6.1 %collective-permute-start.3 = (s32[7,1,5]{0,1,2:T(1,128)S(1)}, s32[7,1,5]{0,1,2:T(1,128)S(1)}, u32[]{:S(2)}, u32[]{:S(2)}) collective-permute-start(s32[7,1,5]{0,1,2:T(1,128)S(1)} %get-tuple-element.95), channel_id=1, source_target_pairs={{0,14},{2,0},{4,2},{6,4},{8,6},{10,8},{12,10},{14,12},{1,15},{3,1}... | collective-permute-start | bytes 428 | tf_op jit(solution)/shard_map/ppermute | solution.py:51
  18.9 3.9 %collective-permute-start.2 = (s32[7,1,5]{0,1,2:T(1,128)S(1)}, s32[7,1,5]{0,1,2:T(1,128)S(1)}, u32[]{:S(2)}, u32[]{:S(2)}) collective-permute-start(s32[7,1,5]{0,1,2:T(1,128)S(1)} %get-tuple-element.96), channel_id=1, source_target_pairs={{0,2},{2,4},{4,6},{6,8},{8,10},{10,12},{12,14},{14,0},{1,3},{3,5},... | collective-permute-start | bytes 428 | tf_op jit(solution)/shard_map/ppermute | solution.py:51
  22.9 25.5 %collective-permute-start.8 = (f32[20,128,128]{2,1,0:T(8,128)}, f32[20,128,128]{2,1,0:T(8,128)}, u32[]{:S(2)}, u32[]{:S(2)}) collective-permute-start(f32[20,128,128]{2,1,0:T(8,128)} %get-tuple-element.77), channel_id=1, source_target_pairs={{0,240},{1,17},{16,0},{17,33},{32,16},{33,49},{48,32},{49,65},{64,... | collective-permute-start | bytes 3932168 | tf_op jit(solution)/shard_map/ppermute | solution.py:57
  22.9 23.1 %collective-permute-start.6 = (f32[15,128,128]{2,1,0:T(8,128)}, f32[15,128,128]{2,1,0:T(8,128)}, u32[]{:S(2)}, u32[]{:S(2)}) collective-permute-start(f32[15,128,128]{2,1,0:T(8,128)} %get-tuple-element.70), channel_id=1, source_target_pairs={{0,2},{2,4},{4,6},{6,8},{8,10},{10,12},{12,14},{14,0},{1,3},{3,5},... | collective-permute-start | bytes 2949128 | tf_op jit(solution)/shard_map/ppermute | solution.py:51
  22.9 23.1 %collective-permute-start.7 = (f32[15,128,128]{2,1,0:T(8,128)}, f32[15,128,128]{2,1,0:T(8,128)}, u32[]{:S(2)}, u32[]{:S(2)}) collective-permute-start(f32[15,128,128]{2,1,0:T(8,128)} %get-tuple-element.71), channel_id=1, source_target_pairs={{0,14},{2,0},{4,2},{6,4},{8,6},{10,8},{12,10},{14,12},{1,15},{3,1}... | collective-permute-start | bytes 2949128 | tf_op jit(solution)/shard_map/ppermute | solution.py:51
  48.4 4.0 %collective-permute-start.9 = (f32[15,128,128]{2,1,0:T(8,128)}, f32[15,128,128]{2,1,0:T(8,128)S(1)}, u32[]{:S(2)}, u32[]{:S(2)}) collective-permute-start(f32[15,128,128]{2,1,0:T(8,128)} %collective-permute-done.6.refs_0_), channel_id=1, source_target_pairs={{0,1},{1,0},{2,3},{3,2},{4,5},{5,4},{6,7},{7,6},{8,9},{9,8},{10,11... | collective-permute-start | bytes 2949128 | tf_op jit(solution)/shard_map/ppermute | solution.py:51
  50.0 5.2 %collective-permute-start.10 = (f32[15,128,128]{2,1,0:T(8,128)}, f32[15,128,128]{2,1,0:T(8,128)S(1)}, u32[]{:S(2)}, u32[]{:S(2)}) collective-permute-start(f32[15,128,128]{2,1,0:T(8,128)} %collective-permute-done.7.refs_1_), channel_id=1, source_target_pairs={{0,1},{1,0},{2,3},{3,2},{4,5},{5,4},{6,7},{7,6},{8,9},{9,8},{10,11... | collective-permute-start | bytes 2949128 | tf_op jit(solution)/shard_map/ppermute | solution.py:51
  50.1 10.9 %collective-permute-start.12 = (f32[20,128,128]{2,1,0:T(8,128)}, f32[20,128,128]{2,1,0:T(8,128)S(1)}, u32[]{:S(2)}, u32[]{:S(2)}) collective-permute-start(f32[20,128,128]{2,1,0:T(8,128)} %collective-permute-done.8.refs_3_), channel_id=1, source_target_pairs={{0,1},{1,0},{2,3},{3,2},{4,5},{5,4},{6,7},{7,6},{8,9},{9,8},{10,11... | collective-permute-start | bytes 3932168 | tf_op jit(solution)/shard_map/ppermute | solution.py:51
  50.5 10.5 %collective-permute-start.11 = (f32[20,128,128]{2,1,0:T(8,128)S(1)}, f32[20,128,128]{2,1,0:T(8,128)S(1)}, u32[]{:S(2)}, u32[]{:S(2)}) collective-permute-start(f32[20,128,128]{2,1,0:T(8,128)S(1)} %collective-permute-done.5.refs_0_.refs_2_), channel_id=1, source_target_pairs={{0,1},{1,0},{2,3},{3,2},{4,5},{5,4},{6,7},{7,6},{8,9},{9,8},{10,11... | collective-permute-start | bytes 3932168 | tf_op jit(solution)/shard_map/ppermute | solution.py:51
  50.6 21.3 %collective-permute-start.15 = (f32[20,128,128]{2,1,0:T(8,128)S(1)}, f32[20,128,128]{2,1,0:T(8,128)S(1)}, u32[]{:S(2)}, u32[]{:S(2)}) collective-permute-start(f32[20,128,128]{2,1,0:T(8,128)S(1)} %pack.7), channel_id=1, source_target_pairs={{0,240},{1,17},{16,0},{17,33},{32,16},{33,49},{48,32},{49,65},{64,... | collective-permute-start | bytes 3932168 | tf_op jit(solution)/shard_map/ppermute | solution.py:57
  52.4 19.5 %collective-permute-start.13 = (f32[10,128,128]{2,1,0:T(8,128)S(1)}, f32[10,128,128]{2,1,0:T(8,128)S(1)}, u32[]{:S(2)}, u32[]{:S(2)}) collective-permute-start(f32[10,128,128]{2,1,0:T(8,128)S(1)} %get-tuple-element.73), channel_id=1, source_target_pairs={{0,2},{2,4},{4,6},{6,8},{8,10},{10,12},{12,14},{14,0},{1,3},{3,5},... | collective-permute-start | bytes 1966088 | tf_op jit(solution)/shard_map/ppermute | solution.py:51
  55.2 16.7 %collective-permute-start.14 = (f32[10,128,128]{2,1,0:T(8,128)S(1)}, f32[10,128,128]{2,1,0:T(8,128)S(1)}, u32[]{:S(2)}, u32[]{:S(2)}) collective-permute-start(f32[10,128,128]{2,1,0:T(8,128)S(1)} %get-tuple-element.74), channel_id=1, source_target_pairs={{0,14},{2,0},{4,2},{6,4},{8,6},{10,8},{12,10},{14,12},{1,15},{3,1}... | collective-permute-start | bytes 1966088 | tf_op jit(solution)/shard_map/ppermute | solution.py:51
  71.9 6.9 %collective-permute-start.18 = (f32[20,128,128]{2,1,0:T(8,128)S(1)}, f32[20,128,128]{2,1,0:T(8,128)S(1)}, u32[]{:S(2)}, u32[]{:S(2)}) collective-permute-start(f32[20,128,128]{2,1,0:T(8,128)S(1)} %collective-permute-done.15.refs_2_), channel_id=1, source_target_pairs={{0,1},{1,0},{2,3},{3,2},{4,5},{5,4},{6,7},{7,6},{8,9},{9,8},{10,11... | collective-permute-start | bytes 3932168 | tf_op jit(solution)/shard_map/ppermute | solution.py:51
  74.2 3.6 %collective-permute-start.16 = (f32[10,128,128]{2,1,0:T(8,128)S(1)}, f32[10,128,128]{2,1,0:T(8,128)S(1)}, u32[]{:S(2)}, u32[]{:S(2)}) collective-permute-start(f32[10,128,128]{2,1,0:T(8,128)S(1)} %collective-permute-done.13.refs_0_), channel_id=1, source_target_pairs={{0,1},{1,0},{2,3},{3,2},{4,5},{5,4},{6,7},{7,6},{8,9},{9,8},{10,11... | collective-permute-start | bytes 1966088 | tf_op jit(solution)/shard_map/ppermute | solution.py:51
  74.3 4.4 %collective-permute-start.17 = (f32[10,128,128]{2,1,0:T(8,128)S(1)}, f32[10,128,128]{2,1,0:T(8,128)S(1)}, u32[]{:S(2)}, u32[]{:S(2)}) collective-permute-start(f32[10,128,128]{2,1,0:T(8,128)S(1)} %collective-permute-done.14.refs_1_), channel_id=1, source_target_pairs={{0,1},{1,0},{2,3},{3,2},{4,5},{5,4},{6,7},{7,6},{8,9},{9,8},{10,11... | collective-permute-start | bytes 1966088 | tf_op jit(solution)/shard_map/ppermute | solution.py:51

commit v3 on v2

--- a/solution.py
+++ b/solution.py
@@ -204,16 +204,16 @@
     lax.fori_loop(0, count, step, 0, unroll=2)
 
 
-def run_list(codes, count, left, right, total, unroll=UNROLL):
+def run_list(codes, count, left, right, total):
     def step(at, _):
-        for u in range(unroll):
-            code = codes[at * unroll + u]
+        for u in range(UNROLL):
+            code = codes[at * UNROLL + u]
             b = right[(code >> 10) & 1023]
             out = jnp.dot(left[code & 1023], jnp.concatenate([b, b], axis=0), preferred_element_type=jnp.float32)
             total[code >> 20] += out[:, :128] + out[:, 128:]
         return 0
 
-    lax.fori_loop(0, (count + unroll - 1) // unroll, step, 0)
+    lax.fori_loop(0, (count + UNROLL - 1) // UNROLL, step, 0)
 
 
 def zero_blocks(ref, count):
@@ -298,7 +298,7 @@
 def late_kernel(codes, tail_codes, touched, counts, blocks_in, square_in, halves_in, cube_in, *refs):
     pieces, (out, blocks, square, halves, cube, stage, sems) = refs[:-7], refs[-7:]
     load_and_split(pieces, stage, sems, blocks, EARLY + LATE)
-    run_list(codes, counts[1], blocks, blocks, square, 8)
+    run_list(codes, counts[1], blocks, blocks, square)
 
     def resplit(n, _):
         o = touched[n]
@@ -308,7 +308,7 @@
         return 0
 
     lax.fori_loop(0, counts[6], resplit, 0)
-    run_list(tail_codes, counts[3], halves, blocks, cube, 16)
+    run_list(tail_codes, counts[3], halves, blocks, cube)
     base = counts[7]
     copies = []
     for i in range(CELLS):
@@ -418,12 +418,12 @@
 def body(density, pattern, filt):
     blocks = flat(density)
     row = COLS * HALF
-    above, below = shift(pattern[1:], "dom", 1), shift(pattern[:2], "dom", -1)
+    above, below = shift(pattern, "dom", 1), shift(pattern, "dom", -1)
     own_other = shift(blocks, "rep", 1)
     one, two = pack([blocks], [[(0, (row, 0), 2 * row)], [(0, (0, row), 2 * row)]], far=True)
     above, below, one = lax.optimization_barrier((above, below, one))
     one = cross(one, 1)
-    near = jnp.concatenate([above, pattern, below], axis=0)
+    near = jnp.concatenate([above[ROWS - 2:], pattern, below[:2]], axis=0)
     before, after = shift(near[:, 1:], "col", 1), shift(near[:, :1], "col", -1)
     edge_r, edge_l = pack([blocks], [[(0, r * row + q, HALF) for r in range(ROWS)] for q in (HALF, 0)])
     before, after, two, edge_r, edge_l = lax.optimization_barrier((before, after, two, edge_r, edge_l))

time: 83.7 us -> 85.7 us (1.024)
  starting transfers between devices: 24.1 us -> 26.6 us
  Pallas kernels: 38.2 us -> 36.9 us
  waiting for transfers between devices: 10.5 us -> 11.8 us
  local copies, waits for them, and re-layouts: 3.51 us -> 2.62 us
    ppermute x16, waiting for transfers between devices: 9.45 us -> 11.8 us  [shift(): lax.ppermute(array, axis, [(i, (i + step) % peers) for i in range(peers)])]
    ppermute x16, starting transfers between devices: 22.5 us -> 24.1 us  [shift(): lax.ppermute(array, axis, [(i, (i + step) % peers) for i in range(peers)])]
    pallas_call x5, Pallas kernels: 23.2 us -> 21.9 us  [call(): pl.pallas_call(kernel, out_shape=outs, in_specs=[smem()] * len(lists) + [...]
    ppermute x3, waiting for transfers between devices: 1.07 us -> 0.01 us  [cross(): return lax.ppermute(array, ('dom', 'rep'), pairs)]
    slice x3 -> x1, local copies, waits for them, and re-layouts: 0.96 us -> 0.07 us  [body(): near = jnp.concatenate([above[ROWS - 2:], pattern, below[:2]], axis=0)]
  transfers between devices with their start and end apart: 19 -> 19, of which waited for: 6 -> 6; matrix products, arithmetic and copies ran while one was open for 3% -> 1% of each run, Pallas kernels for 39% -> 37%
where the time goes in v3:
time: 85.7 us; the launch traced here: 86.1 us
  Pallas kernels  36.9 us (43%)
  starting transfers between devices  26.6 us (31%)
  waiting for transfers between devices  11.8 us (14%)
  blocking collectives  7.57 us (9%)
  local copies, waits for them, and re-layouts  2.62 us (3%)
    ppermute x16, starting transfers between devices, shift(): lax.ppermute(array, axis, [(i, (i + step) % peers) for i in range(peers)])  24.1 us
    pallas_call x5, Pallas kernels, call(): pl.pallas_call(kernel, out_shape=outs, in_specs=[smem()] * len(lists) + [...  21.9 us
    ppermute x16, waiting for transfers between devices, shift(): lax.ppermute(array, axis, [(i, (i + step) % peers) for i in range(peers)])  11.8 us
    pallas_call x1, Pallas kernels, make_lists(): pl.pallas_call(functools.partial(list_kernel, grid), out_shape=[jax.Shape...  9.48 us
    all_gather x1, blocking collectives, body(): lax.all_gather(jnp.concatenate([rim, own_filt], axis=0), 'rep', axis=2, t...  7.57 us
    pallas_call x4, Pallas kernels, pack(): pl.pallas_call(kernel, out_shape=[out((n, 128, 128), jnp.float32) for n i...  5.58 us
    unnamed x12, local copies, waits for them, and re-layouts  2.43 us
    ppermute x3, starting transfers between devices, cross(): return lax.ppermute(array, ('dom', 'rep'), pairs)  2.42 us
  transfers between devices with their start and end apart: 19, of which 6 were waited for; matrix products, arithmetic and copies ran while one was open for 1% of the time, Pallas kernels for 37%

profile of v3, /device:TPU:1, one launch (start us, length us, event | category | flops | bytes accessed | tf_op | source)
XLA Modules:
  0.0 86.1 jit_solution(3052800307111296050)
XLA Ops:
  0.0 0.0 copy-start.4
  0.0 3.2 %collective-permute-start.4 = (f32[30,128,128]{2,1,0:T(8,128)}, f32[30,128,128]{2,1,0:T(8,128)}, u32[]{:S(2)}, u32[]{:S(2)}) collective-permute-start(f32[30,128,128]{2,1,0:T(8,128)} %bitcast.3), channel_id=1, source_target_pairs={{0,1},{1,0},{2,3},{3,2},{4,5},{5,4},{6,7},{7,6},{8,9},{9,8},{10,11... | collective-permute-start | bytes 5898248 | tf_op jit(solution)/shard_map/ppermute | solution.py:51
  3.2 0.8 copy.14
  4.0 3.2 %collective-permute-start.1 = (s32[3,2,5]{0,1,2:T(2,128)S(1)}, s32[3,2,5]{0,1,2:T(2,128)S(1)}, u32[]{:S(2)}, u32[]{:S(2)}) collective-permute-start(s32[3,2,5]{0,1,2:T(2,128)S(1)} %copy.14), channel_id=1, source_target_pairs={{0,240},{16,0},{32,16},{48,32},{64,48},{80,64},{96,80},{112,96},{1... | collective-permute-start | bytes 368 | tf_op jit(solution)/shard_map/ppermute | solution.py:51
  7.2 0.0 collective-permute-start
  7.2 0.0 copy-start
  7.2 1.5 %copy-done = f32[3,2,5,128,128]{4,3,2,1,0:T(8,128)S(1)} copy-done((f32[3,2,5,128,128]{4,3,2,1,0:T(8,128)S(1)}, f32[3,2,5,128,128]{4,3,2,1,0:T(8,128)}, u32[]{:S(2)}) %copy-start) | copy-done | bytes 1966104
  8.8 0.0 copy-start.1
  8.8 0.0 copy-start.2
  8.8 1.8 %pack.4 = (f32[20,128,128]{2,1,0:T(8,128)}, f32[20,128,128]{2,1,0:T(8,128)}) custom-call(f32[30,128,128]{2,1,0:T(8,128)S(1)} %bitcast.4), custom_call_target="tpu_custom_call" | custom-call | flops 1000 | bytes 1000 | tf_op jit(solution)/shard_map/pack/pallas_call | solution.py:361
  10.6 0.0 collective-permute-done.1
  10.6 2.4 %collective-permute-done = s32[3,2,5]{0,1,2:T(2,128)S(1)} collective-permute-done((s32[3,2,5]{0,1,2:T(2,128)S(1)}, s32[3,2,5]{0,1,2:T(2,128)S(1)}, u32[]{:S(2)}, u32[]{:S(2)}) %collective-permute-start) | collective-permute-done | bytes 152 | tf_op jit(solution)/shard_map/ppermute | solution.py:51
  13.0 0.1 slice.12
  13.1 2.4 %collective-permute-start.5 = (f32[20,128,128]{2,1,0:T(8,128)}, f32[20,128,128]{2,1,0:T(8,128)S(1)}, u32[]{:S(2)}, u32[]{:S(2)}) collective-permute-start(f32[20,128,128]{2,1,0:T(8,128)} %get-tuple-element.68), channel_id=1, source_target_pairs={{0,16},{1,241},{16,32},{17,1},{32,48},{33,17},{48,64},{49,33},{64,... | collective-permute-start | bytes 3932168 | tf_op jit(solution)/shard_map/ppermute | solution.py:57
  15.5 0.1 pad_add_fusion
  15.6 5.7 %collective-permute-start.3 = (s32[7,1,5]{0,1,2:T(1,128)S(1)}, s32[7,1,5]{0,1,2:T(1,128)S(1)}, u32[]{:S(2)}, u32[]{:S(2)}) collective-permute-start(s32[7,1,5]{0,1,2:T(1,128)S(1)} %get-tuple-element.95), channel_id=1, source_target_pairs={{0,14},{2,0},{4,2},{6,4},{8,6},{10,8},{12,10},{14,12},{1,15},{3,1}... | collective-permute-start | bytes 428 | tf_op jit(solution)/shard_map/ppermute | solution.py:51
  21.2 0.0 collective-permute-start.2
  21.2 0.0 copy-done.1
  21.2 2.0 %pack.5 = (f32[15,128,128]{2,1,0:T(8,128)}, f32[15,128,128]{2,1,0:T(8,128)}) custom-call(f32[30,128,128]{2,1,0:T(8,128)S(1)} %bitcast.5), custom_call_target="tpu_custom_call" | custom-call | flops 1000 | bytes 1000 | tf_op jit(solution)/shard_map/pack/pallas_call | solution.py:361
  23.2 0.0 collective-permute-done.3
  23.3 1.9 %collective-permute-done.2 = s32[7,1,5]{0,1,2:T(1,128)S(1)} collective-permute-done((s32[7,1,5]{0,1,2:T(1,128)S(1)}, s32[7,1,5]{0,1,2:T(1,128)S(1)}, u32[]{:S(2)}, u32[]{:S(2)}) %collective-permute-start.2) | collective-permute-done | bytes 172 | tf_op jit(solution)/shard_map/ppermute | solution.py:51
  25.2 0.0 collective-permute-start.8
  25.2 0.0 collective-permute-start.6
  25.2 2.7 %collective-permute-start.7 = (f32[15,128,128]{2,1,0:T(8,128)}, f32[15,128,128]{2,1,0:T(8,128)}, u32[]{:S(2)}, u32[]{:S(2)}) collective-permute-start(f32[15,128,128]{2,1,0:T(8,128)} %get-tuple-element.71), channel_id=1, source_target_pairs={{0,14},{2,0},{4,2},{6,4},{8,6},{10,8},{12,10},{14,12},{1,15},{3,1}... | collective-permute-start | bytes 2949128 | tf_op jit(solution)/shard_map/ppermute | solution.py:51
  27.9 0.0 copy-done.4
  27.9 0.1 copy.17
  28.0 0.0 copy-done.2
  28.0 0.0 copy-done.3
  28.0 0.1 select_add_fusion
  28.1 7.6 %all_gather.3 = s32[10,4,10]{0,1,2:T(4,128)S(1)} all-gather(s32[10,4,5]{0,1,2:T(4,128)S(1)} %select_add_fusion), channel_id=1, replica_groups=mesh['dom'=16,'col'=8,'rep'=2] {'rep'}, dimensions={2}, use_global_device_ids=true | all-gather | bytes 2400 | tf_op jit(solution)/shard_map/all_gather | solution.py:434
  35.6 0.1 copy.18.known
  35.8 9.5 %lists.1 = (s32[632]{0:T(1024)S(1)}, s32[632]{0:T(1024)S(1)}, s32[332]{0:T(512)S(1)}, s32[632]{0:T(1024)S(1)}, s32[61]{0:T(128)S(1)}, /*index=5*/s32[8]{0:T(128)S(1)}) custom-call(s32[10,4,10]{2,1,0:T(4,128)S(1)} %copy.18.known, s32[7,4,10]{2,1,0:T(4,128)S(1)} %broadcast_select_fusion.stored), custom_call_target="tpu_custom_call" | custom-call | flops 1000 | bytes 1000 | tf_op jit(solution)/shard_map/lists/pallas_call | solution.py:172
  45.2 0.0 collective-permute-done.4.refs_1_
  45.3 2.7 %first.1 = (bf16[281,128,256]{2,1,0:T(8,128)(2,1)S(1)}, f32[61,128,128]{2,1,0:T(8,128)S(1)}) custom-call(f32[30,128,128]{2,1,0:T(8,128)S(1)} %bitcast.6, f32[30,128,128]{2,1,0:T(8,128)} %collective-permute-done.4.refs_1_), custom_call_target="tpu_custom_call" | custom-call | flops 1000 | bytes 1000 | tf_op jit(solution)/shard_map/first/pallas_call | solution.py:397
  48.0 0.0 collective-permute-done.5.refs_0_.refs_2_
  48.0 0.5 pack.6
  48.4 0.0 collective-permute-done.6.refs_0_
  48.4 0.0 collective-permute-done.7.refs_1_
  48.5 1.3 %pack.7 = f32[20,128,128]{2,1,0:T(8,128)S(1)} custom-call(f32[15,128,128]{2,1,0:T(8,128)} %collective-permute-done.6.refs_0_, f32[15,128,128]{2,1,0:T(8,128)} %collective-permute-done.7.refs_1_), custom_call_target="tpu_custom_call" | custom-call | flops 1000 | bytes 1000 | tf_op jit(solution)/shard_map/pack/pallas_call | solution.py:361
  49.8 0.0 collective-permute-done.8.refs_3_
  49.8 2.5 %collective-permute-start.9 = (f32[15,128,128]{2,1,0:T(8,128)}, f32[15,128,128]{2,1,0:T(8,128)S(1)}, u32[]{:S(2)}, u32[]{:S(2)}) collective-permute-start(f32[15,128,128]{2,1,0:T(8,128)} %collective-permute-done.6.refs_0_), channel_id=1, source_target_pairs={{0,1},{1,0},{2,3},{3,2},{4,5},{5,4},{6,7},{7,6},{8,9},{9,8},{10,11... | collective-permute-start | bytes 2949128 | tf_op jit(solution)/shard_map/ppermute | solution.py:51
  52.3 0.1 collective-permute-start.10
  52.4 0.4 collective-permute-start.12
  52.8 0.1 collective-permute-start.11
  52.9 0.0 collective-permute-start.15
  52.9 1.8 %collective-permute-done.9.refs_0_ = f32[15,128,128]{2,1,0:T(8,128)S(1)} collective-permute-done((f32[15,128,128]{2,1,0:T(8,128)}, f32[15,128,128]{2,1,0:T(8,128)S(1)}, u32[]{:S(2)}, u32[]{:S(2)}) %collective-permute-start.9) | collective-permute-done | bytes 983072 | tf_op jit(solution)/shard_map/ppermute | solution.py:51
  54.7 0.0 collective-permute-start.13
  54.7 2.8 %collective-permute-done.10.refs_1_ = f32[15,128,128]{2,1,0:T(8,128)S(1)} collective-permute-done((f32[15,128,128]{2,1,0:T(8,128)}, f32[15,128,128]{2,1,0:T(8,128)S(1)}, u32[]{:S(2)}, u32[]{:S(2)}) %collective-permute-start.10) | collective-permute-done | bytes 983072 | tf_op jit(solution)/shard_map/ppermute | solution.py:51
  57.5 2.8 %collective-permute-start.14 = (f32[10,128,128]{2,1,0:T(8,128)S(1)}, f32[10,128,128]{2,1,0:T(8,128)S(1)}, u32[]{:S(2)}, u32[]{:S(2)}) collective-permute-start(f32[10,128,128]{2,1,0:T(8,128)S(1)} %get-tuple-element.74), channel_id=1, source_target_pairs={{0,14},{2,0},{4,2},{6,4},{8,6},{10,8},{12,10},{14,12},{1,15},{3,1}... | collective-permute-start | bytes 1966088 | tf_op jit(solution)/shard_map/ppermute | solution.py:51
  60.3 3.1 %rows.1._ = bf16[281,128,256]{2,1,0:T(8,128)(2,1)S(1)} custom-call(bf16[281,128,256]{2,1,0:T(8,128)(2,1)S(1)} %get-tuple-element.69._, f32[15,128,128]{2,1,0:T(8,128)} %collective-permute-done.6.refs_0_, f32[15,128,128]{2,1,0:T(8,128)} %collective-permute-done.7.refs_1_, ...), custom_call_target="tpu_custom_call", output_to_operand_aliasing={{}: (0, {})} | custom-call | flops 1000 | bytes 1000 | tf_op jit(solution)/shard_map/rows/pallas_call | solution.py:397
  63.4 0.0 collective-permute-done.12.refs_3_
  63.4 0.0 collective-permute-done.11.refs_2_
  63.4 10.1 %early.1 = (bf16[281,128,256]{2,1,0:T(8,128)(2,1)S(1)}, f32[61,128,128]{2,1,0:T(8,128)S(1)}, bf16[121,128,256]{2,1,0:T(8,128)(2,1)S(1)}, f32[31,128,128]{2,1,0:T(8,128)S(1)}) custom-call(s32[632]{0:T(1024)S(1)} %get-tuple-element.63.codes, s32[332]{0:T(512)S(1)} %get-tuple-element.64.cube_codes, ...), custom_call_target="tpu_custom_call", output_to_operand_aliasing={{0}: (3, {}), {1}: (4, {})} | custom-call | flops 1000 | bytes 1000 | tf_op jit(solution)/shard_map/early/pallas_call | solution.py:397
  73.6 0.0 collective-permute-done.13.refs_0_
  73.6 0.0 collective-permute-done.14.refs_1_
  73.6 0.0 collective-permute-done.15.refs_2_
  73.6 2.9 %collective-permute-start.18 = (f32[20,128,128]{2,1,0:T(8,128)S(1)}, f32[20,128,128]{2,1,0:T(8,128)S(1)}, u32[]{:S(2)}, u32[]{:S(2)}) collective-permute-start(f32[20,128,128]{2,1,0:T(8,128)S(1)} %collective-permute-done.15.refs_2_), channel_id=1, source_target_pairs={{0,1},{1,0},{2,3},{3,2},{4,5},{5,4},{6,7},{7,6},{8,9},{9,8},{10,11... | collective-permute-start | bytes 3932168 | tf_op jit(solution)/shard_map/ppermute | solution.py:51
  76.5 0.1 collective-permute-start.16
  76.6 0.4 collective-permute-start.17
  77.0 1.1 %corner.1.blocks_in = bf16[281,128,256]{2,1,0:T(8,128)(2,1)S(1)} custom-call(bf16[281,128,256]{2,1,0:T(8,128)(2,1)S(1)} %get-tuple-element.87._, f32[10,128,128]{2,1,0:T(8,128)S(1)} %collective-permute-done.13.refs_0_, f32[10,128,128]{2,1,0:T(8,128)S(1)} %collective-permute-done.14.refs_1_, ...), custom_call_target="tpu_custom_call", output_to_operand_aliasing={{}: (0, {})} | custom-call | flops 1000 | bytes 1000 | tf_op jit(solution)/shard_map/corner/pallas_call | solution.py:397
  78.2 2.0 %collective-permute-done.16.refs_0_ = f32[10,128,128]{2,1,0:T(8,128)S(1)} collective-permute-done((f32[10,128,128]{2,1,0:T(8,128)S(1)}, f32[10,128,128]{2,1,0:T(8,128)S(1)}, u32[]{:S(2)}, u32[]{:S(2)}) %collective-permute-start.16) | collective-permute-done | bytes 655392 | tf_op jit(solution)/shard_map/ppermute | solution.py:51
  80.1 0.9 %collective-permute-done.17.refs_1_ = f32[10,128,128]{2,1,0:T(8,128)S(1)} collective-permute-done((f32[10,128,128]{2,1,0:T(8,128)S(1)}, f32[10,128,128]{2,1,0:T(8,128)S(1)}, u32[]{:S(2)}, u32[]{:S(2)}) %collective-permute-start.17) | collective-permute-done | bytes 655392 | tf_op jit(solution)/shard_map/ppermute | solution.py:51
  81.1 0.0 collective-permute-done.18.refs_2_
  81.1 4.8 %late.1 = (f32[30,128,128]{2,1,0:T(8,128)}, bf16[281,128,256]{2,1,0:T(8,128)(2,1)S(1)}, f32[61,128,128]{2,1,0:T(8,128)S(1)}, bf16[121,128,256]{2,1,0:T(8,128)(2,1)S(1)}, f32[31,128,128]{2,1,0:T(8,128)S(1)}) custom-call(s32[632]{0:T(1024)S(1)} %get-tuple-element.58.codes, ...), custom_call_target="tpu_custom_call", output_to_operand_aliasing={{1}: (4, {}), {2}: (5, {}), {3}: (6, {}), {4}: (7, {})} | custom-call | flops 1000 | bytes 1000 | tf_op jit(solution)/shard_map/late/pallas_call | solution.py:397
  (3 shorter events, 0.0 us)
Async XLA Ops:
  0.0 27.9 %copy-start.4 = (s32[3,2,5]{2,1,0:T(2,128)S(1)}, s32[3,2,5]{2,1,0:T(2,128)}, u32[]{:S(2)}) copy-start(s32[3,2,5]{2,1,0:T(2,128)} %param.7) | copy-start | bytes 364
  0.0 45.2 %collective-permute-start.4 = (f32[30,128,128]{2,1,0:T(8,128)}, f32[30,128,128]{2,1,0:T(8,128)}, u32[]{:S(2)}, u32[]{:S(2)}) collective-permute-start(f32[30,128,128]{2,1,0:T(8,128)} %bitcast.3), channel_id=1, source_target_pairs={{0,1},{1,0},{2,3},{3,2},{4,5},{5,4},{6,7},{7,6},{8,9},{9,8},{10,11... | collective-permute-start | bytes 5898248 | tf_op jit(solution)/shard_map/ppermute | solution.py:51
  4.0 6.6 %collective-permute-start.1 = (s32[3,2,5]{0,1,2:T(2,128)S(1)}, s32[3,2,5]{0,1,2:T(2,128)S(1)}, u32[]{:S(2)}, u32[]{:S(2)}) collective-permute-start(s32[3,2,5]{0,1,2:T(2,128)S(1)} %copy.14), channel_id=1, source_target_pairs={{0,240},{16,0},{32,16},{48,32},{64,48},{80,64},{96,80},{112,96},{1... | collective-permute-start | bytes 368 | tf_op jit(solution)/shard_map/ppermute | solution.py:51
  7.2 5.8 %collective-permute-start = (s32[3,2,5]{0,1,2:T(2,128)S(1)}, s32[3,2,5]{0,1,2:T(2,128)S(1)}, u32[]{:S(2)}, u32[]{:S(2)}) collective-permute-start(s32[3,2,5]{0,1,2:T(2,128)S(1)} %copy.14), channel_id=1, source_target_pairs={{0,16},{16,32},{32,48},{48,64},{64,80},{80,96},{96,112},{112,128},... | collective-permute-start | bytes 368 | tf_op jit(solution)/shard_map/ppermute | solution.py:51
  7.2 1.5 %copy-start = (f32[3,2,5,128,128]{4,3,2,1,0:T(8,128)S(1)}, f32[3,2,5,128,128]{4,3,2,1,0:T(8,128)}, u32[]{:S(2)}) copy-start(f32[3,2,5,128,128]{4,3,2,1,0:T(8,128)} %param.5) | copy-start | bytes 5898244
  8.8 12.5 %copy-start.1 = (f32[3,2,5,128,128]{4,3,2,1,0:T(8,128)S(1)}, f32[3,2,5,128,128]{4,3,2,1,0:T(8,128)}, u32[]{:S(2)}) copy-start(f32[3,2,5,128,128]{4,3,2,1,0:T(8,128)} %param.5) | copy-start | bytes 5898244
  8.8 19.2 %copy-start.2 = (s32[7,4,10]{2,1,0:T(4,128)S(1)}, s32[7,4,10]{2,1,0:T(4,128)}, u32[]{:S(2)}) copy-start(s32[7,4,10]{2,1,0:T(4,128)} %constant.13.clone) | copy-start | bytes 3364
  8.8 19.2 %copy-start.3 = (s32[7,4,10]{2,1,0:T(4,128)S(1)}, s32[7,4,10]{2,1,0:T(4,128)}, u32[]{:S(2)}) copy-start(s32[7,4,10]{2,1,0:T(4,128)} %constant.12.clone) | copy-start | bytes 3364
  13.1 34.9 %collective-permute-start.5 = (f32[20,128,128]{2,1,0:T(8,128)}, f32[20,128,128]{2,1,0:T(8,128)S(1)}, u32[]{:S(2)}, u32[]{:S(2)}) collective-permute-start(f32[20,128,128]{2,1,0:T(8,128)} %get-tuple-element.68), channel_id=1, source_target_pairs={{0,16},{1,241},{16,32},{17,1},{32,48},{33,17},{48,64},{49,33},{64,... | collective-permute-start | bytes 3932168 | tf_op jit(solution)/shard_map/ppermute | solution.py:57
  15.6 7.7 %collective-permute-start.3 = (s32[7,1,5]{0,1,2:T(1,128)S(1)}, s32[7,1,5]{0,1,2:T(1,128)S(1)}, u32[]{:S(2)}, u32[]{:S(2)}) collective-permute-start(s32[7,1,5]{0,1,2:T(1,128)S(1)} %get-tuple-element.95), channel_id=1, source_target_pairs={{0,14},{2,0},{4,2},{6,4},{8,6},{10,8},{12,10},{14,12},{1,15},{3,1}... | collective-permute-start | bytes 428 | tf_op jit(solution)/shard_map/ppermute | solution.py:51
  21.2 3.9 %collective-permute-start.2 = (s32[7,1,5]{0,1,2:T(1,128)S(1)}, s32[7,1,5]{0,1,2:T(1,128)S(1)}, u32[]{:S(2)}, u32[]{:S(2)}) collective-permute-start(s32[7,1,5]{0,1,2:T(1,128)S(1)} %get-tuple-element.96), channel_id=1, source_target_pairs={{0,2},{2,4},{4,6},{6,8},{8,10},{10,12},{12,14},{14,0},{1,3},{3,5},... | collective-permute-start | bytes 428 | tf_op jit(solution)/shard_map/ppermute | solution.py:51
  25.2 24.6 %collective-permute-start.8 = (f32[20,128,128]{2,1,0:T(8,128)}, f32[20,128,128]{2,1,0:T(8,128)}, u32[]{:S(2)}, u32[]{:S(2)}) collective-permute-start(f32[20,128,128]{2,1,0:T(8,128)} %get-tuple-element.77), channel_id=1, source_target_pairs={{0,240},{1,17},{16,0},{17,33},{32,16},{33,49},{48,32},{49,65},{64,... | collective-permute-start | bytes 3932168 | tf_op jit(solution)/shard_map/ppermute | solution.py:57
  25.2 23.3 %collective-permute-start.6 = (f32[15,128,128]{2,1,0:T(8,128)}, f32[15,128,128]{2,1,0:T(8,128)}, u32[]{:S(2)}, u32[]{:S(2)}) collective-permute-start(f32[15,128,128]{2,1,0:T(8,128)} %get-tuple-element.70), channel_id=1, source_target_pairs={{0,2},{2,4},{4,6},{6,8},{8,10},{10,12},{12,14},{14,0},{1,3},{3,5},... | collective-permute-start | bytes 2949128 | tf_op jit(solution)/shard_map/ppermute | solution.py:51
  25.2 23.3 %collective-permute-start.7 = (f32[15,128,128]{2,1,0:T(8,128)}, f32[15,128,128]{2,1,0:T(8,128)}, u32[]{:S(2)}, u32[]{:S(2)}) collective-permute-start(f32[15,128,128]{2,1,0:T(8,128)} %get-tuple-element.71), channel_id=1, source_target_pairs={{0,14},{2,0},{4,2},{6,4},{8,6},{10,8},{12,10},{14,12},{1,15},{3,1}... | collective-permute-start | bytes 2949128 | tf_op jit(solution)/shard_map/ppermute | solution.py:51
  49.8 4.9 %collective-permute-start.9 = (f32[15,128,128]{2,1,0:T(8,128)}, f32[15,128,128]{2,1,0:T(8,128)S(1)}, u32[]{:S(2)}, u32[]{:S(2)}) collective-permute-start(f32[15,128,128]{2,1,0:T(8,128)} %collective-permute-done.6.refs_0_), channel_id=1, source_target_pairs={{0,1},{1,0},{2,3},{3,2},{4,5},{5,4},{6,7},{7,6},{8,9},{9,8},{10,11... | collective-permute-start | bytes 2949128 | tf_op jit(solution)/shard_map/ppermute | solution.py:51
  52.3 5.2 %collective-permute-start.10 = (f32[15,128,128]{2,1,0:T(8,128)}, f32[15,128,128]{2,1,0:T(8,128)S(1)}, u32[]{:S(2)}, u32[]{:S(2)}) collective-permute-start(f32[15,128,128]{2,1,0:T(8,128)} %collective-permute-done.7.refs_1_), channel_id=1, source_target_pairs={{0,1},{1,0},{2,3},{3,2},{4,5},{5,4},{6,7},{7,6},{8,9},{9,8},{10,11... | collective-permute-start | bytes 2949128 | tf_op jit(solution)/shard_map/ppermute | solution.py:51
  52.4 11.0 %collective-permute-start.12 = (f32[20,128,128]{2,1,0:T(8,128)}, f32[20,128,128]{2,1,0:T(8,128)S(1)}, u32[]{:S(2)}, u32[]{:S(2)}) collective-permute-start(f32[20,128,128]{2,1,0:T(8,128)} %collective-permute-done.8.refs_3_), channel_id=1, source_target_pairs={{0,1},{1,0},{2,3},{3,2},{4,5},{5,4},{6,7},{7,6},{8,9},{9,8},{10,11... | collective-permute-start | bytes 3932168 | tf_op jit(solution)/shard_map/ppermute | solution.py:51
  52.8 10.6 %collective-permute-start.11 = (f32[20,128,128]{2,1,0:T(8,128)S(1)}, f32[20,128,128]{2,1,0:T(8,128)S(1)}, u32[]{:S(2)}, u32[]{:S(2)}) collective-permute-start(f32[20,128,128]{2,1,0:T(8,128)S(1)} %collective-permute-done.5.refs_0_.refs_2_), channel_id=1, source_target_pairs={{0,1},{1,0},{2,3},{3,2},{4,5},{5,4},{6,7},{7,6},{8,9},{9,8},{10,11... | collective-permute-start | bytes 3932168 | tf_op jit(solution)/shard_map/ppermute | solution.py:51
  52.9 20.7 %collective-permute-start.15 = (f32[20,128,128]{2,1,0:T(8,128)S(1)}, f32[20,128,128]{2,1,0:T(8,128)S(1)}, u32[]{:S(2)}, u32[]{:S(2)}) collective-permute-start(f32[20,128,128]{2,1,0:T(8,128)S(1)} %pack.7), channel_id=1, source_target_pairs={{0,240},{1,17},{16,0},{17,33},{32,16},{33,49},{48,32},{49,65},{64,... | collective-permute-start | bytes 3932168 | tf_op jit(solution)/shard_map/ppermute | solution.py:57
  54.7 18.9 %collective-permute-start.13 = (f32[10,128,128]{2,1,0:T(8,128)S(1)}, f32[10,128,128]{2,1,0:T(8,128)S(1)}, u32[]{:S(2)}, u32[]{:S(2)}) collective-permute-start(f32[10,128,128]{2,1,0:T(8,128)S(1)} %get-tuple-element.73), channel_id=1, source_target_pairs={{0,2},{2,4},{4,6},{6,8},{8,10},{10,12},{12,14},{14,0},{1,3},{3,5},... | collective-permute-start | bytes 1966088 | tf_op jit(solution)/shard_map/ppermute | solution.py:51
  57.5 16.1 %collective-permute-start.14 = (f32[10,128,128]{2,1,0:T(8,128)S(1)}, f32[10,128,128]{2,1,0:T(8,128)S(1)}, u32[]{:S(2)}, u32[]{:S(2)}) collective-permute-start(f32[10,128,128]{2,1,0:T(8,128)S(1)} %get-tuple-element.74), channel_id=1, source_target_pairs={{0,14},{2,0},{4,2},{6,4},{8,6},{10,8},{12,10},{14,12},{1,15},{3,1}... | collective-permute-start | bytes 1966088 | tf_op jit(solution)/shard_map/ppermute | solution.py:51
  73.6 7.5 %collective-permute-start.18 = (f32[20,128,128]{2,1,0:T(8,128)S(1)}, f32[20,128,128]{2,1,0:T(8,128)S(1)}, u32[]{:S(2)}, u32[]{:S(2)}) collective-permute-start(f32[20,128,128]{2,1,0:T(8,128)S(1)} %collective-permute-done.15.refs_2_), channel_id=1, source_target_pairs={{0,1},{1,0},{2,3},{3,2},{4,5},{5,4},{6,7},{7,6},{8,9},{9,8},{10,11... | collective-permute-start | bytes 3932168 | tf_op jit(solution)/shard_map/ppermute | solution.py:51
  76.5 3.6 %collective-permute-start.16 = (f32[10,128,128]{2,1,0:T(8,128)S(1)}, f32[10,128,128]{2,1,0:T(8,128)S(1)}, u32[]{:S(2)}, u32[]{:S(2)}) collective-permute-start(f32[10,128,128]{2,1,0:T(8,128)S(1)} %collective-permute-done.13.refs_0_), channel_id=1, source_target_pairs={{0,1},{1,0},{2,3},{3,2},{4,5},{5,4},{6,7},{7,6},{8,9},{9,8},{10,11... | collective-permute-start | bytes 1966088 | tf_op jit(solution)/shard_map/ppermute | solution.py:51
  76.6 4.4 %collective-permute-start.17 = (f32[10,128,128]{2,1,0:T(8,128)S(1)}, f32[10,128,128]{2,1,0:T(8,128)S(1)}, u32[]{:S(2)}, u32[]{:S(2)}) collective-permute-start(f32[10,128,128]{2,1,0:T(8,128)S(1)} %collective-permute-done.14.refs_1_), channel_id=1, source_target_pairs={{0,1},{1,0},{2,3},{3,2},{4,5},{5,4},{6,7},{7,6},{8,9},{9,8},{10,11... | collective-permute-start | bytes 1966088 | tf_op jit(solution)/shard_map/ppermute | solution.py:51

commit v4 on v2

--- a/solution.py
+++ b/solution.py
@@ -418,12 +418,12 @@
 def body(density, pattern, filt):
     blocks = flat(density)
     row = COLS * HALF
-    above, below = shift(pattern[1:], "dom", 1), shift(pattern[:2], "dom", -1)
+    above, below = shift(pattern, "dom", 1), shift(pattern, "dom", -1)
     own_other = shift(blocks, "rep", 1)
     one, two = pack([blocks], [[(0, (row, 0), 2 * row)], [(0, (0, row), 2 * row)]], far=True)
     above, below, one = lax.optimization_barrier((above, below, one))
     one = cross(one, 1)
-    near = jnp.concatenate([above, pattern, below], axis=0)
+    near = jnp.concatenate([above[ROWS - 2:], pattern, below[:2]], axis=0)
     before, after = shift(near[:, 1:], "col", 1), shift(near[:, :1], "col", -1)
     edge_r, edge_l = pack([blocks], [[(0, r * row + q, HALF) for r in range(ROWS)] for q in (HALF, 0)])
     before, after, two, edge_r, edge_l = lax.optimization_barrier((before, after, two, edge_r, edge_l))

time: 83.7 us -> 85.3 us (1.019); the launches traced: 84.3 us -> 84.3 us
  Pallas kernels: 38.2 us -> 35.7 us
  waiting for transfers between devices: 10.5 us -> 12.3 us
  starting transfers between devices: 24.1 us -> 25.6 us
  local copies, waits for them, and re-layouts: 3.51 us -> 2.62 us
    ppermute x16, waiting for transfers between devices: 9.45 us -> 12.3 us  [shift(): lax.ppermute(array, axis, [(i, (i + step) % peers) for i in range(peers)])]
    pallas_call x5, Pallas kernels: 23.2 us -> 20.7 us  [call(): pl.pallas_call(kernel, out_shape=outs, in_specs=[smem()] * len(lists) + [...]
    ppermute x3, waiting for transfers between devices: 1.07 us -> 0.01 us  [cross(): return lax.ppermute(array, ('dom', 'rep'), pairs)]
    slice x3 -> x1, local copies, waits for them, and re-layouts: 0.96 us -> 0.07 us  [body(): near = jnp.concatenate([above[ROWS - 2:], pattern, below[:2]], axis=0)]
  transfers between devices with their start and end apart: 19 -> 19, of which waited for: 6 -> 7; matrix products, arithmetic and copies ran while one was open for 3% -> 1% of each run, Pallas kernels for 39% -> 37%
where the time goes in v4:
time: 85.3 us; the launch traced here: 84.3 us
  Pallas kernels  35.7 us (42%)
  starting transfers between devices  25.6 us (30%)
  waiting for transfers between devices  12.3 us (14%)
  blocking collectives  7.57 us (9%)
  local copies, waits for them, and re-layouts  2.62 us (3%)
    ppermute x16, starting transfers between devices, shift(): lax.ppermute(array, axis, [(i, (i + step) % peers) for i in range(peers)])  23.2 us
    pallas_call x5, Pallas kernels, call(): pl.pallas_call(kernel, out_shape=outs, in_specs=[smem()] * len(lists) + [...  20.7 us
    ppermute x16, waiting for transfers between devices, shift(): lax.ppermute(array, axis, [(i, (i + step) % peers) for i in range(peers)])  12.3 us
    pallas_call x1, Pallas kernels, make_lists(): pl.pallas_call(functools.partial(list_kernel, grid), out_shape=[jax.Shape...  9.48 us
    all_gather x1, blocking collectives, body(): lax.all_gather(jnp.concatenate([rim, own_filt], axis=0), 'rep', axis=2, t...  7.57 us
    pallas_call x4, Pallas kernels, pack(): pl.pallas_call(kernel, out_shape=[out((n, 128, 128), jnp.float32) for n i...  5.58 us
    unnamed x12, local copies, waits for them, and re-layouts  2.43 us
    ppermute x3, starting transfers between devices, cross(): return lax.ppermute(array, ('dom', 'rep'), pairs)  2.42 us
  transfers between devices with their start and end apart: 19, of which 7 were waited for; matrix products, arithmetic and copies ran while one was open for 1% of the time, Pallas kernels for 37%

profile of v4, /device:TPU:1, one launch (start us, length us, event | category | flops | bytes accessed | tf_op | source)
XLA Modules:
  0.0 84.3 jit_solution(984516247820096330)
XLA Ops:
  0.0 0.0 copy-start.4
  0.0 3.2 %collective-permute-start.4 = (f32[30,128,128]{2,1,0:T(8,128)}, f32[30,128,128]{2,1,0:T(8,128)}, u32[]{:S(2)}, u32[]{:S(2)}) collective-permute-start(f32[30,128,128]{2,1,0:T(8,128)} %bitcast.3), channel_id=1, source_target_pairs={{0,1},{1,0},{2,3},{3,2},{4,5},{5,4},{6,7},{7,6},{8,9},{9,8},{10,11... | collective-permute-start | bytes 5898248 | tf_op jit(solution)/shard_map/ppermute | solution.py:51
  3.2 0.8 copy.14
  4.0 3.2 %collective-permute-start.1 = (s32[3,2,5]{0,1,2:T(2,128)S(1)}, s32[3,2,5]{0,1,2:T(2,128)S(1)}, u32[]{:S(2)}, u32[]{:S(2)}) collective-permute-start(s32[3,2,5]{0,1,2:T(2,128)S(1)} %copy.14), channel_id=1, source_target_pairs={{0,240},{16,0},{32,16},{48,32},{64,48},{80,64},{96,80},{112,96},{1... | collective-permute-start | bytes 368 | tf_op jit(solution)/shard_map/ppermute | solution.py:51
  7.2 0.0 collective-permute-start
  7.2 0.0 copy-start
  7.2 1.5 %copy-done = f32[3,2,5,128,128]{4,3,2,1,0:T(8,128)S(1)} copy-done((f32[3,2,5,128,128]{4,3,2,1,0:T(8,128)S(1)}, f32[3,2,5,128,128]{4,3,2,1,0:T(8,128)}, u32[]{:S(2)}) %copy-start) | copy-done | bytes 1966104
  8.8 0.0 copy-start.1
  8.8 0.0 copy-start.2
  8.8 1.8 %pack.4 = (f32[20,128,128]{2,1,0:T(8,128)}, f32[20,128,128]{2,1,0:T(8,128)}) custom-call(f32[30,128,128]{2,1,0:T(8,128)S(1)} %bitcast.4), custom_call_target="tpu_custom_call" | custom-call | flops 1000 | bytes 1000 | tf_op jit(solution)/shard_map/pack/pallas_call | solution.py:361
  10.6 0.0 collective-permute-done.1
  10.6 2.4 %collective-permute-done = s32[3,2,5]{0,1,2:T(2,128)S(1)} collective-permute-done((s32[3,2,5]{0,1,2:T(2,128)S(1)}, s32[3,2,5]{0,1,2:T(2,128)S(1)}, u32[]{:S(2)}, u32[]{:S(2)}) %collective-permute-start) | collective-permute-done | bytes 152 | tf_op jit(solution)/shard_map/ppermute | solution.py:51
  13.0 0.1 slice.12
  13.1 2.4 %collective-permute-start.5 = (f32[20,128,128]{2,1,0:T(8,128)}, f32[20,128,128]{2,1,0:T(8,128)S(1)}, u32[]{:S(2)}, u32[]{:S(2)}) collective-permute-start(f32[20,128,128]{2,1,0:T(8,128)} %get-tuple-element.68), channel_id=1, source_target_pairs={{0,16},{1,241},{16,32},{17,1},{32,48},{33,17},{48,64},{49,33},{64,... | collective-permute-start | bytes 3932168 | tf_op jit(solution)/shard_map/ppermute | solution.py:57
  15.5 0.1 pad_add_fusion
  15.6 5.7 %collective-permute-start.3 = (s32[7,1,5]{0,1,2:T(1,128)S(1)}, s32[7,1,5]{0,1,2:T(1,128)S(1)}, u32[]{:S(2)}, u32[]{:S(2)}) collective-permute-start(s32[7,1,5]{0,1,2:T(1,128)S(1)} %get-tuple-element.95), channel_id=1, source_target_pairs={{0,14},{2,0},{4,2},{6,4},{8,6},{10,8},{12,10},{14,12},{1,15},{3,1}... | collective-permute-start | bytes 428 | tf_op jit(solution)/shard_map/ppermute | solution.py:51
  21.2 0.0 collective-permute-start.2
  21.2 0.0 copy-done.1
  21.2 2.0 %pack.5 = (f32[15,128,128]{2,1,0:T(8,128)}, f32[15,128,128]{2,1,0:T(8,128)}) custom-call(f32[30,128,128]{2,1,0:T(8,128)S(1)} %bitcast.5), custom_call_target="tpu_custom_call" | custom-call | flops 1000 | bytes 1000 | tf_op jit(solution)/shard_map/pack/pallas_call | solution.py:361
  23.2 0.0 collective-permute-done.3
  23.3 1.9 %collective-permute-done.2 = s32[7,1,5]{0,1,2:T(1,128)S(1)} collective-permute-done((s32[7,1,5]{0,1,2:T(1,128)S(1)}, s32[7,1,5]{0,1,2:T(1,128)S(1)}, u32[]{:S(2)}, u32[]{:S(2)}) %collective-permute-start.2) | collective-permute-done | bytes 172 | tf_op jit(solution)/shard_map/ppermute | solution.py:51
  25.2 0.0 collective-permute-start.8
  25.2 0.0 collective-permute-start.6
  25.2 2.7 %collective-permute-start.7 = (f32[15,128,128]{2,1,0:T(8,128)}, f32[15,128,128]{2,1,0:T(8,128)}, u32[]{:S(2)}, u32[]{:S(2)}) collective-permute-start(f32[15,128,128]{2,1,0:T(8,128)} %get-tuple-element.71), channel_id=1, source_target_pairs={{0,14},{2,0},{4,2},{6,4},{8,6},{10,8},{12,10},{14,12},{1,15},{3,1}... | collective-permute-start | bytes 2949128 | tf_op jit(solution)/shard_map/ppermute | solution.py:51
  27.9 0.0 copy-done.4
  27.9 0.1 copy.17
  28.0 0.0 copy-done.2
  28.0 0.0 copy-done.3
  28.0 0.1 select_add_fusion
  28.1 7.6 %all_gather.3 = s32[10,4,10]{0,1,2:T(4,128)S(1)} all-gather(s32[10,4,5]{0,1,2:T(4,128)S(1)} %select_add_fusion), channel_id=1, replica_groups=mesh['dom'=16,'col'=8,'rep'=2] {'rep'}, dimensions={2}, use_global_device_ids=true | all-gather | bytes 2400 | tf_op jit(solution)/shard_map/all_gather | solution.py:434
  35.6 0.1 copy.18.known
  35.8 9.5 %lists.1 = (s32[632]{0:T(1024)S(1)}, s32[632]{0:T(1024)S(1)}, s32[332]{0:T(512)S(1)}, s32[632]{0:T(1024)S(1)}, s32[61]{0:T(128)S(1)}, /*index=5*/s32[8]{0:T(128)S(1)}) custom-call(s32[10,4,10]{2,1,0:T(4,128)S(1)} %copy.18.known, s32[7,4,10]{2,1,0:T(4,128)S(1)} %broadcast_select_fusion.stored), custom_call_target="tpu_custom_call" | custom-call | flops 1000 | bytes 1000 | tf_op jit(solution)/shard_map/lists/pallas_call | solution.py:172
  45.2 0.0 collective-permute-done.4.refs_1_
  45.3 2.7 %first.1 = (bf16[281,128,256]{2,1,0:T(8,128)(2,1)S(1)}, f32[61,128,128]{2,1,0:T(8,128)S(1)}) custom-call(f32[30,128,128]{2,1,0:T(8,128)S(1)} %bitcast.6, f32[30,128,128]{2,1,0:T(8,128)} %collective-permute-done.4.refs_1_), custom_call_target="tpu_custom_call" | custom-call | flops 1000 | bytes 1000 | tf_op jit(solution)/shard_map/first/pallas_call | solution.py:397
  48.0 0.0 collective-permute-done.5.refs_0_.refs_2_
  48.0 0.5 pack.6
  48.4 0.0 collective-permute-done.6.refs_0_
  48.4 0.0 collective-permute-done.7.refs_1_
  48.5 1.3 %pack.7 = f32[20,128,128]{2,1,0:T(8,128)S(1)} custom-call(f32[15,128,128]{2,1,0:T(8,128)} %collective-permute-done.6.refs_0_, f32[15,128,128]{2,1,0:T(8,128)} %collective-permute-done.7.refs_1_), custom_call_target="tpu_custom_call" | custom-call | flops 1000 | bytes 1000 | tf_op jit(solution)/shard_map/pack/pallas_call | solution.py:361
  49.8 0.0 collective-permute-done.8.refs_3_
  49.8 2.5 %collective-permute-start.9 = (f32[15,128,128]{2,1,0:T(8,128)}, f32[15,128,128]{2,1,0:T(8,128)S(1)}, u32[]{:S(2)}, u32[]{:S(2)}) collective-permute-start(f32[15,128,128]{2,1,0:T(8,128)} %collective-permute-done.6.refs_0_), channel_id=1, source_target_pairs={{0,1},{1,0},{2,3},{3,2},{4,5},{5,4},{6,7},{7,6},{8,9},{9,8},{10,11... | collective-permute-start | bytes 2949128 | tf_op jit(solution)/shard_map/ppermute | solution.py:51
  52.3 0.1 collective-permute-start.10
  52.4 0.4 collective-permute-start.12
  52.8 0.1 collective-permute-start.11
  52.9 0.0 collective-permute-start.15
  52.9 1.8 %collective-permute-done.9.refs_0_ = f32[15,128,128]{2,1,0:T(8,128)S(1)} collective-permute-done((f32[15,128,128]{2,1,0:T(8,128)}, f32[15,128,128]{2,1,0:T(8,128)S(1)}, u32[]{:S(2)}, u32[]{:S(2)}) %collective-permute-start.9) | collective-permute-done | bytes 983072 | tf_op jit(solution)/shard_map/ppermute | solution.py:51
  54.7 0.0 collective-permute-start.13
  54.7 2.8 %collective-permute-done.10.refs_1_ = f32[15,128,128]{2,1,0:T(8,128)S(1)} collective-permute-done((f32[15,128,128]{2,1,0:T(8,128)}, f32[15,128,128]{2,1,0:T(8,128)S(1)}, u32[]{:S(2)}, u32[]{:S(2)}) %collective-permute-start.10) | collective-permute-done | bytes 983072 | tf_op jit(solution)/shard_map/ppermute | solution.py:51
  57.5 2.8 %collective-permute-start.14 = (f32[10,128,128]{2,1,0:T(8,128)S(1)}, f32[10,128,128]{2,1,0:T(8,128)S(1)}, u32[]{:S(2)}, u32[]{:S(2)}) collective-permute-start(f32[10,128,128]{2,1,0:T(8,128)S(1)} %get-tuple-element.74), channel_id=1, source_target_pairs={{0,14},{2,0},{4,2},{6,4},{8,6},{10,8},{12,10},{14,12},{1,15},{3,1}... | collective-permute-start | bytes 1966088 | tf_op jit(solution)/shard_map/ppermute | solution.py:51
  60.3 3.1 %rows.1._ = bf16[281,128,256]{2,1,0:T(8,128)(2,1)S(1)} custom-call(bf16[281,128,256]{2,1,0:T(8,128)(2,1)S(1)} %get-tuple-element.69._, f32[15,128,128]{2,1,0:T(8,128)} %collective-permute-done.6.refs_0_, f32[15,128,128]{2,1,0:T(8,128)} %collective-permute-done.7.refs_1_, ...), custom_call_target="tpu_custom_call", output_to_operand_aliasing={{}: (0, {})} | custom-call | flops 1000 | bytes 1000 | tf_op jit(solution)/shard_map/rows/pallas_call | solution.py:397
  63.4 0.0 collective-permute-done.12.refs_3_
  63.4 0.0 collective-permute-done.11.refs_2_
  63.4 9.4 %early.1 = (bf16[281,128,256]{2,1,0:T(8,128)(2,1)S(1)}, f32[61,128,128]{2,1,0:T(8,128)S(1)}, bf16[121,128,256]{2,1,0:T(8,128)(2,1)S(1)}, f32[31,128,128]{2,1,0:T(8,128)S(1)}) custom-call(s32[632]{0:T(1024)S(1)} %get-tuple-element.63.codes, s32[332]{0:T(512)S(1)} %get-tuple-element.64.cube_codes, ...), custom_call_target="tpu_custom_call", output_to_operand_aliasing={{0}: (3, {}), {1}: (4, {})} | custom-call | flops 1000 | bytes 1000 | tf_op jit(solution)/shard_map/early/pallas_call | solution.py:397
  72.8 0.0 collective-permute-done.13.refs_0_
  72.8 0.5 collective-permute-done.14.refs_1_
  73.3 0.0 collective-permute-done.15.refs_2_
  73.3 2.0 %collective-permute-start.18 = (f32[20,128,128]{2,1,0:T(8,128)S(1)}, f32[20,128,128]{2,1,0:T(8,128)S(1)}, u32[]{:S(2)}, u32[]{:S(2)}) collective-permute-start(f32[20,128,128]{2,1,0:T(8,128)S(1)} %collective-permute-done.15.refs_2_), channel_id=1, source_target_pairs={{0,1},{1,0},{2,3},{3,2},{4,5},{5,4},{6,7},{7,6},{8,9},{9,8},{10,11... | collective-permute-start | bytes 3932168 | tf_op jit(solution)/shard_map/ppermute | solution.py:51
  75.2 0.0 collective-permute-start.16
  75.3 0.5 collective-permute-start.17
  75.8 1.1 %corner.1.blocks_in = bf16[281,128,256]{2,1,0:T(8,128)(2,1)S(1)} custom-call(bf16[281,128,256]{2,1,0:T(8,128)(2,1)S(1)} %get-tuple-element.87._, f32[10,128,128]{2,1,0:T(8,128)S(1)} %collective-permute-done.13.refs_0_, f32[10,128,128]{2,1,0:T(8,128)S(1)} %collective-permute-done.14.refs_1_, ...), custom_call_target="tpu_custom_call", output_to_operand_aliasing={{}: (0, {})} | custom-call | flops 1000 | bytes 1000 | tf_op jit(solution)/shard_map/corner/pallas_call | solution.py:397
  76.9 2.0 %collective-permute-done.16.refs_0_ = f32[10,128,128]{2,1,0:T(8,128)S(1)} collective-permute-done((f32[10,128,128]{2,1,0:T(8,128)S(1)}, f32[10,128,128]{2,1,0:T(8,128)S(1)}, u32[]{:S(2)}, u32[]{:S(2)}) %collective-permute-start.16) | collective-permute-done | bytes 655392 | tf_op jit(solution)/shard_map/ppermute | solution.py:51
  78.8 0.9 %collective-permute-done.17.refs_1_ = f32[10,128,128]{2,1,0:T(8,128)S(1)} collective-permute-done((f32[10,128,128]{2,1,0:T(8,128)S(1)}, f32[10,128,128]{2,1,0:T(8,128)S(1)}, u32[]{:S(2)}, u32[]{:S(2)}) %collective-permute-start.17) | collective-permute-done | bytes 655392 | tf_op jit(solution)/shard_map/ppermute | solution.py:51
  79.8 0.0 collective-permute-done.18.refs_2_
  79.8 4.4 %late.1 = (f32[30,128,128]{2,1,0:T(8,128)}, bf16[281,128,256]{2,1,0:T(8,128)(2,1)S(1)}, f32[61,128,128]{2,1,0:T(8,128)S(1)}, bf16[121,128,256]{2,1,0:T(8,128)(2,1)S(1)}, f32[31,128,128]{2,1,0:T(8,128)S(1)}) custom-call(s32[632]{0:T(1024)S(1)} %get-tuple-element.58.codes, ...), custom_call_target="tpu_custom_call", output_to_operand_aliasing={{1}: (4, {}), {2}: (5, {}), {3}: (6, {}), {4}: (7, {})} | custom-call | flops 1000 | bytes 1000 | tf_op jit(solution)/shard_map/late/pallas_call | solution.py:397
  (3 shorter events, 0.0 us)
Async XLA Ops:
  0.0 27.9 %copy-start.4 = (s32[3,2,5]{2,1,0:T(2,128)S(1)}, s32[3,2,5]{2,1,0:T(2,128)}, u32[]{:S(2)}) copy-start(s32[3,2,5]{2,1,0:T(2,128)} %param.7) | copy-start | bytes 364
  0.0 45.2 %collective-permute-start.4 = (f32[30,128,128]{2,1,0:T(8,128)}, f32[30,128,128]{2,1,0:T(8,128)}, u32[]{:S(2)}, u32[]{:S(2)}) collective-permute-start(f32[30,128,128]{2,1,0:T(8,128)} %bitcast.3), channel_id=1, source_target_pairs={{0,1},{1,0},{2,3},{3,2},{4,5},{5,4},{6,7},{7,6},{8,9},{9,8},{10,11... | collective-permute-start | bytes 5898248 | tf_op jit(solution)/shard_map/ppermute | solution.py:51
  4.0 6.6 %collective-permute-start.1 = (s32[3,2,5]{0,1,2:T(2,128)S(1)}, s32[3,2,5]{0,1,2:T(2,128)S(1)}, u32[]{:S(2)}, u32[]{:S(2)}) collective-permute-start(s32[3,2,5]{0,1,2:T(2,128)S(1)} %copy.14), channel_id=1, source_target_pairs={{0,240},{16,0},{32,16},{48,32},{64,48},{80,64},{96,80},{112,96},{1... | collective-permute-start | bytes 368 | tf_op jit(solution)/shard_map/ppermute | solution.py:51
  7.2 5.8 %collective-permute-start = (s32[3,2,5]{0,1,2:T(2,128)S(1)}, s32[3,2,5]{0,1,2:T(2,128)S(1)}, u32[]{:S(2)}, u32[]{:S(2)}) collective-permute-start(s32[3,2,5]{0,1,2:T(2,128)S(1)} %copy.14), channel_id=1, source_target_pairs={{0,16},{16,32},{32,48},{48,64},{64,80},{80,96},{96,112},{112,128},... | collective-permute-start | bytes 368 | tf_op jit(solution)/shard_map/ppermute | solution.py:51
  7.2 1.5 %copy-start = (f32[3,2,5,128,128]{4,3,2,1,0:T(8,128)S(1)}, f32[3,2,5,128,128]{4,3,2,1,0:T(8,128)}, u32[]{:S(2)}) copy-start(f32[3,2,5,128,128]{4,3,2,1,0:T(8,128)} %param.5) | copy-start | bytes 5898244
  8.8 12.5 %copy-start.1 = (f32[3,2,5,128,128]{4,3,2,1,0:T(8,128)S(1)}, f32[3,2,5,128,128]{4,3,2,1,0:T(8,128)}, u32[]{:S(2)}) copy-start(f32[3,2,5,128,128]{4,3,2,1,0:T(8,128)} %param.5) | copy-start | bytes 5898244
  8.8 19.2 %copy-start.2 = (s32[7,4,10]{2,1,0:T(4,128)S(1)}, s32[7,4,10]{2,1,0:T(4,128)}, u32[]{:S(2)}) copy-start(s32[7,4,10]{2,1,0:T(4,128)} %constant.13.clone) | copy-start | bytes 3364
  8.8 19.2 %copy-start.3 = (s32[7,4,10]{2,1,0:T(4,128)S(1)}, s32[7,4,10]{2,1,0:T(4,128)}, u32[]{:S(2)}) copy-start(s32[7,4,10]{2,1,0:T(4,128)} %constant.12.clone) | copy-start | bytes 3364
  13.1 34.9 %collective-permute-start.5 = (f32[20,128,128]{2,1,0:T(8,128)}, f32[20,128,128]{2,1,0:T(8,128)S(1)}, u32[]{:S(2)}, u32[]{:S(2)}) collective-permute-start(f32[20,128,128]{2,1,0:T(8,128)} %get-tuple-element.68), channel_id=1, source_target_pairs={{0,16},{1,241},{16,32},{17,1},{32,48},{33,17},{48,64},{49,33},{64,... | collective-permute-start | bytes 3932168 | tf_op jit(solution)/shard_map/ppermute | solution.py:57
  15.6 7.7 %collective-permute-start.3 = (s32[7,1,5]{0,1,2:T(1,128)S(1)}, s32[7,1,5]{0,1,2:T(1,128)S(1)}, u32[]{:S(2)}, u32[]{:S(2)}) collective-permute-start(s32[7,1,5]{0,1,2:T(1,128)S(1)} %get-tuple-element.95), channel_id=1, source_target_pairs={{0,14},{2,0},{4,2},{6,4},{8,6},{10,8},{12,10},{14,12},{1,15},{3,1}... | collective-permute-start | bytes 428 | tf_op jit(solution)/shard_map/ppermute | solution.py:51
  21.2 3.9 %collective-permute-start.2 = (s32[7,1,5]{0,1,2:T(1,128)S(1)}, s32[7,1,5]{0,1,2:T(1,128)S(1)}, u32[]{:S(2)}, u32[]{:S(2)}) collective-permute-start(s32[7,1,5]{0,1,2:T(1,128)S(1)} %get-tuple-element.96), channel_id=1, source_target_pairs={{0,2},{2,4},{4,6},{6,8},{8,10},{10,12},{12,14},{14,0},{1,3},{3,5},... | collective-permute-start | bytes 428 | tf_op jit(solution)/shard_map/ppermute | solution.py:51
  25.2 24.6 %collective-permute-start.8 = (f32[20,128,128]{2,1,0:T(8,128)}, f32[20,128,128]{2,1,0:T(8,128)}, u32[]{:S(2)}, u32[]{:S(2)}) collective-permute-start(f32[20,128,128]{2,1,0:T(8,128)} %get-tuple-element.77), channel_id=1, source_target_pairs={{0,240},{1,17},{16,0},{17,33},{32,16},{33,49},{48,32},{49,65},{64,... | collective-permute-start | bytes 3932168 | tf_op jit(solution)/shard_map/ppermute | solution.py:57
  25.2 23.3 %collective-permute-start.6 = (f32[15,128,128]{2,1,0:T(8,128)}, f32[15,128,128]{2,1,0:T(8,128)}, u32[]{:S(2)}, u32[]{:S(2)}) collective-permute-start(f32[15,128,128]{2,1,0:T(8,128)} %get-tuple-element.70), channel_id=1, source_target_pairs={{0,2},{2,4},{4,6},{6,8},{8,10},{10,12},{12,14},{14,0},{1,3},{3,5},... | collective-permute-start | bytes 2949128 | tf_op jit(solution)/shard_map/ppermute | solution.py:51
  25.2 23.3 %collective-permute-start.7 = (f32[15,128,128]{2,1,0:T(8,128)}, f32[15,128,128]{2,1,0:T(8,128)}, u32[]{:S(2)}, u32[]{:S(2)}) collective-permute-start(f32[15,128,128]{2,1,0:T(8,128)} %get-tuple-element.71), channel_id=1, source_target_pairs={{0,14},{2,0},{4,2},{6,4},{8,6},{10,8},{12,10},{14,12},{1,15},{3,1}... | collective-permute-start | bytes 2949128 | tf_op jit(solution)/shard_map/ppermute | solution.py:51
  49.8 4.9 %collective-permute-start.9 = (f32[15,128,128]{2,1,0:T(8,128)}, f32[15,128,128]{2,1,0:T(8,128)S(1)}, u32[]{:S(2)}, u32[]{:S(2)}) collective-permute-start(f32[15,128,128]{2,1,0:T(8,128)} %collective-permute-done.6.refs_0_), channel_id=1, source_target_pairs={{0,1},{1,0},{2,3},{3,2},{4,5},{5,4},{6,7},{7,6},{8,9},{9,8},{10,11... | collective-permute-start | bytes 2949128 | tf_op jit(solution)/shard_map/ppermute | solution.py:51
  52.3 5.2 %collective-permute-start.10 = (f32[15,128,128]{2,1,0:T(8,128)}, f32[15,128,128]{2,1,0:T(8,128)S(1)}, u32[]{:S(2)}, u32[]{:S(2)}) collective-permute-start(f32[15,128,128]{2,1,0:T(8,128)} %collective-permute-done.7.refs_1_), channel_id=1, source_target_pairs={{0,1},{1,0},{2,3},{3,2},{4,5},{5,4},{6,7},{7,6},{8,9},{9,8},{10,11... | collective-permute-start | bytes 2949128 | tf_op jit(solution)/shard_map/ppermute | solution.py:51
  52.4 11.0 %collective-permute-start.12 = (f32[20,128,128]{2,1,0:T(8,128)}, f32[20,128,128]{2,1,0:T(8,128)S(1)}, u32[]{:S(2)}, u32[]{:S(2)}) collective-permute-start(f32[20,128,128]{2,1,0:T(8,128)} %collective-permute-done.8.refs_3_), channel_id=1, source_target_pairs={{0,1},{1,0},{2,3},{3,2},{4,5},{5,4},{6,7},{7,6},{8,9},{9,8},{10,11... | collective-permute-start | bytes 3932168 | tf_op jit(solution)/shard_map/ppermute | solution.py:51
  52.8 10.6 %collective-permute-start.11 = (f32[20,128,128]{2,1,0:T(8,128)S(1)}, f32[20,128,128]{2,1,0:T(8,128)S(1)}, u32[]{:S(2)}, u32[]{:S(2)}) collective-permute-start(f32[20,128,128]{2,1,0:T(8,128)S(1)} %collective-permute-done.5.refs_0_.refs_2_), channel_id=1, source_target_pairs={{0,1},{1,0},{2,3},{3,2},{4,5},{5,4},{6,7},{7,6},{8,9},{9,8},{10,11... | collective-permute-start | bytes 3932168 | tf_op jit(solution)/shard_map/ppermute | solution.py:51
  52.9 20.4 %collective-permute-start.15 = (f32[20,128,128]{2,1,0:T(8,128)S(1)}, f32[20,128,128]{2,1,0:T(8,128)S(1)}, u32[]{:S(2)}, u32[]{:S(2)}) collective-permute-start(f32[20,128,128]{2,1,0:T(8,128)S(1)} %pack.7), channel_id=1, source_target_pairs={{0,240},{1,17},{16,0},{17,33},{32,16},{33,49},{48,32},{49,65},{64,... | collective-permute-start | bytes 3932168 | tf_op jit(solution)/shard_map/ppermute | solution.py:57
  54.7 18.1 %collective-permute-start.13 = (f32[10,128,128]{2,1,0:T(8,128)S(1)}, f32[10,128,128]{2,1,0:T(8,128)S(1)}, u32[]{:S(2)}, u32[]{:S(2)}) collective-permute-start(f32[10,128,128]{2,1,0:T(8,128)S(1)} %get-tuple-element.73), channel_id=1, source_target_pairs={{0,2},{2,4},{4,6},{6,8},{8,10},{10,12},{12,14},{14,0},{1,3},{3,5},... | collective-permute-start | bytes 1966088 | tf_op jit(solution)/shard_map/ppermute | solution.py:51
  57.5 15.8 %collective-permute-start.14 = (f32[10,128,128]{2,1,0:T(8,128)S(1)}, f32[10,128,128]{2,1,0:T(8,128)S(1)}, u32[]{:S(2)}, u32[]{:S(2)}) collective-permute-start(f32[10,128,128]{2,1,0:T(8,128)S(1)} %get-tuple-element.74), channel_id=1, source_target_pairs={{0,14},{2,0},{4,2},{6,4},{8,6},{10,8},{12,10},{14,12},{1,15},{3,1}... | collective-permute-start | bytes 1966088 | tf_op jit(solution)/shard_map/ppermute | solution.py:51
  73.3 6.5 %collective-permute-start.18 = (f32[20,128,128]{2,1,0:T(8,128)S(1)}, f32[20,128,128]{2,1,0:T(8,128)S(1)}, u32[]{:S(2)}, u32[]{:S(2)}) collective-permute-start(f32[20,128,128]{2,1,0:T(8,128)S(1)} %collective-permute-done.15.refs_2_), channel_id=1, source_target_pairs={{0,1},{1,0},{2,3},{3,2},{4,5},{5,4},{6,7},{7,6},{8,9},{9,8},{10,11... | collective-permute-start | bytes 3932168 | tf_op jit(solution)/shard_map/ppermute | solution.py:51
  75.2 3.6 %collective-permute-start.16 = (f32[10,128,128]{2,1,0:T(8,128)S(1)}, f32[10,128,128]{2,1,0:T(8,128)S(1)}, u32[]{:S(2)}, u32[]{:S(2)}) collective-permute-start(f32[10,128,128]{2,1,0:T(8,128)S(1)} %collective-permute-done.13.refs_0_), channel_id=1, source_target_pairs={{0,1},{1,0},{2,3},{3,2},{4,5},{5,4},{6,7},{7,6},{8,9},{9,8},{10,11... | collective-permute-start | bytes 1966088 | tf_op jit(solution)/shard_map/ppermute | solution.py:51
  75.3 4.5 %collective-permute-start.17 = (f32[10,128,128]{2,1,0:T(8,128)S(1)}, f32[10,128,128]{2,1,0:T(8,128)S(1)}, u32[]{:S(2)}, u32[]{:S(2)}) collective-permute-start(f32[10,128,128]{2,1,0:T(8,128)S(1)} %collective-permute-done.14.refs_1_), channel_id=1, source_target_pairs={{0,1},{1,0},{2,3},{3,2},{4,5},{5,4},{6,7},{7,6},{8,9},{9,8},{10,11... | collective-permute-start | bytes 1966088 | tf_op jit(solution)/shard_map/ppermute | solution.py:51
